TPU v7x, 128 devices: a whole 4x4x4 slice. The times are simulated.
128 devices in a mesh: section: 8 (over y_hi, x), tensor: 16 (over y_lo, z, core).
Axes of the slice: x: 4, y: 4 (y_hi: 2, y_lo: 2; y = y_hi * 2 + y_lo), z: 4, core: 2. Of those that a mesh axis runs over, the one named last changes fastest.
Arguments:
- incoming: bfloat16 [8, 3, 384, 8192], P('section', None, 'tensor'), may hold values from -6 to 6
- norm_gain: bfloat16 [8, 8192], P('section'), may hold values from 0.099609375 to 1.8984375
- w_query: bfloat16 [8, 8192, 8192], P('section', None, 'tensor'), may hold values from -0.0625 to 0.0625
- w_key_value: bfloat16 [8, 8192, 2, 1024], P('section', None, None, 'tensor'), may hold values from -0.0625 to 0.0625
- w_out: bfloat16 [8, 8192, 8192], P('section', 'tensor'), may hold values from -0.0625 to 0.0625
- kv_cache: bfloat16 [8, 2, 384, 1024], P('section'), may hold values from -1000 to 1000, as said below
- offsets: int32 [8, 3], P('section'), may hold values from 0 to 1152, as said below
Outputs:
- outgoing: bfloat16 [8, 3, 384, 8192], P('section', None, 'tensor')
Inputs may be any that keep to these rules, and one draw needn't show every extreme that they name: offsets[s, j] = offsets[s, 0] + j * 384; offsets[s, 0] lies between 0 and 384, and is 0 at some section and 384 at another. `kv_cache`: cached keys are stored after the rotary embedding of their positions.
All inputs are finite; a program needn't handle non-finite values.
Results may differ from a plain program's by a relative error of at most 0.015.
Values may be sent and summed in bfloat16 or wider, within the bound.
No kernel may reach another device: no remote copies, remote signals or barrier semaphores. Data moves between devices by JAX's collectives and lax.ppermute only.
A program may use at most 128 MiB of HBM per device.

v0:
```python
import math

import jax
import jax.numpy as jnp
from jax import lax
from jax.sharding import PartitionSpec as P

HD = 128
BLOCK = 384
CACHE = 384


def from_partner(value, axis, bit):
    return lax.ppermute(value, axis, [(i, i ^ 1 << bit) for i in range(lax.axis_size(axis))])


def from_behind(value, axis, by):
    devices = lax.axis_size(axis)
    return lax.ppermute(value, axis, [(i, (i + by) % devices) for i in range(devices)])


def rotary(values, position):
    half = values.shape[-1] // 2
    freq = 500000.0 ** (-jnp.arange(half, dtype=jnp.float32) * 2.0 / values.shape[-1])
    angle = position.astype(jnp.float32)[..., None, None] * freq
    cosine = jnp.cos(angle)
    sine = jnp.sin(angle)
    first = values[..., :half]
    second = values[..., half:]
    return jnp.concatenate(
        [first * cosine - second * sine, second * cosine + first * sine], axis=-1
    )


def normalize(handed, gain):
    widened = handed.astype(jnp.float32)
    return (
        widened
        * lax.rsqrt(jnp.mean(widened * widened, axis=-1, keepdims=True) + 1e-05)
        * gain.astype(jnp.float32)
    ).astype(jnp.bfloat16)


def attend(query, key_block, value_block, position, key_position, key_ok):
    scores = jnp.einsum("chd,kd->hck", query, key_block, preferred_element_type=jnp.float32) * (
        1.0 / math.sqrt(query.shape[-1])
    )
    allowed = (key_position[None, :] <= position[:, None]) & key_ok[None, :]
    scores = jnp.where(allowed[None], scores, -1e30)
    weights = jax.nn.softmax(scores, axis=-1).astype(jnp.bfloat16)
    attended = jnp.einsum(
        "hck,kd->chd", weights, value_block, preferred_element_type=jnp.float32
    ).astype(jnp.bfloat16)
    return attended.reshape(query.shape[0], -1)


def shards(incoming, norm_gain, w_query, w_key_value, w_out, kv_cache, offsets):
    tensors = lax.axis_size("tensor")
    index = lax.axis_index("tensor")
    width_q = w_query.shape[2]
    heads_dev = width_q // HD
    width_kv = w_key_value.shape[3]
    kv_heads = kv_cache.shape[3] // HD
    group = tensors // kv_heads
    kv_head = index // group
    combined = jnp.concatenate(
        [w_query[0], w_key_value[0].reshape(w_key_value.shape[1], 2 * width_kv)], axis=1
    )
    cache_keys = lax.dynamic_slice_in_dim(kv_cache[0, 0], kv_head * HD, HD, 1)
    cache_values = lax.dynamic_slice_in_dim(kv_cache[0, 1], kv_head * HD, HD, 1)
    offset_row = offsets[0]
    slots = jnp.arange(CACHE, dtype=jnp.int32)
    within = jnp.arange(BLOCK, dtype=jnp.int32)
    window_position = (offset_row[:, None] + within[None, :]).reshape(-1)
    key_position = jnp.concatenate([slots, window_position])
    key_ok = jnp.concatenate([slots < offset_row[0], jnp.ones((3 * BLOCK,), dtype=bool)])
    window_keys = jnp.zeros((3 * BLOCK, HD), jnp.bfloat16)
    window_values = jnp.zeros((3 * BLOCK, HD), jnp.bfloat16)
    results = []
    for which in range(3):
        handed = from_behind(incoming[0, which], "section", 1)
        normed = normalize(handed, norm_gain[0])
        projected = jnp.dot(
            lax.all_gather(normed, "tensor", axis=0, tiled=True),
            combined,
            preferred_element_type=jnp.float32,
        )
        position = offset_row[which] + within
        query = rotary(projected[:, :width_q].reshape(-1, heads_dev, HD), position).astype(
            jnp.bfloat16
        )
        piece_kv = projected[:, width_q:].astype(jnp.bfloat16)
        rows = piece_kv.shape[0]
        block = piece_kv.reshape(rows, 2, width_kv)
        other = from_partner(block.reshape(rows, -1), "tensor", 0).reshape(block.shape)
        upper = index >> 0 & 1 == 1
        block = jnp.where(
            upper, jnp.concatenate([other, block], axis=2), jnp.concatenate([block, other], axis=2)
        )
        keys = rotary(block[:, 0:1].astype(jnp.float32), position)[:, 0].astype(jnp.bfloat16)
        query, keys, values = (query, keys, block[:, 1])
        window_keys = window_keys.at[which * BLOCK : (which + 1) * BLOCK].set(keys)
        window_values = window_values.at[which * BLOCK : (which + 1) * BLOCK].set(values)
        attended = attend(
            query,
            jnp.concatenate([cache_keys, window_keys], axis=0),
            jnp.concatenate([cache_values, window_values], axis=0),
            position,
            key_position,
            key_ok,
        )

        def term_rows(start, count, attended=attended):
            return jnp.dot(attended, w_out[0], preferred_element_type=jnp.float32)

        summed = lax.psum_scatter(
            term_rows(jnp.int32(0), lax.axis_size("tensor") * handed.shape[0]).astype(jnp.bfloat16),
            "tensor",
            scatter_dimension=0,
            tiled=True,
        ).astype(jnp.float32)
        results.append((handed.astype(jnp.float32) + summed).astype(jnp.bfloat16))
    return jnp.stack(results)[None]


def solution(mesh):
    placed = (
        P("section", None, "tensor", None),
        P("section", None),
        P("section", None, "tensor"),
        P("section", None, None, "tensor"),
        P("section", "tensor", None),
        P("section", None, None, None),
        P("section", None),
    )
    return jax.shard_map(
        shards,
        mesh=mesh,
        in_specs=placed,
        out_specs=P("section", None, "tensor", None),
        check_vma=False,
    )
```

profile of v0, /device:TPU:0, one launch (start us, length us, event | category | flops | bytes accessed | tf_op | source)
XLA Modules:
  0.0 495.1 jit_solution(14385624090992725366)
XLA Ops:
  6.5 1.3 slice_bitcast_fusion
  7.9 1.6 collective-permute-start.4
  9.5 1.5 collective-permute-start.2
  11.0 1.2 collective-permute-start
  12.2 0.8 mul.393
  13.0 10.5 %collective-permute-done.4 = bf16[24,8192]{1,0:T(8,128)(2,1)S(1)} collective-permute-done((bf16[24,8192]{1,0:T(8,128)(2,1)S(1)}, bf16[24,8192]{1,0:T(8,128)(2,1)S(1)}, u32[]{:S(2)}, u32[]{:S(2)}) %collective-permute-start.4) | collective-permute-done | bytes 393248 | tf_op jit(solution)/shard_map/ppermute | solution.py:19
  23.8 8.2 %collective-permute-done.2 = bf16[24,8192]{1,0:T(8,128)(2,1)S(1)} collective-permute-done((bf16[24,8192]{1,0:T(8,128)(2,1)S(1)}, bf16[24,8192]{1,0:T(8,128)(2,1)S(1)}, u32[]{:S(2)}, u32[]{:S(2)}) %collective-permute-start.2) | collective-permute-done | bytes 393248 | tf_op jit(solution)/shard_map/ppermute | solution.py:19
  32.2 7.2 %collective-permute-done = bf16[24,8192]{1,0:T(8,128)(2,1)S(1)} collective-permute-done((bf16[24,8192]{1,0:T(8,128)(2,1)S(1)}, bf16[24,8192]{1,0:T(8,128)(2,1)S(1)}, u32[]{:S(2)}, u32[]{:S(2)}) %collective-permute-start) | collective-permute-done | bytes 393248 | tf_op jit(solution)/shard_map/ppermute | solution.py:19
  39.6 1.2 fusion.43
  43.1 1.5 fusion.136
  45.4 4.1 copy.57
  53.6 3.1 multiply_cosine_fusion.2
  56.7 3.1 compare_and_fusion.2
  59.7 23.6 %all-gather.4.cloned.1.call-done = bf16[384,8192]{1,0:T(8,128)(2,1)} async-done(((bf16[24,8192]{1,0:T(8,128)(2,1)}), bf16[384,8192]{1,0:T(8,128)(2,1)}) %all-gather.4.cloned.1.call-update) | async-done | bytes 6291472 | tf_op jit(solution)/shard_map/all_gather | solution.py:84
  83.3 10.8 %fusion.29 = f32[384,640]{1,0:T(8,128)S(1)} fusion(bf16[384,8192]{1,0:T(8,128)(2,1)} %all-gather.4.cloned.1.call-done, bf16[8192,128]{1,0:T(8,128)(2,1)} %copy.57, bf16[8192,512]{1,0:T(8,128)(2,1)} %bitcast.167), kind=kOutput, calls=%fused_computation.39 | convolution fusion | flops 4047503360 | bytes 17760256 | tf_op jit(solution)/shard_map/dot_general | solution.py:83
  94.9 33.4 %all-gather.6.cloned.1.call-done = bf16[384,8192]{1,0:T(8,128)(2,1)} async-done(((bf16[24,8192]{1,0:T(8,128)(2,1)}), bf16[384,8192]{1,0:T(8,128)(2,1)}) %all-gather.6.cloned.1.call-update) | async-done | bytes 6291472 | tf_op jit(solution)/shard_map/all_gather | solution.py:84
  128.3 10.8 %fusion.28 = f32[384,640]{1,0:T(8,128)S(1)} fusion(bf16[384,8192]{1,0:T(8,128)(2,1)} %all-gather.6.cloned.1.call-done, bf16[8192,128]{1,0:T(8,128)(2,1)} %copy.57, bf16[8192,512]{1,0:T(8,128)(2,1)} %bitcast.168), kind=kOutput, calls=%fused_computation.38 | convolution fusion | flops 4047503360 | bytes 17760256 | tf_op jit(solution)/shard_map/dot_general | solution.py:83
  139.9 33.4 %all-gather.8.cloned.1.call-done = bf16[384,8192]{1,0:T(8,128)(2,1)} async-done(((bf16[24,8192]{1,0:T(8,128)(2,1)}), bf16[384,8192]{1,0:T(8,128)(2,1)}) %all-gather.8.cloned.1.call-update) | async-done | bytes 6291472 | tf_op jit(solution)/shard_map/all_gather | solution.py:84
  173.3 22.9 %fusion.27 = f32[384,640]{1,0:T(8,128)S(1)} fusion(bf16[384,8192]{1,0:T(8,128)(2,1)} %all-gather.8.cloned.1.call-done, bf16[8192,128]{1,0:T(8,128)(2,1)} %copy.57, bf16[8192,512]{1,0:T(8,128)(2,1)} %bitcast.169), kind=kOutput, calls=%fused_computation.37 | convolution fusion | flops 4047503360 | bytes 17760256 | tf_op jit(solution)/shard_map/dot_general | solution.py:83
  196.9 1.0 slice.256
  199.0 1.6 fusion.137
  201.3 1.4 reshape.707
  203.2 2.6 subtract_convert_fusion.2
  205.7 2.1 subtract_convert_fusion.1
  207.9 1.2 subtract_convert_fusion
  209.1 1.0 copy.59
  210.1 1.0 copy.72
  211.1 1.0 copy.66
  212.1 1.0 copy.58
  213.2 1.0 copy.71
  214.3 1.0 copy.65
  215.5 1.3 fusion.94
  218.3 8.6 %fusion.151 = (f32[4,384]{1,0:T(4,128)S(1)}, f32[4,384,1536]{1,2,0:T(8,128)}) fusion(pred[384,1536]{0,1:T(8,128)(4,1)} %get-tuple-element.105, bf16[384,128]{0,1:T(8,128)(2,1)} %bitcast.160, bf16[1152,128]{0,1:T(8,128)(2,1)} %scatter.21, bf16[384,4,64]{2,0,1:T(8,128)(2,1)} %get-tuple-element.78, bf16[384,4,64]{2,0,1:T(8,128)(2,1)} %get-tuple-element.77), kind=kOutput, calls=%fused_computation.196 | convolution fusion | flops 614991360 | bytes 10819584 | tf_op jit(solution)/shard_map/sub | solution.py:50
  226.9 5.5 %fusion.32 = bf16[128,4,384]{2,0,1:T(8,128)(2,1)} fusion(f32[4,384,1536]{1,2,0:T(8,128)} %get-tuple-element.130, f32[4,384]{1,0:T(4,128)S(1)} %get-tuple-element.129, bf16[384,128]{0,1:T(8,128)(2,1)} %bitcast.163, bf16[1152,128]{0,1:T(8,128)(2,1)} %scatter.20), kind=kOutput, calls=%fused_computation.45 | convolution fusion | flops 609681408 | bytes 10229760 | tf_op jit(solution)/shard_map/hck,kd->chd/dot_general | solution.py:51
  233.7 8.3 %fusion.146 = (f32[4,384]{1,0:T(4,128)S(1)}, f32[4,384,1536]{1,2,0:T(8,128)}) fusion(pred[384,1536]{0,1:T(8,128)(4,1)S(1)} %copy-done.2, bf16[384,128]{0,1:T(8,128)(2,1)} %bitcast.161, bf16[1152,128]{0,1:T(8,128)(2,1)} %fusion.107, bf16[384,4,64]{2,0,1:T(8,128)(2,1)} %get-tuple-element.80, bf16[384,4,64]{2,0,1:T(8,128)(2,1)S(1)} %copy-done.3), kind=kOutput, calls=%fused_computation.195 | convolution fusion | flops 614991360 | bytes 10819584 | tf_op jit(solution)/shard_map/sub | solution.py:50
  242.0 4.7 fusion.31
  248.0 8.3 %fusion.141 = (f32[4,384]{1,0:T(4,128)S(1)}, f32[4,384,1536]{1,2,0:T(8,128)}) fusion(pred[384,1536]{0,1:T(8,128)(4,1)S(1)} %copy-done.1, bf16[384,128]{0,1:T(8,128)(2,1)S(1)} %bitcast.162, bf16[1152,128]{0,1:T(8,128)(2,1)} %fusion.108, bf16[384,4,64]{2,0,1:T(8,128)(2,1)S(1)} %get-tuple-element.82, bf16[384,4,64]{2,0,1:T(8,128)(2,1)S(1)} %get-tuple-element.81), kind=kOutput, calls=%fused_computation.194 | convolution fusion | flops 614991360 | bytes 10819584 | tf_op jit(solution)/shard_map/sub | solution.py:50
  256.3 4.6 fusion.30
  260.9 9.5 %convolution_convert_fusion = bf16[384,8192]{1,0:T(8,128)(2,1)} fusion(bf16[384,512]{0,1:T(8,128)(2,1)S(1)} %bitcast.158, bf16[1,512,8192]{2,1,0:T(8,128)(2,1)} %param.23), kind=kOutput, calls=%fused_computation.3 | convolution fusion | flops 3224371200 | bytes 15073280 | tf_op jit(solution)/shard_map/dot_general | solution.py:114
  270.5 9.5 %convolution_convert_fusion.1 = bf16[384,8192]{1,0:T(8,128)(2,1)} fusion(bf16[384,512]{0,1:T(8,128)(2,1)S(1)} %bitcast.157, bf16[1,512,8192]{2,1,0:T(8,128)(2,1)} %param.23), kind=kOutput, calls=%fused_computation.4 | convolution fusion | flops 3224371200 | bytes 15073280 | tf_op jit(solution)/shard_map/dot_general | solution.py:114
  280.1 9.5 %convolution_convert_fusion.2 = bf16[384,8192]{1,0:T(8,128)(2,1)} fusion(bf16[384,512]{0,1:T(8,128)(2,1)S(1)} %bitcast.156, bf16[1,512,8192]{2,1,0:T(8,128)(2,1)} %param.23), kind=kOutput, calls=%fused_computation.5 | convolution fusion | flops 3224371200 | bytes 15073280 | tf_op jit(solution)/shard_map/dot_general | solution.py:114
  289.6 52.8 %reduce-scatter.8.cloned.1.call-done = bf16[24,8192]{1,0:T(8,128)(2,1)} async-done(((bf16[384,8192]{1,0:T(8,128)(2,1)}), bf16[24,8192]{1,0:T(8,128)(2,1)}) %reduce-scatter.8.cloned.1.call-update) | async-done | bytes 393232 | tf_op jit(solution)/shard_map/reduce_scatter | solution.py:116
  342.4 1.1 fusion.54
  343.5 70.6 %reduce-scatter.6.cloned.1.call-done = bf16[24,8192]{1,0:T(8,128)(2,1)} async-done(((bf16[384,8192]{1,0:T(8,128)(2,1)}), bf16[24,8192]{1,0:T(8,128)(2,1)}) %reduce-scatter.6.cloned.1.call-update) | async-done | bytes 393232 | tf_op jit(solution)/shard_map/reduce_scatter | solution.py:116
  414.1 1.1 fusion.55
  415.2 70.6 %reduce-scatter.4.cloned.1.call-done = bf16[24,8192]{1,0:T(8,128)(2,1)} async-done(((bf16[384,8192]{1,0:T(8,128)(2,1)}), bf16[24,8192]{1,0:T(8,128)(2,1)}) %reduce-scatter.4.cloned.1.call-update) | async-done | bytes 393232 | tf_op jit(solution)/shard_map/reduce_scatter | solution.py:116
  485.8 1.1 fusion.56
  486.8 1.1 maximum_bitcast_fusion
  (76 shorter events, 16.7 us)
Async XLA Ops:
  6.5 43.7 %copy-start.7 = (s32[1,3]{1,0:T(1,128)S(1)}, s32[1,3]{1,0:T(1,128)}, u32[]{:S(2)}) copy-start(s32[1,3]{1,0:T(1,128)} %param.25) | copy-start | bytes 40
  6.5 76.8 %all-gather.4.cloned.1.call-start = ((), (), s32[]{:S(2)}) async-start(), calls=%async_computation.3 | async-start | bytes 6684672 | tf_op jit(solution)/shard_map/all_gather | solution.py:84
  7.9 15.7 %collective-permute-start.4 = (bf16[24,8192]{1,0:T(8,128)(2,1)S(1)}, bf16[24,8192]{1,0:T(8,128)(2,1)S(1)}, u32[]{:S(2)}, u32[]{:S(2)}) collective-permute-start(bf16[24,8192]{1,0:T(8,128)(2,1)S(1)} %get-tuple-element.85), channel_id=1, source_target_pairs={{0,16},{16,32},{32,48},{48,64},{64,80},{80,96},{96,112},{112,0},{1... | collective-permute-start | bytes 1179656 | tf_op jit(solution)/shard_map/ppermute | solution.py:19
  9.5 22.5 %collective-permute-start.2 = (bf16[24,8192]{1,0:T(8,128)(2,1)S(1)}, bf16[24,8192]{1,0:T(8,128)(2,1)S(1)}, u32[]{:S(2)}, u32[]{:S(2)}) collective-permute-start(bf16[24,8192]{1,0:T(8,128)(2,1)S(1)} %get-tuple-element.87), channel_id=1, source_target_pairs={{0,16},{16,32},{32,48},{48,64},{64,80},{80,96},{96,112},{112,0},{1... | collective-permute-start | bytes 1179656 | tf_op jit(solution)/shard_map/ppermute | solution.py:19
  11.0 28.4 %collective-permute-start = (bf16[24,8192]{1,0:T(8,128)(2,1)S(1)}, bf16[24,8192]{1,0:T(8,128)(2,1)S(1)}, u32[]{:S(2)}, u32[]{:S(2)}) collective-permute-start(bf16[24,8192]{1,0:T(8,128)(2,1)S(1)} %get-tuple-element.86), channel_id=1, source_target_pairs={{0,16},{16,32},{32,48},{48,64},{64,80},{80,96},{96,112},{112,0},{1... | collective-permute-start | bytes 1179656 | tf_op jit(solution)/shard_map/ppermute | solution.py:19
  40.8 87.5 %all-gather.6.cloned.1.call-start = ((), (), s32[]{:S(2)}) async-start(), calls=%async_computation.5 | async-start | bytes 6684672 | tf_op jit(solution)/shard_map/all_gather | solution.py:84
  41.6 131.7 %all-gather.8.cloned.1.call-start = ((), (), s32[]{:S(2)}) async-start(), calls=%async_computation.7 | async-start | bytes 6684672 | tf_op jit(solution)/shard_map/all_gather | solution.py:84
  42.3 300.1 %reduce-scatter.8.cloned.1.call-start = ((), (), s32[]{:S(2)}) async-start(), calls=%async_computation.8 | async-start | bytes 6684672 | tf_op jit(solution)/shard_map/reduce_scatter | solution.py:116
  94.1 45.0 %copy-start = (f32[384,640]{1,0:T(8,128)}, f32[384,640]{1,0:T(8,128)S(1)}, u32[]{:S(2)}) copy-start(f32[384,640]{1,0:T(8,128)S(1)} %fusion.29) | copy-start | bytes 2949124
  139.9 58.8 %slice-start = ((f32[384,640]{1,0:T(8,128)}), f32[384,512]{1,0:T(8,128)S(1)}, s32[]{:S(2)}) async-start(f32[384,640]{1,0:T(8,128)} %copy-done), calls=%async_computation.9 | async-start | bytes 1572864 | tf_op jit(solution)/shard_map/slice | solution.py:89
  197.9 14.2 %collective-permute-start.1 = (bf16[384,128]{1,0:T(8,128)(2,1)}, bf16[384,128]{1,0:T(8,128)(2,1)}, u32[]{:S(2)}, u32[]{:S(2)}) collective-permute-start(bf16[384,128]{1,0:T(8,128)(2,1)} %slice.289), channel_id=1, source_target_pairs={{0,1},{1,0},{2,3},{3,2},{4,5},{5,4},{6,7},{7,6},{8,9},{9,8},{10,11... | collective-permute-start | bytes 294920 | tf_op jit(solution)/shard_map/ppermute | solution.py:14
  198.2 15.0 %collective-permute-start.5 = (bf16[384,128]{1,0:T(8,128)(2,1)}, bf16[384,128]{1,0:T(8,128)(2,1)}, u32[]{:S(2)}, u32[]{:S(2)}) collective-permute-start(bf16[384,128]{1,0:T(8,128)(2,1)} %slice.287), channel_id=1, source_target_pairs={{0,1},{1,0},{2,3},{3,2},{4,5},{5,4},{6,7},{7,6},{8,9},{9,8},{10,11... | collective-permute-start | bytes 294920 | tf_op jit(solution)/shard_map/ppermute | solution.py:14
  198.4 15.9 %collective-permute-start.3 = (bf16[384,128]{1,0:T(8,128)(2,1)}, bf16[384,128]{1,0:T(8,128)(2,1)}, u32[]{:S(2)}, u32[]{:S(2)}) collective-permute-start(bf16[384,128]{1,0:T(8,128)(2,1)} %slice.288), channel_id=1, source_target_pairs={{0,1},{1,0},{2,3},{3,2},{4,5},{5,4},{6,7},{7,6},{8,9},{9,8},{10,11... | collective-permute-start | bytes 294920 | tf_op jit(solution)/shard_map/ppermute | solution.py:14
  226.9 6.8 %copy-start.2 = (pred[384,1536]{0,1:T(8,128)(4,1)S(1)}, pred[384,1536]{0,1:T(8,128)(4,1)}, u32[]{:S(2)}) copy-start(pred[384,1536]{0,1:T(8,128)(4,1)} %get-tuple-element.106) | copy-start | bytes 1769476
  226.9 6.8 %copy-start.3 = (bf16[384,4,64]{2,0,1:T(8,128)(2,1)S(1)}, bf16[384,4,64]{2,0,1:T(8,128)(2,1)}, u32[]{:S(2)}) copy-start(bf16[384,4,64]{2,0,1:T(8,128)(2,1)} %get-tuple-element.79) | copy-start | bytes 589828
  242.0 6.1 %copy-start.1 = (pred[384,1536]{0,1:T(8,128)(4,1)S(1)}, pred[384,1536]{0,1:T(8,128)(4,1)}, u32[]{:S(2)}) copy-start(pred[384,1536]{0,1:T(8,128)(4,1)} %get-tuple-element.107) | copy-start | bytes 1769476
  242.0 6.1 %copy-start.5 = (bf16[1,1,384,128]{2,3,1,0:T(8,128)(2,1)S(1)}, bf16[1,1,384,128]{2,3,1,0:T(8,128)(2,1)}, u32[]{:S(2)}) copy-start(bf16[1,1,384,128]{2,3,1,0:T(8,128)(2,1)} %copy.60) | copy-start | bytes 294916
  246.7 9.6 %copy-start.6 = (bf16[1,1,384,128]{2,3,1,0:T(8,128)(2,1)S(1)}, bf16[1,1,384,128]{2,3,1,0:T(8,128)(2,1)}, u32[]{:S(2)}) copy-start(bf16[1,1,384,128]{2,3,1,0:T(8,128)(2,1)} %copy.56) | copy-start | bytes 294916
  270.5 143.6 %reduce-scatter.6.cloned.1.call-start = ((), (), s32[]{:S(2)}) async-start(), calls=%async_computation.6 | async-start | bytes 6684672 | tf_op jit(solution)/shard_map/reduce_scatter | solution.py:116
  270.5 9.6 %copy-start.4 = (bf16[128,4,384]{2,0,1:T(8,128)(2,1)S(1)}, bf16[128,4,384]{2,0,1:T(8,128)(2,1)}, u32[]{:S(2)}) copy-start(bf16[128,4,384]{2,0,1:T(8,128)(2,1)} %fusion.32) | copy-start | bytes 1179652
  280.1 205.7 %reduce-scatter.4.cloned.1.call-start = ((), (), s32[]{:S(2)}) async-start(), calls=%async_computation.4 | async-start | bytes 6684672 | tf_op jit(solution)/shard_map/reduce_scatter | solution.py:116
Sparse Core Ops, SparseCore 0:
  41.0 42.3 all-gather.3
  85.0 43.2 all-gather.5
  130.0 43.2 all-gather.7
  270.6 71.7 reduce-scatter.7
  344.7 69.3 reduce-scatter.5
  416.4 69.3 reduce-scatter.3
where the time goes:
time: 500 us; the launch traced here: 495 us
  waiting for transfers between devices  312 us (62%)
  matrix products  113 us (23%)
  local copies, waits for them, and re-layouts  25.6 us (5%)
  other arithmetic  25.4 us (5%)
  between operations  14 us (3%)
  starting transfers between devices  5.3 us (1%)
    reduce_scatter x3, waiting for transfers between devices, shards(): lax.psum_scatter(term_rows(jnp.int32(0), lax.axis_size('tensor') * handed...  194 us
    all_gather x3, waiting for transfers between devices, shards(): lax.all_gather(normed, 'tensor', axis=0, tiled=True)  90.4 us
    dot_general x3, matrix products, shards(): jnp.dot(lax.all_gather(normed, 'tensor', axis=0, tiled=True), combined, p...  44.6 us
    dot_general x3, matrix products, term_rows(): return jnp.dot(attended, w_out[0], preferred_element_type=jnp.float32)  28.5 us
    ppermute x3, waiting for transfers between devices, from_behind(): lax.ppermute(value, axis, [(i, (i + by) % devices) for i in range(devices)])  25.9 us
    sub x3, matrix products, attend(): weights = jax.nn.softmax(scores, axis=-1).astype(jnp.bfloat16)  25.2 us
    dot_general x3, matrix products, attend(): jnp.einsum('hck,kd->chd', weights, value_block, preferred_element_type=jn...  14.8 us
  transfers between devices with their start and end apart: 12, of which 9 were waited for; matrix products, arithmetic and copies ran while one was open for 16% of the time, Pallas kernels for 0%

commit v1 on v0

v1 whole, which is shorter than its diff:
```python
import functools
import math

import jax
import jax.numpy as jnp
from jax import lax
from jax.experimental import pallas as pl
from jax.experimental.pallas import tpu as pltpu
from jax.sharding import PartitionSpec as P

HD = 128
BLOCK = 384
CACHE = 384
D = 8192
HALF = D // 2
NZ = 4
ROWS = 192
PIECE = 48
K_CHUNK = 1024
N_CHUNK = 1024
SLOTS = (0, -1, 1, 2)


def tensor_index(y, z, c):
    return (y * NZ + z % NZ) * 2 + c


def move(value, dy=0, dz=0, dc=0):
    pairs = []
    for y in range(2):
        for z in range(NZ):
            for c in range(2):
                pairs.append((tensor_index(y, z, c), tensor_index(y ^ dy, z + dz, c ^ dc)))
    return lax.ppermute(value, "tensor", pairs)


def from_behind(value, axis, by):
    devices = lax.axis_size(axis)
    return lax.ppermute(value, axis, [(i, (i + by) % devices) for i in range(devices)])


def normalize(handed, gain):
    widened = handed.astype(jnp.float32)
    return (
        widened
        * lax.rsqrt(jnp.mean(widened * widened, axis=-1, keepdims=True) + 1e-05)
        * gain.astype(jnp.float32)
    ).astype(jnp.bfloat16)


def project_kernel(
    core, own, left, right, far_a, far_b, wq_mine, wq_other, wkv_mine, wkv_other, cosine, sine,
    query, kv, acc_q, acc_kv,
):
    step = pl.program_id(0)
    steps = pl.num_programs(0)
    far = jnp.where(step < steps // 2, far_a[...], far_b[...])
    x = jnp.concatenate([own[...], left[...], right[...], far], axis=0)

    @pl.when(step == 0)
    def _():
        acc_q[...] = jnp.zeros_like(acc_q)
        acc_kv[...] = jnp.zeros_like(acc_kv)

    for half, (wq, wkv) in enumerate(((wq_mine, wkv_mine), (wq_other, wkv_other))):
        acc_q[:, half * 512 : half * 512 + 512] += jnp.dot(
            x, wq[...], preferred_element_type=jnp.float32
        )
        acc_kv[:, half * HD : half * HD + HD] += jnp.dot(
            x, wkv[...], preferred_element_type=jnp.float32
        )

    @pl.when(step == steps - 1)
    def _():
        cos = cosine[...]
        sin = sine[...]

        def turn(u):
            return u * cos + pltpu.roll(u, HD // 2, 1) * sin

        for head in range(8):
            query[head] = turn(acc_q[:, head * HD : head * HD + HD]).astype(jnp.bfloat16)
        mine = acc_kv[:, :HD]
        other = acc_kv[:, HD:]
        first = core[0] == 0
        low = jnp.where(first, mine, other)
        high = jnp.where(first, other, mine)
        lower = lax.broadcasted_iota(jnp.int32, (ROWS, HD), 1) < HD // 2
        keys = jnp.where(lower, low, pltpu.roll(high, HD // 2, 1))
        values = jnp.where(lower, pltpu.roll(low, HD // 2, 1), high)
        keys = keys.astype(jnp.bfloat16).astype(jnp.float32)
        kv[0] = turn(keys).astype(jnp.bfloat16)
        kv[1] = values.astype(jnp.bfloat16)


def project(core, pieces, weights, cosine, sine):
    steps = D // K_CHUNK
    near = pl.BlockSpec((PIECE, K_CHUNK), lambda k, c: (0, k))
    specs = [near, near, near]
    specs.append(pl.BlockSpec((PIECE, K_CHUNK), lambda k, c: (0, jnp.minimum(k, steps // 2 - 1))))
    specs.append(pl.BlockSpec((PIECE, K_CHUNK), lambda k, c: (0, jnp.maximum(k - steps // 2, 0))))
    for w in weights:
        specs.append(pl.BlockSpec((K_CHUNK, w.shape[1]), lambda k, c: (k, 0)))
    table = pl.BlockSpec((ROWS, HD), lambda k, c: (0, 0))
    specs += [table, table]
    return pl.pallas_call(
        project_kernel,
        out_shape=(
            jax.ShapeDtypeStruct((8, ROWS, HD), jnp.bfloat16),
            jax.ShapeDtypeStruct((2, ROWS, HD), jnp.bfloat16),
        ),
        grid_spec=pltpu.PrefetchScalarGridSpec(
            num_scalar_prefetch=1,
            grid=(steps,),
            in_specs=specs,
            out_specs=(
                pl.BlockSpec((8, ROWS, HD), lambda k, c: (0, 0, 0)),
                pl.BlockSpec((2, ROWS, HD), lambda k, c: (0, 0, 0)),
            ),
            scratch_shapes=[
                pltpu.VMEM((ROWS, 1024), jnp.float32),
                pltpu.VMEM((ROWS, 2 * HD), jnp.float32),
            ],
        ),
        compiler_params=pltpu.CompilerParams(vmem_limit_bytes=40 * 2**20),
        cost_estimate=pl.CostEstimate(
            flops=2 * ROWS * D * 1280, bytes_accessed=24 * 2**20, transcendentals=0
        ),
        name="project",
    )(core, *pieces, *weights, cosine, sine)


def attend_kernel(blocks, scalars, query, cache, q_place, k_place, *refs):
    windows = refs[: 2 * blocks]
    wo_mine, wo_other = refs[2 * blocks : 2 * blocks + 2]
    own, minus, plus, far_a, far_b = refs[2 * blocks + 2 : 2 * blocks + 7]
    attended, wo, sems = refs[2 * blocks + 7 :]
    step = pl.program_id(0)
    steps = pl.num_programs(0)

    def fetch(n, half):
        source = (wo_mine, wo_other)[half]
        return pltpu.make_async_copy(
            source.at[:, pl.ds(pl.multiple_of(n * N_CHUNK, N_CHUNK), N_CHUNK)],
            wo.at[n, pl.ds(half * 512, 512), :],
            sems.at[n, half],
        )

    @pl.when(step == 0)
    def _():
        for n in range(D // N_CHUNK):
            fetch(n, 0).start()
            fetch(n, 1).start()
        scale = math.log2(math.e) / math.sqrt(HD)
        slot = lax.broadcasted_iota(jnp.int32, (1, CACHE), 1)
        cache_bias = jnp.where(slot < scalars[1], 0.0, -1e30)
        causal_bias = jnp.where(k_place[...] <= q_place[...], 0.0, -1e30)
        keys = [cache[0]] + [w[0] for w in windows]
        values = [cache[1]] + [w[1] for w in windows]
        keys = jnp.concatenate(keys, axis=0)
        values = jnp.concatenate(values, axis=0)
        before = CACHE + (blocks - 1) * BLOCK
        for head in range(8):
            scores = lax.dot_general(
                query[head], keys, (((1,), (1,)), ((), ())), preferred_element_type=jnp.float32
            )
            parts = [scores[:, :CACHE] + cache_bias]
            if blocks > 1:
                parts.append(scores[:, CACHE:before])
            parts.append(scores[:, before:] + causal_bias)
            scores = jnp.concatenate(parts, axis=1)
            top = jnp.max(scores, axis=1, keepdims=True)
            grown = jnp.exp2((scores - top) * scale)
            total = jnp.sum(grown, axis=1, keepdims=True)
            out = jnp.dot(grown.astype(jnp.bfloat16), values, preferred_element_type=jnp.float32)
            attended[:, head * HD : head * HD + HD] = (out / total).astype(jnp.bfloat16)

    fetch(step, 0).wait()
    fetch(step, 1).wait()
    term = jnp.dot(attended[...], wo[step], preferred_element_type=jnp.float32).astype(jnp.bfloat16)
    own[...] = term[:PIECE]
    minus[...] = term[PIECE : 2 * PIECE]
    plus[...] = term[2 * PIECE : 3 * PIECE]

    @pl.when(step < steps // 2)
    def _():
        far_a[...] = term[3 * PIECE :]

    @pl.when(step >= steps // 2)
    def _():
        far_b[...] = term[3 * PIECE :]


def attend(scalars, query, cache, q_place, k_place, windows, wo_mine, wo_other):
    steps = D // N_CHUNK
    blocks = len(windows) // 2
    whole = lambda a: pl.BlockSpec(a.shape, lambda n, s: (0,) * a.ndim)
    specs = [
        whole(query),
        pl.BlockSpec((2, CACHE, HD), lambda n, s: (0, 0, s[0])),
        whole(q_place),
        whole(k_place),
        *[whole(w) for w in windows],
        pl.BlockSpec(memory_space=pl.ANY),
        pl.BlockSpec(memory_space=pl.ANY),
    ]
    near = pl.BlockSpec((PIECE, N_CHUNK), lambda n, s: (0, n))
    full = jax.ShapeDtypeStruct((PIECE, D), jnp.bfloat16)
    half = jax.ShapeDtypeStruct((PIECE, HALF), jnp.bfloat16)
    keys = CACHE + blocks * BLOCK
    return pl.pallas_call(
        functools.partial(attend_kernel, blocks),
        out_shape=(full, full, full, half, half),
        grid_spec=pltpu.PrefetchScalarGridSpec(
            num_scalar_prefetch=1,
            grid=(steps,),
            in_specs=specs,
            out_specs=(
                near,
                near,
                near,
                pl.BlockSpec((PIECE, N_CHUNK), lambda n, s: (0, jnp.minimum(n, steps // 2 - 1))),
                pl.BlockSpec((PIECE, N_CHUNK), lambda n, s: (0, jnp.maximum(n - steps // 2, 0))),
            ),
            scratch_shapes=[
                pltpu.VMEM((ROWS, 1024), jnp.bfloat16),
                pltpu.VMEM((steps, 1024, N_CHUNK), jnp.bfloat16),
                pltpu.SemaphoreType.DMA((steps, 2)),
            ],
        ),
        compiler_params=pltpu.CompilerParams(vmem_limit_bytes=52 * 2**20),
        cost_estimate=pl.CostEstimate(
            flops=2 * ROWS * D * 1024 + 4 * 8 * ROWS * keys * HD,
            bytes_accessed=21 * 2**20,
            transcendentals=8 * ROWS * keys,
        ),
        name="attend",
    )(scalars, query, cache, q_place, k_place, *windows, wo_mine, wo_other)


def shards(incoming, norm_gain, w_query, w_key_value, w_out, kv_cache, offsets):
    index = lax.axis_index("tensor")
    core = index % 2
    z = index // 2 % NZ
    y = index // (2 * NZ)
    head = index // 2
    offset = offsets[0, 0]
    handed = [from_behind(incoming[0, which], "section", 1) for which in range(3)]

    wkv = w_key_value[0].reshape(D, 2 * w_key_value.shape[3])
    wq = w_query[0]
    wo = w_out[0]
    wq_other = move(wq, dc=1)
    wkv_other = move(wkv, dc=1)
    wo_other = move(wo, dc=1)
    weights = (wq, wq_other, wkv, wkv_other)

    within = jnp.arange(24, dtype=jnp.int32)

    def places(c):
        return jnp.concatenate(
            [tensor_index(y ^ dy, z + dz, c) * 24 + within for dz in SLOTS for dy in range(2)]
        )

    mine = places(core)
    other = places(1 - core)
    q_place = mine[:, None]
    k_place = jnp.concatenate([mine, other])[None, :]
    freq = 500000.0 ** (-jnp.arange(HD // 2, dtype=jnp.float32) * 2.0 / HD)
    cosines = []
    sines = []
    for which in range(3):
        angle = (offsets[0, which] + mine).astype(jnp.float32)[:, None] * freq
        cos = jnp.cos(angle)
        sin = jnp.sin(angle)
        cosines.append(jnp.concatenate([cos, cos], axis=1))
        sines.append(jnp.concatenate([-sin, sin], axis=1))
    core_scalar = core.reshape(1)
    scalars = jnp.stack([head, offset])
    cache = kv_cache[0]

    windows = []
    results = []
    for which in range(3):
        normed = normalize(handed[which], norm_gain[0])
        own = jnp.concatenate([normed, move(normed, dy=1)], axis=0)
        left = move(own, dz=1)
        right = move(own, dz=-1)
        far_a = move(left[:, :HALF], dz=1)
        far_b = move(right[:, HALF:], dz=-1)
        query, kv = project(
            core_scalar, (own, left, right, far_a, far_b), weights, cosines[which], sines[which]
        )
        windows += [kv, move(kv, dc=1)]
        own, minus, plus, far_a, far_b = attend(
            scalars, query, cache, q_place, k_place, tuple(windows), wo, wo_other
        )
        far_a = move(far_a, dz=1)
        far_b = move(far_b, dz=-1)
        f32 = lambda a: a.astype(jnp.float32)
        plus = jnp.concatenate(
            [(f32(plus[:, :HALF]) + f32(far_a)).astype(jnp.bfloat16), plus[:, HALF:]], axis=1
        )
        minus = jnp.concatenate(
            [minus[:, :HALF], (f32(minus[:, HALF:]) + f32(far_b)).astype(jnp.bfloat16)], axis=1
        )
        summed = f32(own) + f32(move(plus, dz=1)) + f32(move(minus, dz=-1))
        passed = move(summed[24:].astype(jnp.bfloat16), dy=1)
        results.append(
            (f32(handed[which]) + summed[:24] + f32(passed)).astype(jnp.bfloat16)
        )
    return jnp.stack(results)[None]


def solution(mesh):
    placed = (
        P("section", None, "tensor", None),
        P("section", None),
        P("section", None, "tensor"),
        P("section", None, None, "tensor"),
        P("section", "tensor", None),
        P("section", None, None, None),
        P("section", None),
    )
    return jax.shard_map(
        shards,
        mesh=mesh,
        in_specs=placed,
        out_specs=P("section", None, "tensor", None),
        check_vma=False,
    )
```

time: 500 us -> 292 us (0.58)
  waiting for transfers between devices: 312 us -> 134 us
  matrix products: 113 us -> 0 us
  Pallas kernels: 0 us -> 70.5 us
  starting transfers between devices: 5.3 us -> 51.7 us
  between operations: 14 us -> 0.87 us
  other arithmetic: 25.4 us -> 12.9 us
    reduce_scatter x3 -> x0, waiting for transfers between devices: 194 us -> none  [shards(): lax.psum_scatter(term_rows(jnp.int32(0), lax.axis_size('tensor') * handed...]
    ppermute x3 -> x36, waiting for transfers between devices: 0.01 us -> 110 us  [move(): return lax.ppermute(value, 'tensor', pairs)]
    all_gather x3 -> x0, waiting for transfers between devices: 90.4 us -> none  [shards(): lax.all_gather(normed, 'tensor', axis=0, tiled=True)]
    dot_general x9 -> x0, matrix products: 87.9 us -> none  [the longest x3 44.6 us: shards(): jnp.dot(lax.all_gather(normed, 'tensor', axis=0, tiled=True), combined, p...]
    pallas_call x0 -> x6, Pallas kernels: none -> 70.5 us  [the longest x3 35.7 us: project(): pl.pallas_call(project_kernel, out_shape=(jax.ShapeDtypeStruct((8, ROWS,...]
    ppermute x3 -> x36, starting transfers between devices: 0.77 us -> 47.4 us  [move(): return lax.ppermute(value, 'tensor', pairs)]
    sub x3 -> x0, matrix products: 25.2 us -> none  [attend(): weights = jax.nn.softmax(scores, axis=-1).astype(jnp.bfloat16)]
    another operation x5 -> x1, other arithmetic: 7.26 us -> 0.74 us  [shards(): scalars = jnp.stack([head, offset])]
  transfers between devices with their start and end apart: 12 -> 39, of which waited for: 9 -> 22; matrix products, arithmetic and copies ran while one was open for 16% -> 10% of each run, Pallas kernels for 0% -> 20%
where the time goes in v1:
time: 292 us; the launch traced here: 291 us
  waiting for transfers between devices  134 us (46%)
  Pallas kernels  70.5 us (24%)
  starting transfers between devices  51.7 us (18%)
  local copies, waits for them, and re-layouts  21.1 us (7%)
  other arithmetic  12.9 us (4%)
    ppermute x36, waiting for transfers between devices, move(): return lax.ppermute(value, 'tensor', pairs)  110 us
    ppermute x36, starting transfers between devices, move(): return lax.ppermute(value, 'tensor', pairs)  47.4 us
    pallas_call x3, Pallas kernels, project(): pl.pallas_call(project_kernel, out_shape=(jax.ShapeDtypeStruct((8, ROWS,...  35.7 us
    pallas_call x3, Pallas kernels, attend(): pl.pallas_call(functools.partial(attend_kernel, blocks), out_shape=(full,...  34.8 us
    ppermute x3, waiting for transfers between devices, from_behind(): lax.ppermute(value, axis, [(i, (i + by) % devices) for i in range(devices)])  24.1 us
  transfers between devices with their start and end apart: 39, of which 22 were waited for; matrix products, arithmetic and copies ran while one was open for 10% of the time, Pallas kernels for 20%

profile of v1, /device:TPU:0, one launch (start us, length us, event | category | flops | bytes accessed | tf_op | source)
XLA Modules:
  0.0 291.1 jit_solution(9779271702553509647)
XLA Ops:
  0.0 2.3 slice_bitcast_fusion.1
  2.3 1.6 collective-permute-start.15
  6.7 3.2 %copy.10.wkv_mine = bf16[8192,128]{1,0:T(8,128)(2,1)S(1)} copy(bf16[8192,128]{0,1:T(8,128)(2,1)} %bitcast.37) | data formatting | bytes 4194304 | tf_op jit(solution)/shard_map/reshape;squeeze | solution.py:250
  10.0 7.9 %collective-permute-done.15 = bf16[24,8192]{1,0:T(8,128)(2,1)S(1)} collective-permute-done((bf16[24,8192]{1,0:T(8,128)(2,1)}, bf16[24,8192]{1,0:T(8,128)(2,1)S(1)}, u32[]{:S(2)}, u32[]{:S(2)}) %collective-permute-start.15) | collective-permute-done | bytes 393248 | tf_op jit(solution)/shard_map/ppermute | solution.py:39
  18.2 8.2 %collective-permute-done.27 = bf16[24,8192]{1,0:T(8,128)(2,1)S(1)} collective-permute-done((bf16[24,8192]{1,0:T(8,128)(2,1)}, bf16[24,8192]{1,0:T(8,128)(2,1)S(1)}, u32[]{:S(2)}, u32[]{:S(2)}) %collective-permute-start.27) | collective-permute-done | bytes 393248 | tf_op jit(solution)/shard_map/ppermute | solution.py:39
  26.6 8.0 %collective-permute-done = bf16[24,8192]{1,0:T(8,128)(2,1)S(1)} collective-permute-done((bf16[24,8192]{1,0:T(8,128)(2,1)}, bf16[24,8192]{1,0:T(8,128)(2,1)S(1)}, u32[]{:S(2)}, u32[]{:S(2)}) %collective-permute-start) | collective-permute-done | bytes 393248 | tf_op jit(solution)/shard_map/ppermute | solution.py:39
  35.2 1.6 collective-permute-start.28
  38.0 1.5 collective-permute-start.16
  39.5 7.8 %collective-permute-done.28 = bf16[24,8192]{1,0:T(8,128)(2,1)S(1)} collective-permute-done((bf16[24,8192]{1,0:T(8,128)(2,1)S(1)}, bf16[24,8192]{1,0:T(8,128)(2,1)S(1)}, u32[]{:S(2)}, u32[]{:S(2)}) %collective-permute-start.28) | collective-permute-done | bytes 393248 | tf_op jit(solution)/shard_map/ppermute | solution.py:34
  47.3 2.0 collective-permute-start.29
  49.3 6.4 %collective-permute-done.1 = bf16[24,8192]{1,0:T(8,128)(2,1)S(1)} collective-permute-done((bf16[24,8192]{1,0:T(8,128)(2,1)S(1)}, bf16[24,8192]{1,0:T(8,128)(2,1)S(1)}, u32[]{:S(2)}, u32[]{:S(2)}) %collective-permute-start.1) | collective-permute-done | bytes 393248 | tf_op jit(solution)/shard_map/ppermute | solution.py:34
  55.7 4.0 %collective-permute-start.30 = (bf16[48,8192]{1,0:T(8,128)(2,1)S(1)}, bf16[48,8192]{1,0:T(8,128)(2,1)S(1)}, u32[]{:S(2)}, u32[]{:S(2)}) collective-permute-start(bf16[48,8192]{1,0:T(8,128)(2,1)S(1)} %pad_maximum_fusion.6.own), channel_id=1, source_target_pairs={{0,6},{1,7},{2,0},{3,1},{4,2},{5,3},{6,4},{7,5},{8,14},{9,15},{10,... | collective-permute-start | bytes 2359304 | tf_op jit(solution)/shard_map/ppermute | solution.py:34
  59.8 3.2 %collective-permute-done.16 = bf16[24,8192]{1,0:T(8,128)(2,1)S(1)} collective-permute-done((bf16[24,8192]{1,0:T(8,128)(2,1)S(1)}, bf16[24,8192]{1,0:T(8,128)(2,1)S(1)}, u32[]{:S(2)}, u32[]{:S(2)}) %collective-permute-start.16) | collective-permute-done | bytes 393248 | tf_op jit(solution)/shard_map/ppermute | solution.py:34
  63.0 3.8 %collective-permute-done.29.left = bf16[48,8192]{1,0:T(8,128)(2,1)S(1)} collective-permute-done((bf16[48,8192]{1,0:T(8,128)(2,1)S(1)}, bf16[48,8192]{1,0:T(8,128)(2,1)S(1)}, u32[]{:S(2)}, u32[]{:S(2)}) %collective-permute-start.29) | collective-permute-done | bytes 786464 | tf_op jit(solution)/shard_map/ppermute | solution.py:34
  66.8 7.6 %collective-permute-done.30.right = bf16[48,8192]{1,0:T(8,128)(2,1)S(1)} collective-permute-done((bf16[48,8192]{1,0:T(8,128)(2,1)S(1)}, bf16[48,8192]{1,0:T(8,128)(2,1)S(1)}, u32[]{:S(2)}, u32[]{:S(2)}) %collective-permute-start.30) | collective-permute-done | bytes 786464 | tf_op jit(solution)/shard_map/ppermute | solution.py:34
  74.4 3.7 %collective-permute-start.3 = (bf16[48,8192]{1,0:T(8,128)(2,1)S(1)}, bf16[48,8192]{1,0:T(8,128)(2,1)S(1)}, u32[]{:S(2)}, u32[]{:S(2)}) collective-permute-start(bf16[48,8192]{1,0:T(8,128)(2,1)S(1)} %pad_maximum_fusion.own), channel_id=1, source_target_pairs={{0,6},{1,7},{2,0},{3,1},{4,2},{5,3},{6,4},{7,5},{8,14},{9,15},{10,... | collective-permute-start | bytes 2359304 | tf_op jit(solution)/shard_map/ppermute | solution.py:34
  78.1 7.0 %collective-permute-done.2.left = bf16[48,8192]{1,0:T(8,128)(2,1)S(1)} collective-permute-done((bf16[48,8192]{1,0:T(8,128)(2,1)S(1)}, bf16[48,8192]{1,0:T(8,128)(2,1)S(1)}, u32[]{:S(2)}, u32[]{:S(2)}) %collective-permute-start.2) | collective-permute-done | bytes 786464 | tf_op jit(solution)/shard_map/ppermute | solution.py:34
  85.2 6.9 %collective-permute-done.3.right = bf16[48,8192]{1,0:T(8,128)(2,1)S(1)} collective-permute-done((bf16[48,8192]{1,0:T(8,128)(2,1)S(1)}, bf16[48,8192]{1,0:T(8,128)(2,1)S(1)}, u32[]{:S(2)}, u32[]{:S(2)}) %collective-permute-start.3) | collective-permute-done | bytes 786464 | tf_op jit(solution)/shard_map/ppermute | solution.py:34
  92.1 3.7 %collective-permute-start.18 = (bf16[48,8192]{1,0:T(8,128)(2,1)S(1)}, bf16[48,8192]{1,0:T(8,128)(2,1)S(1)}, u32[]{:S(2)}, u32[]{:S(2)}) collective-permute-start(bf16[48,8192]{1,0:T(8,128)(2,1)S(1)} %pad_maximum_fusion.3.own), channel_id=1, source_target_pairs={{0,6},{1,7},{2,0},{3,1},{4,2},{5,3},{6,4},{7,5},{8,14},{9,15},{10,... | collective-permute-start | bytes 2359304 | tf_op jit(solution)/shard_map/ppermute | solution.py:34
  95.8 1.9 add_convert_fusion.7
  97.7 1.9 fusion.19
  102.7 6.9 %collective-permute-done.18.right = bf16[48,8192]{1,0:T(8,128)(2,1)S(1)} collective-permute-done((bf16[48,8192]{1,0:T(8,128)(2,1)S(1)}, bf16[48,8192]{1,0:T(8,128)(2,1)S(1)}, u32[]{:S(2)}, u32[]{:S(2)}) %collective-permute-start.18) | collective-permute-done | bytes 786464 | tf_op jit(solution)/shard_map/ppermute | solution.py:34
  109.6 3.7 %collective-permute-start.5 = (bf16[48,4096]{1,0:T(8,128)(2,1)}, bf16[48,4096]{1,0:T(8,128)(2,1)}, u32[]{:S(2)}, u32[]{:S(2)}) collective-permute-start(bf16[48,4096]{1,0:T(8,128)(2,1)} %slice.125), channel_id=1, source_target_pairs={{0,6},{1,7},{2,0},{3,1},{4,2},{5,3},{6,4},{7,5},{8,14},{9,15},{10,... | collective-permute-start | bytes 1179656 | tf_op jit(solution)/shard_map/ppermute | solution.py:34
  114.4 1.6 pad_maximum_fusion.10.sine
  117.0 1.8 slice.128
  120.8 3.7 %collective-permute-start.20 = (bf16[48,4096]{1,0:T(8,128)(2,1)}, bf16[48,4096]{1,0:T(8,128)(2,1)}, u32[]{:S(2)}, u32[]{:S(2)}) collective-permute-start(bf16[48,4096]{1,0:T(8,128)(2,1)} %slice.129), channel_id=1, source_target_pairs={{0,6},{1,7},{2,0},{3,1},{4,2},{5,3},{6,4},{7,5},{8,14},{9,15},{10,... | collective-permute-start | bytes 1179656 | tf_op jit(solution)/shard_map/ppermute | solution.py:34
  127.0 3.2 %collective-permute-start.32 = (bf16[48,4096]{1,0:T(8,128)(2,1)S(1)}, bf16[48,4096]{1,0:T(8,128)(2,1)S(1)}, u32[]{:S(2)}, u32[]{:S(2)}) collective-permute-start(bf16[48,4096]{1,0:T(8,128)(2,1)S(1)} %slice.133), channel_id=1, source_target_pairs={{0,6},{1,7},{2,0},{3,1},{4,2},{5,3},{6,4},{7,5},{8,14},{9,15},{10,... | collective-permute-start | bytes 1179656 | tf_op jit(solution)/shard_map/ppermute | solution.py:34
  132.3 12.0 %project.3 = (bf16[8,192,128]{2,1,0:T(8,128)(2,1)S(1)}, bf16[2,192,128]{2,1,0:T(8,128)(2,1)S(1)}) custom-call(s32[1]{0:T(128)} %bitcast.3.core, bf16[48,8192]{1,0:T(8,128)(2,1)S(1)} %copy-done.1, bf16[48,8192]{1,0:T(8,128)(2,1)S(1)} %copy-done.11, bf16[48,8192]{1,0:T(8,128)(2,1)S(1)} %copy-done.16, bf16[48,4096]{1,0:T(8,128)(2,1)} %collective-permute-done.4.far_a, ...), custom_call_target="tpu_custom_call" | custom-call | flops 4026531840 | bytes 25165824 | tf_op jit(solution)/shard_map/project/pallas_call | solution.py:106
  144.7 11.9 %project.4 = (bf16[8,192,128]{2,1,0:T(8,128)(2,1)S(1)}, bf16[2,192,128]{2,1,0:T(8,128)(2,1)S(1)}) custom-call(s32[1]{0:T(128)} %bitcast.3.core, bf16[48,8192]{1,0:T(8,128)(2,1)S(1)} %copy-done.3, bf16[48,8192]{1,0:T(8,128)(2,1)S(1)} %copy-done.9, bf16[48,8192]{1,0:T(8,128)(2,1)S(1)} %copy-done.14, bf16[48,4096]{1,0:T(8,128)(2,1)} %collective-permute-done.19.far_a, ...), custom_call_target="tpu_custom_call" | custom-call | flops 4026531840 | bytes 25165824 | tf_op jit(solution)/shard_map/project/pallas_call | solution.py:106
  157.1 11.8 %project.5 = (bf16[8,192,128]{2,1,0:T(8,128)(2,1)S(1)}, bf16[2,192,128]{2,1,0:T(8,128)(2,1)S(1)}) custom-call(s32[1]{0:T(128)} %bitcast.3.core, bf16[48,8192]{1,0:T(8,128)(2,1)S(1)} %pad_maximum_fusion.6.own, bf16[48,8192]{1,0:T(8,128)(2,1)S(1)} %copy-done.5, bf16[48,8192]{1,0:T(8,128)(2,1)S(1)} %copy-done.7, ...), custom_call_target="tpu_custom_call" | custom-call | flops 4026531840 | bytes 25165824 | tf_op jit(solution)/shard_map/project/pallas_call | solution.py:106
  170.3 12.0 %attend.5 = (bf16[48,8192]{1,0:T(8,128)(2,1)}, bf16[48,8192]{1,0:T(8,128)(2,1)}, bf16[48,8192]{1,0:T(8,128)(2,1)}, bf16[48,4096]{1,0:T(8,128)(2,1)S(1)}, bf16[48,4096]{1,0:T(8,128)(2,1)S(1)}) custom-call(s32[2]{0:T(128)S(1)} %pad_add_fusion.scalars, bf16[8,192,128]{2,1,0:T(8,128)(2,1)S(1)} %get-tuple-element.40.query, bf16[2,384,1024]{2,1,0:T(8,128)(2,1)} %bitcast.34, ...), custom_call_target="tpu_custom_call" | custom-call | flops 4429185024 | bytes 22020096 | tf_op jit(solution)/shard_map/attend/pallas_call | solution.py:211
  184.5 2.3 collective-permute-start.34
  186.8 11.9 %attend.4 = (bf16[48,8192]{1,0:T(8,128)(2,1)}, bf16[48,8192]{1,0:T(8,128)(2,1)}, bf16[48,8192]{1,0:T(8,128)(2,1)}, bf16[48,4096]{1,0:T(8,128)(2,1)S(1)}, bf16[48,4096]{1,0:T(8,128)(2,1)S(1)}) custom-call(s32[2]{0:T(128)S(1)} %pad_add_fusion.scalars, bf16[8,192,128]{2,1,0:T(8,128)(2,1)S(1)} %get-tuple-element.33.query, bf16[2,384,1024]{2,1,0:T(8,128)(2,1)} %bitcast.35, ...), custom_call_target="tpu_custom_call" | custom-call | flops 4127195136 | bytes 22020096 | tf_op jit(solution)/shard_map/attend/pallas_call | solution.py:211
  202.9 10.9 %attend.3 = (bf16[48,8192]{1,0:T(8,128)(2,1)}, bf16[48,8192]{1,0:T(8,128)(2,1)}, bf16[48,8192]{1,0:T(8,128)(2,1)}, bf16[48,4096]{1,0:T(8,128)(2,1)S(1)}, bf16[48,4096]{1,0:T(8,128)(2,1)S(1)}) custom-call(s32[2]{0:T(128)S(1)} %pad_add_fusion.scalars, bf16[8,192,128]{2,1,0:T(8,128)(2,1)S(1)} %get-tuple-element.26.query, bf16[2,384,1024]{2,1,0:T(8,128)(2,1)} %bitcast.36, ...), custom_call_target="tpu_custom_call" | custom-call | flops 3825205248 | bytes 22020096 | tf_op jit(solution)/shard_map/attend/pallas_call | solution.py:211
  213.8 2.5 collective-permute-start.12
  218.7 3.3 %collective-permute-start.37 = (bf16[48,8192]{1,0:T(8,128)(2,1)S(1)}, bf16[48,8192]{1,0:T(8,128)(2,1)S(1)}, u32[]{:S(2)}, u32[]{:S(2)}) collective-permute-start(bf16[48,8192]{1,0:T(8,128)(2,1)S(1)} %pad_maximum_fusion.8), channel_id=1, source_target_pairs={{0,6},{1,7},{2,0},{3,1},{4,2},{5,3},{6,4},{7,5},{8,14},{9,15},{10,... | collective-permute-start | bytes 2359304 | tf_op jit(solution)/shard_map/ppermute | solution.py:34
  222.4 3.3 %collective-permute-start.25 = (bf16[48,8192]{1,0:T(8,128)(2,1)S(1)}, bf16[48,8192]{1,0:T(8,128)(2,1)S(1)}, u32[]{:S(2)}, u32[]{:S(2)}) collective-permute-start(bf16[48,8192]{1,0:T(8,128)(2,1)S(1)} %pad_maximum_fusion.5), channel_id=1, source_target_pairs={{0,6},{1,7},{2,0},{3,1},{4,2},{5,3},{6,4},{7,5},{8,14},{9,15},{10,... | collective-permute-start | bytes 2359304 | tf_op jit(solution)/shard_map/ppermute | solution.py:34
  226.1 5.6 %collective-permute-done.10 = bf16[48,4096]{1,0:T(8,128)(2,1)S(1)} collective-permute-done((bf16[48,4096]{1,0:T(8,128)(2,1)S(1)}, bf16[48,4096]{1,0:T(8,128)(2,1)S(1)}, u32[]{:S(2)}, u32[]{:S(2)}) %collective-permute-start.10) | collective-permute-done | bytes 393248 | tf_op jit(solution)/shard_map/ppermute | solution.py:34
  231.9 10.9 %collective-permute-done.37 = bf16[48,8192]{1,0:T(8,128)(2,1)S(1)} collective-permute-done((bf16[48,8192]{1,0:T(8,128)(2,1)S(1)}, bf16[48,8192]{1,0:T(8,128)(2,1)S(1)}, u32[]{:S(2)}, u32[]{:S(2)}) %collective-permute-start.37) | collective-permute-done | bytes 786464 | tf_op jit(solution)/shard_map/ppermute | solution.py:34
  242.8 5.8 %collective-permute-done.35 = bf16[48,8192]{1,0:T(8,128)(2,1)S(1)} collective-permute-done((bf16[48,8192]{1,0:T(8,128)(2,1)S(1)}, bf16[48,8192]{1,0:T(8,128)(2,1)S(1)}, u32[]{:S(2)}, u32[]{:S(2)}) %collective-permute-start.35) | collective-permute-done | bytes 786464 | tf_op jit(solution)/shard_map/ppermute | solution.py:34
  248.9 1.6 collective-permute-start.38
  250.5 9.1 %collective-permute-done.25 = bf16[48,8192]{1,0:T(8,128)(2,1)S(1)} collective-permute-done((bf16[48,8192]{1,0:T(8,128)(2,1)S(1)}, bf16[48,8192]{1,0:T(8,128)(2,1)S(1)}, u32[]{:S(2)}, u32[]{:S(2)}) %collective-permute-start.25) | collective-permute-done | bytes 786464 | tf_op jit(solution)/shard_map/ppermute | solution.py:34
  259.6 5.8 %collective-permute-done.23 = bf16[48,8192]{1,0:T(8,128)(2,1)S(1)} collective-permute-done((bf16[48,8192]{1,0:T(8,128)(2,1)S(1)}, bf16[48,8192]{1,0:T(8,128)(2,1)S(1)}, u32[]{:S(2)}, u32[]{:S(2)}) %collective-permute-start.23) | collective-permute-done | bytes 786464 | tf_op jit(solution)/shard_map/ppermute | solution.py:34
  265.8 1.6 collective-permute-start.26
  267.4 7.3 %collective-permute-done.13 = bf16[48,8192]{1,0:T(8,128)(2,1)S(1)} collective-permute-done((bf16[48,8192]{1,0:T(8,128)(2,1)S(1)}, bf16[48,8192]{1,0:T(8,128)(2,1)S(1)}, u32[]{:S(2)}, u32[]{:S(2)}) %collective-permute-start.13) | collective-permute-done | bytes 786464 | tf_op jit(solution)/shard_map/ppermute | solution.py:34
  274.7 5.6 %collective-permute-done.11 = bf16[48,8192]{1,0:T(8,128)(2,1)S(1)} collective-permute-done((bf16[48,8192]{1,0:T(8,128)(2,1)S(1)}, bf16[48,8192]{1,0:T(8,128)(2,1)S(1)}, u32[]{:S(2)}, u32[]{:S(2)}) %collective-permute-start.11) | collective-permute-done | bytes 786464 | tf_op jit(solution)/shard_map/ppermute | solution.py:34
  280.6 1.6 collective-permute-start.14
  282.5 7.3 %collective-permute-done.14 = bf16[24,8192]{1,0:T(8,128)(2,1)S(1)} collective-permute-done((bf16[24,8192]{1,0:T(8,128)(2,1)S(1)}, bf16[24,8192]{1,0:T(8,128)(2,1)S(1)}, u32[]{:S(2)}, u32[]{:S(2)}) %collective-permute-start.14) | collective-permute-done | bytes 393248 | tf_op jit(solution)/shard_map/ppermute | solution.py:34
  (178 shorter events, 31.0 us)
Async XLA Ops:
  0.0 127.0 %collective-permute-start.6 = (bf16[8192,512]{1,0:T(8,128)(2,1)}, bf16[8192,512]{1,0:T(8,128)(2,1)}, u32[]{:S(2)}, u32[]{:S(2)}) collective-permute-start(bf16[8192,512]{1,0:T(8,128)(2,1)} %bitcast.30), channel_id=1, source_target_pairs={{0,1},{1,0},{2,3},{3,2},{4,5},{5,4},{6,7},{7,6},{8,9},{9,8},{10,11... | collective-permute-start | bytes 25165832 | tf_op jit(solution)/shard_map/ppermute | solution.py:34
  2.3 15.7 %collective-permute-start.15 = (bf16[24,8192]{1,0:T(8,128)(2,1)}, bf16[24,8192]{1,0:T(8,128)(2,1)S(1)}, u32[]{:S(2)}, u32[]{:S(2)}) collective-permute-start(bf16[24,8192]{1,0:T(8,128)(2,1)} %get-tuple-element.47), channel_id=1, source_target_pairs={{0,16},{16,32},{32,48},{48,64},{64,80},{80,96},{96,112},{112,0},{1... | collective-permute-start | bytes 1179656 | tf_op jit(solution)/shard_map/ppermute | solution.py:39
  3.9 22.6 %collective-permute-start.27 = (bf16[24,8192]{1,0:T(8,128)(2,1)}, bf16[24,8192]{1,0:T(8,128)(2,1)S(1)}, u32[]{:S(2)}, u32[]{:S(2)}) collective-permute-start(bf16[24,8192]{1,0:T(8,128)(2,1)} %get-tuple-element.49), channel_id=1, source_target_pairs={{0,16},{16,32},{32,48},{48,64},{64,80},{80,96},{96,112},{112,0},{1... | collective-permute-start | bytes 1179656 | tf_op jit(solution)/shard_map/ppermute | solution.py:39
  5.3 29.2 %collective-permute-start = (bf16[24,8192]{1,0:T(8,128)(2,1)}, bf16[24,8192]{1,0:T(8,128)(2,1)S(1)}, u32[]{:S(2)}, u32[]{:S(2)}) collective-permute-start(bf16[24,8192]{1,0:T(8,128)(2,1)} %get-tuple-element.48), channel_id=1, source_target_pairs={{0,16},{16,32},{32,48},{48,64},{64,80},{80,96},{96,112},{112,0},{1... | collective-permute-start | bytes 1179656 | tf_op jit(solution)/shard_map/ppermute | solution.py:39
  6.5 163.3 %collective-permute-start.9 = (bf16[512,8192]{1,0:T(8,128)(2,1)}, bf16[512,8192]{1,0:T(8,128)(2,1)}, u32[]{:S(2)}, u32[]{:S(2)}) collective-permute-start(bf16[512,8192]{1,0:T(8,128)(2,1)} %bitcast.26), channel_id=1, source_target_pairs={{0,1},{1,0},{2,3},{3,2},{4,5},{5,4},{6,7},{7,6},{8,9},{9,8},{10,11... | collective-permute-start | bytes 25165832 | tf_op jit(solution)/shard_map/ppermute | solution.py:34
  18.0 17.2 %copy-start.18 = (bf16[24,8192]{1,0:T(8,128)(2,1)}, bf16[24,8192]{1,0:T(8,128)(2,1)S(1)}, u32[]{:S(2)}) copy-start(bf16[24,8192]{1,0:T(8,128)(2,1)S(1)} %collective-permute-done.15) | copy-start | bytes 1179652
  18.2 18.6 %copy-start.35 = (s32[1,3]{1,0:T(1,128)S(1)}, s32[1,3]{1,0:T(1,128)}, u32[]{:S(2)}) copy-start(s32[1,3]{1,0:T(1,128)} %param.13) | copy-start | bytes 40
  35.2 12.1 %collective-permute-start.28 = (bf16[24,8192]{1,0:T(8,128)(2,1)S(1)}, bf16[24,8192]{1,0:T(8,128)(2,1)S(1)}, u32[]{:S(2)}, u32[]{:S(2)}) collective-permute-start(bf16[24,8192]{1,0:T(8,128)(2,1)S(1)} %get-tuple-element.51), channel_id=1, source_target_pairs={{0,8},{1,9},{2,10},{3,11},{4,12},{5,13},{6,14},{7,15},{8,0},{9,1},... | collective-permute-start | bytes 1179656 | tf_op jit(solution)/shard_map/ppermute | solution.py:34
  37.5 18.2 %collective-permute-start.1 = (bf16[24,8192]{1,0:T(8,128)(2,1)S(1)}, bf16[24,8192]{1,0:T(8,128)(2,1)S(1)}, u32[]{:S(2)}, u32[]{:S(2)}) collective-permute-start(bf16[24,8192]{1,0:T(8,128)(2,1)S(1)} %get-tuple-element.52), channel_id=1, source_target_pairs={{0,8},{1,9},{2,10},{3,11},{4,12},{5,13},{6,14},{7,15},{8,0},{9,1},... | collective-permute-start | bytes 1179656 | tf_op jit(solution)/shard_map/ppermute | solution.py:34
  38.0 25.0 %collective-permute-start.16 = (bf16[24,8192]{1,0:T(8,128)(2,1)S(1)}, bf16[24,8192]{1,0:T(8,128)(2,1)S(1)}, u32[]{:S(2)}, u32[]{:S(2)}) collective-permute-start(bf16[24,8192]{1,0:T(8,128)(2,1)S(1)} %get-tuple-element.50), channel_id=1, source_target_pairs={{0,8},{1,9},{2,10},{3,11},{4,12},{5,13},{6,14},{7,15},{8,0},{9,1},... | collective-permute-start | bytes 1179656 | tf_op jit(solution)/shard_map/ppermute | solution.py:34
  47.3 19.5 %collective-permute-start.29 = (bf16[48,8192]{1,0:T(8,128)(2,1)S(1)}, bf16[48,8192]{1,0:T(8,128)(2,1)S(1)}, u32[]{:S(2)}, u32[]{:S(2)}) collective-permute-start(bf16[48,8192]{1,0:T(8,128)(2,1)S(1)} %pad_maximum_fusion.6.own), channel_id=1, source_target_pairs={{0,2},{1,3},{2,4},{3,5},{4,6},{5,7},{6,0},{7,1},{8,10},{9,11},{10,... | collective-permute-start | bytes 2359304 | tf_op jit(solution)/shard_map/ppermute | solution.py:34
  55.7 18.6 %collective-permute-start.30 = (bf16[48,8192]{1,0:T(8,128)(2,1)S(1)}, bf16[48,8192]{1,0:T(8,128)(2,1)S(1)}, u32[]{:S(2)}, u32[]{:S(2)}) collective-permute-start(bf16[48,8192]{1,0:T(8,128)(2,1)S(1)} %pad_maximum_fusion.6.own), channel_id=1, source_target_pairs={{0,6},{1,7},{2,0},{3,1},{4,2},{5,3},{6,4},{7,5},{8,14},{9,15},{10,... | collective-permute-start | bytes 2359304 | tf_op jit(solution)/shard_map/ppermute | solution.py:34
  59.8 40.8 %copy-start = (bf16[48,8192]{1,0:T(8,128)(2,1)}, bf16[48,8192]{1,0:T(8,128)(2,1)S(1)}, u32[]{:S(2)}) copy-start(bf16[48,8192]{1,0:T(8,128)(2,1)S(1)} %pad_maximum_fusion.own) | copy-start | bytes 2359300
  63.0 63.9 %collective-permute-start.7 = (bf16[8192,128]{1,0:T(8,128)(2,1)S(1)}, bf16[8192,128]{1,0:T(8,128)(2,1)}, u32[]{:S(2)}, u32[]{:S(2)}) collective-permute-start(bf16[8192,128]{1,0:T(8,128)(2,1)S(1)} %copy.10.wkv_mine), channel_id=1, source_target_pairs={{0,1},{1,0},{2,3},{3,2},{4,5},{5,4},{6,7},{7,6},{8,9},{9,8},{10,11... | collective-permute-start | bytes 6291464 | tf_op jit(solution)/shard_map/ppermute | solution.py:34
  66.8 18.4 %collective-permute-start.2 = (bf16[48,8192]{1,0:T(8,128)(2,1)S(1)}, bf16[48,8192]{1,0:T(8,128)(2,1)S(1)}, u32[]{:S(2)}, u32[]{:S(2)}) collective-permute-start(bf16[48,8192]{1,0:T(8,128)(2,1)S(1)} %pad_maximum_fusion.own), channel_id=1, source_target_pairs={{0,2},{1,3},{2,4},{3,5},{4,6},{5,7},{6,0},{7,1},{8,10},{9,11},{10,... | collective-permute-start | bytes 2359304 | tf_op jit(solution)/shard_map/ppermute | solution.py:34
  74.4 26.3 %copy-start.6 = (bf16[48,8192]{1,0:T(8,128)(2,1)}, bf16[48,8192]{1,0:T(8,128)(2,1)S(1)}, u32[]{:S(2)}) copy-start(bf16[48,8192]{1,0:T(8,128)(2,1)S(1)} %collective-permute-done.30.right) | copy-start | bytes 2359300
  74.4 17.7 %collective-permute-start.3 = (bf16[48,8192]{1,0:T(8,128)(2,1)S(1)}, bf16[48,8192]{1,0:T(8,128)(2,1)S(1)}, u32[]{:S(2)}, u32[]{:S(2)}) collective-permute-start(bf16[48,8192]{1,0:T(8,128)(2,1)S(1)} %pad_maximum_fusion.own), channel_id=1, source_target_pairs={{0,6},{1,7},{2,0},{3,1},{4,2},{5,3},{6,4},{7,5},{8,14},{9,15},{10,... | collective-permute-start | bytes 2359304 | tf_op jit(solution)/shard_map/ppermute | solution.py:34
  78.1 23.3 %copy-start.2 = (bf16[48,8192]{1,0:T(8,128)(2,1)}, bf16[48,8192]{1,0:T(8,128)(2,1)S(1)}, u32[]{:S(2)}) copy-start(bf16[48,8192]{1,0:T(8,128)(2,1)S(1)} %pad_maximum_fusion.3.own) | copy-start | bytes 2359300
  85.2 28.1 %copy-start.10 = (bf16[48,8192]{1,0:T(8,128)(2,1)}, bf16[48,8192]{1,0:T(8,128)(2,1)S(1)}, u32[]{:S(2)}) copy-start(bf16[48,8192]{1,0:T(8,128)(2,1)S(1)} %collective-permute-done.2.left) | copy-start | bytes 2359300
  85.2 17.5 %collective-permute-start.17 = (bf16[48,8192]{1,0:T(8,128)(2,1)S(1)}, bf16[48,8192]{1,0:T(8,128)(2,1)S(1)}, u32[]{:S(2)}, u32[]{:S(2)}) collective-permute-start(bf16[48,8192]{1,0:T(8,128)(2,1)S(1)} %pad_maximum_fusion.3.own), channel_id=1, source_target_pairs={{0,2},{1,3},{2,4},{3,5},{4,6},{5,7},{6,0},{7,1},{8,10},{9,11},{10,... | collective-permute-start | bytes 2359304 | tf_op jit(solution)/shard_map/ppermute | solution.py:34
  92.1 21.2 %copy-start.15 = (bf16[48,8192]{1,0:T(8,128)(2,1)}, bf16[48,8192]{1,0:T(8,128)(2,1)S(1)}, u32[]{:S(2)}) copy-start(bf16[48,8192]{1,0:T(8,128)(2,1)S(1)} %collective-permute-done.3.right) | copy-start | bytes 2359300
  92.1 17.5 %collective-permute-start.18 = (bf16[48,8192]{1,0:T(8,128)(2,1)S(1)}, bf16[48,8192]{1,0:T(8,128)(2,1)S(1)}, u32[]{:S(2)}, u32[]{:S(2)}) collective-permute-start(bf16[48,8192]{1,0:T(8,128)(2,1)S(1)} %pad_maximum_fusion.3.own), channel_id=1, source_target_pairs={{0,6},{1,7},{2,0},{3,1},{4,2},{5,3},{6,4},{7,5},{8,14},{9,15},{10,... | collective-permute-start | bytes 2359304 | tf_op jit(solution)/shard_map/ppermute | solution.py:34
  102.7 16.9 %collective-permute-start.4 = (bf16[48,4096]{1,0:T(8,128)(2,1)}, bf16[48,4096]{1,0:T(8,128)(2,1)}, u32[]{:S(2)}, u32[]{:S(2)}) collective-permute-start(bf16[48,4096]{1,0:T(8,128)(2,1)} %slice.124), channel_id=1, source_target_pairs={{0,2},{1,3},{2,4},{3,5},{4,6},{5,7},{6,0},{7,1},{8,10},{9,11},{10,... | collective-permute-start | bytes 1179656 | tf_op jit(solution)/shard_map/ppermute | solution.py:34
  109.6 11.3 %collective-permute-start.5 = (bf16[48,4096]{1,0:T(8,128)(2,1)}, bf16[48,4096]{1,0:T(8,128)(2,1)}, u32[]{:S(2)}, u32[]{:S(2)}) collective-permute-start(bf16[48,4096]{1,0:T(8,128)(2,1)} %slice.125), channel_id=1, source_target_pairs={{0,6},{1,7},{2,0},{3,1},{4,2},{5,3},{6,4},{7,5},{8,14},{9,15},{10,... | collective-permute-start | bytes 1179656 | tf_op jit(solution)/shard_map/ppermute | solution.py:34
  119.6 24.8 %collective-permute-start.19 = (bf16[48,4096]{1,0:T(8,128)(2,1)}, bf16[48,4096]{1,0:T(8,128)(2,1)}, u32[]{:S(2)}, u32[]{:S(2)}) collective-permute-start(bf16[48,4096]{1,0:T(8,128)(2,1)} %slice.128), channel_id=1, source_target_pairs={{0,2},{1,3},{2,4},{3,5},{4,6},{5,7},{6,0},{7,1},{8,10},{9,11},{10,... | collective-permute-start | bytes 1179656 | tf_op jit(solution)/shard_map/ppermute | solution.py:34
  120.8 23.8 %collective-permute-start.20 = (bf16[48,4096]{1,0:T(8,128)(2,1)}, bf16[48,4096]{1,0:T(8,128)(2,1)}, u32[]{:S(2)}, u32[]{:S(2)}) collective-permute-start(bf16[48,4096]{1,0:T(8,128)(2,1)} %slice.129), channel_id=1, source_target_pairs={{0,6},{1,7},{2,0},{3,1},{4,2},{5,3},{6,4},{7,5},{8,14},{9,15},{10,... | collective-permute-start | bytes 1179656 | tf_op jit(solution)/shard_map/ppermute | solution.py:34
  127.0 30.2 %collective-permute-start.31 = (bf16[48,4096]{1,0:T(8,128)(2,1)S(1)}, bf16[48,4096]{1,0:T(8,128)(2,1)S(1)}, u32[]{:S(2)}, u32[]{:S(2)}) collective-permute-start(bf16[48,4096]{1,0:T(8,128)(2,1)S(1)} %slice.132), channel_id=1, source_target_pairs={{0,2},{1,3},{2,4},{3,5},{4,6},{5,7},{6,0},{7,1},{8,10},{9,11},{10,... | collective-permute-start | bytes 1179656 | tf_op jit(solution)/shard_map/ppermute | solution.py:34
  127.0 30.1 %collective-permute-start.32 = (bf16[48,4096]{1,0:T(8,128)(2,1)S(1)}, bf16[48,4096]{1,0:T(8,128)(2,1)S(1)}, u32[]{:S(2)}, u32[]{:S(2)}) collective-permute-start(bf16[48,4096]{1,0:T(8,128)(2,1)S(1)} %slice.133), channel_id=1, source_target_pairs={{0,6},{1,7},{2,0},{3,1},{4,2},{5,3},{6,4},{7,5},{8,14},{9,15},{10,... | collective-permute-start | bytes 1179656 | tf_op jit(solution)/shard_map/ppermute | solution.py:34
  144.4 25.5 %collective-permute-start.8 = (bf16[2,192,128]{2,1,0:T(8,128)(2,1)S(1)}, bf16[2,192,128]{2,1,0:T(8,128)(2,1)S(1)}, u32[]{:S(2)}, u32[]{:S(2)}) collective-permute-start(bf16[2,192,128]{2,1,0:T(8,128)(2,1)S(1)} %get-tuple-element.27.refs_0_), channel_id=1, source_target_pairs={{0,1},{1,0},{2,3},{3,2},{4,5},{5,4},{6,7},{7,6},{8,9},{9,8},{10,11... | collective-permute-start | bytes 294920 | tf_op jit(solution)/shard_map/ppermute | solution.py:34
  156.6 13.2 %collective-permute-start.21 = (bf16[2,192,128]{2,1,0:T(8,128)(2,1)S(1)}, bf16[2,192,128]{2,1,0:T(8,128)(2,1)S(1)}, u32[]{:S(2)}, u32[]{:S(2)}) collective-permute-start(bf16[2,192,128]{2,1,0:T(8,128)(2,1)S(1)} %get-tuple-element.34.refs_2_), channel_id=1, source_target_pairs={{0,1},{1,0},{2,3},{3,2},{4,5},{5,4},{6,7},{7,6},{8,9},{9,8},{10,11... | collective-permute-start | bytes 294920 | tf_op jit(solution)/shard_map/ppermute | solution.py:34
  168.9 1.4 collective-permute-start.33
  182.3 36.1 %collective-permute-start.36 = (bf16[48,4096]{1,0:T(8,128)(2,1)S(1)}, bf16[48,4096]{1,0:T(8,128)(2,1)S(1)}, u32[]{:S(2)}, u32[]{:S(2)}) collective-permute-start(bf16[48,4096]{1,0:T(8,128)(2,1)S(1)} %get-tuple-element.46), channel_id=1, source_target_pairs={{0,6},{1,7},{2,0},{3,1},{4,2},{5,3},{6,4},{7,5},{8,14},{9,15},{10,... | collective-permute-start | bytes 1179656 | tf_op jit(solution)/shard_map/ppermute | solution.py:34
  184.5 34.2 %collective-permute-start.34 = (bf16[48,4096]{1,0:T(8,128)(2,1)S(1)}, bf16[48,4096]{1,0:T(8,128)(2,1)S(1)}, u32[]{:S(2)}, u32[]{:S(2)}) collective-permute-start(bf16[48,4096]{1,0:T(8,128)(2,1)S(1)} %get-tuple-element.44), channel_id=1, source_target_pairs={{0,2},{1,3},{2,4},{3,5},{4,6},{5,7},{6,0},{7,1},{8,10},{9,11},{10,... | collective-permute-start | bytes 1179656 | tf_op jit(solution)/shard_map/ppermute | solution.py:34
  198.7 23.4 %collective-permute-start.24 = (bf16[48,4096]{1,0:T(8,128)(2,1)S(1)}, bf16[48,4096]{1,0:T(8,128)(2,1)S(1)}, u32[]{:S(2)}, u32[]{:S(2)}) collective-permute-start(bf16[48,4096]{1,0:T(8,128)(2,1)S(1)} %get-tuple-element.39), channel_id=1, source_target_pairs={{0,6},{1,7},{2,0},{3,1},{4,2},{5,3},{6,4},{7,5},{8,14},{9,15},{10,... | collective-permute-start | bytes 1179656 | tf_op jit(solution)/shard_map/ppermute | solution.py:34
  202.1 20.3 %collective-permute-start.22 = (bf16[48,4096]{1,0:T(8,128)(2,1)S(1)}, bf16[48,4096]{1,0:T(8,128)(2,1)S(1)}, u32[]{:S(2)}, u32[]{:S(2)}) collective-permute-start(bf16[48,4096]{1,0:T(8,128)(2,1)S(1)} %get-tuple-element.37), channel_id=1, source_target_pairs={{0,2},{1,3},{2,4},{3,5},{4,6},{5,7},{6,0},{7,1},{8,10},{9,11},{10,... | collective-permute-start | bytes 1179656 | tf_op jit(solution)/shard_map/ppermute | solution.py:34
  213.8 12.1 %collective-permute-start.12 = (bf16[48,4096]{1,0:T(8,128)(2,1)S(1)}, bf16[48,4096]{1,0:T(8,128)(2,1)S(1)}, u32[]{:S(2)}, u32[]{:S(2)}) collective-permute-start(bf16[48,4096]{1,0:T(8,128)(2,1)S(1)} %get-tuple-element.32), channel_id=1, source_target_pairs={{0,6},{1,7},{2,0},{3,1},{4,2},{5,3},{6,4},{7,5},{8,14},{9,15},{10,... | collective-permute-start | bytes 1179656 | tf_op jit(solution)/shard_map/ppermute | solution.py:34
  218.4 13.3 %collective-permute-start.10 = (bf16[48,4096]{1,0:T(8,128)(2,1)S(1)}, bf16[48,4096]{1,0:T(8,128)(2,1)S(1)}, u32[]{:S(2)}, u32[]{:S(2)}) collective-permute-start(bf16[48,4096]{1,0:T(8,128)(2,1)S(1)} %get-tuple-element.30), channel_id=1, source_target_pairs={{0,2},{1,3},{2,4},{3,5},{4,6},{5,7},{6,0},{7,1},{8,10},{9,11},{10,... | collective-permute-start | bytes 1179656 | tf_op jit(solution)/shard_map/ppermute | solution.py:34
  218.7 24.1 %collective-permute-start.37 = (bf16[48,8192]{1,0:T(8,128)(2,1)S(1)}, bf16[48,8192]{1,0:T(8,128)(2,1)S(1)}, u32[]{:S(2)}, u32[]{:S(2)}) collective-permute-start(bf16[48,8192]{1,0:T(8,128)(2,1)S(1)} %pad_maximum_fusion.8), channel_id=1, source_target_pairs={{0,6},{1,7},{2,0},{3,1},{4,2},{5,3},{6,4},{7,5},{8,14},{9,15},{10,... | collective-permute-start | bytes 2359304 | tf_op jit(solution)/shard_map/ppermute | solution.py:34
  222.1 26.4 %collective-permute-start.35 = (bf16[48,8192]{1,0:T(8,128)(2,1)S(1)}, bf16[48,8192]{1,0:T(8,128)(2,1)S(1)}, u32[]{:S(2)}, u32[]{:S(2)}) collective-permute-start(bf16[48,8192]{1,0:T(8,128)(2,1)S(1)} %pad_maximum_fusion.7), channel_id=1, source_target_pairs={{0,2},{1,3},{2,4},{3,5},{4,6},{5,7},{6,0},{7,1},{8,10},{9,11},{10,... | collective-permute-start | bytes 2359304 | tf_op jit(solution)/shard_map/ppermute | solution.py:34
  222.4 37.2 %collective-permute-start.25 = (bf16[48,8192]{1,0:T(8,128)(2,1)S(1)}, bf16[48,8192]{1,0:T(8,128)(2,1)S(1)}, u32[]{:S(2)}, u32[]{:S(2)}) collective-permute-start(bf16[48,8192]{1,0:T(8,128)(2,1)S(1)} %pad_maximum_fusion.5), channel_id=1, source_target_pairs={{0,6},{1,7},{2,0},{3,1},{4,2},{5,3},{6,4},{7,5},{8,14},{9,15},{10,... | collective-permute-start | bytes 2359304 | tf_op jit(solution)/shard_map/ppermute | solution.py:34
  225.9 39.5 %collective-permute-start.23 = (bf16[48,8192]{1,0:T(8,128)(2,1)S(1)}, bf16[48,8192]{1,0:T(8,128)(2,1)S(1)}, u32[]{:S(2)}, u32[]{:S(2)}) collective-permute-start(bf16[48,8192]{1,0:T(8,128)(2,1)S(1)} %pad_maximum_fusion.4), channel_id=1, source_target_pairs={{0,2},{1,3},{2,4},{3,5},{4,6},{5,7},{6,0},{7,1},{8,10},{9,11},{10,... | collective-permute-start | bytes 2359304 | tf_op jit(solution)/shard_map/ppermute | solution.py:34
  226.1 22.5 %copy-start.30 = (bf16[48,8192]{1,0:T(8,128)(2,1)S(1)}, bf16[48,8192]{1,0:T(8,128)(2,1)}, u32[]{:S(2)}) copy-start(bf16[48,8192]{1,0:T(8,128)(2,1)} %get-tuple-element.42) | copy-start | bytes 2359300
  231.7 43.0 %collective-permute-start.13 = (bf16[48,8192]{1,0:T(8,128)(2,1)S(1)}, bf16[48,8192]{1,0:T(8,128)(2,1)S(1)}, u32[]{:S(2)}, u32[]{:S(2)}) collective-permute-start(bf16[48,8192]{1,0:T(8,128)(2,1)S(1)} %pad_maximum_fusion.2), channel_id=1, source_target_pairs={{0,6},{1,7},{2,0},{3,1},{4,2},{5,3},{6,4},{7,5},{8,14},{9,15},{10,... | collective-permute-start | bytes 2359304 | tf_op jit(solution)/shard_map/ppermute | solution.py:34
  242.8 37.5 %collective-permute-start.11 = (bf16[48,8192]{1,0:T(8,128)(2,1)S(1)}, bf16[48,8192]{1,0:T(8,128)(2,1)S(1)}, u32[]{:S(2)}, u32[]{:S(2)}) collective-permute-start(bf16[48,8192]{1,0:T(8,128)(2,1)S(1)} %pad_maximum_fusion.1), channel_id=1, source_target_pairs={{0,2},{1,3},{2,4},{3,5},{4,6},{5,7},{6,0},{7,1},{8,10},{9,11},{10,... | collective-permute-start | bytes 2359304 | tf_op jit(solution)/shard_map/ppermute | solution.py:34
  248.6 16.9 %copy-start.31 = (bf16[48,8192]{1,0:T(8,128)(2,1)S(1)}, bf16[48,8192]{1,0:T(8,128)(2,1)}, u32[]{:S(2)}) copy-start(bf16[48,8192]{1,0:T(8,128)(2,1)} %get-tuple-element.35) | copy-start | bytes 2359300
  248.9 33.3 %collective-permute-start.38 = (bf16[24,8192]{1,0:T(8,128)(2,1)S(1)}, bf16[24,8192]{1,0:T(8,128)(2,1)S(1)}, u32[]{:S(2)}, u32[]{:S(2)}) collective-permute-start(bf16[24,8192]{1,0:T(8,128)(2,1)S(1)} %slice.157), channel_id=1, source_target_pairs={{0,8},{1,9},{2,10},{3,11},{4,12},{5,13},{6,14},{7,15},{8,0},{9,1},... | collective-permute-start | bytes 1179656 | tf_op jit(solution)/shard_map/ppermute | solution.py:34
  265.8 16.6 %collective-permute-start.26 = (bf16[24,8192]{1,0:T(8,128)(2,1)S(1)}, bf16[24,8192]{1,0:T(8,128)(2,1)S(1)}, u32[]{:S(2)}, u32[]{:S(2)}) collective-permute-start(bf16[24,8192]{1,0:T(8,128)(2,1)S(1)} %slice.158), channel_id=1, source_target_pairs={{0,8},{1,9},{2,10},{3,11},{4,12},{5,13},{6,14},{7,15},{8,0},{9,1},... | collective-permute-start | bytes 1179656 | tf_op jit(solution)/shard_map/ppermute | solution.py:34
  280.6 9.2 %collective-permute-start.14 = (bf16[24,8192]{1,0:T(8,128)(2,1)S(1)}, bf16[24,8192]{1,0:T(8,128)(2,1)S(1)}, u32[]{:S(2)}, u32[]{:S(2)}) collective-permute-start(bf16[24,8192]{1,0:T(8,128)(2,1)S(1)} %slice.159), channel_id=1, source_target_pairs={{0,8},{1,9},{2,10},{3,11},{4,12},{5,13},{6,14},{7,15},{8,0},{9,1},... | collective-permute-start | bytes 1179656 | tf_op jit(solution)/shard_map/ppermute | solution.py:34
  (27 other events, 188.6 us)

commit v2 on v1

v2 whole, which is shorter than its diff:
```python
import functools
import math

import jax
import jax.numpy as jnp
from jax import lax
from jax.experimental import pallas as pl
from jax.experimental.pallas import tpu as pltpu
from jax.sharding import PartitionSpec as P

HD = 128
BLOCK = 384
CACHE = 384
D = 8192
NZ = 4
SHARD = 24
ROWS = 192
K_CHUNK = 2048
N_CHUNK = 2048
PROJECT_COST = (12,12,12)
ATTEND_COST = (0,12,12)
Y, A, B = (1, 0), (0, 1), (0, 3)

HALF = D // 2
PIECE = 2 * SHARD

ORDER_IN = (Y, A, B)
SCATTER = (
    ((0, 8192, (A, B, Y)),),
    ((0, 4096, (B, Y, A)), (4096, 4096, (A, B, Y)),),
    ((0, 4096, (Y, A, B)), (4096, 4096, (A, B, Y)),),
)


def steps_to(order, block):
    y = z = 0
    for bit in range(3):
        if block >> bit & 1:
            y ^= order[bit][0]
            z ^= order[bit][1]
    return y, z


def reorder(source, target):
    known = [steps_to(source, block) for block in range(8)]
    return [known.index(steps_to(target, block)) for block in range(8)]


def tensor_index(y, z, c):
    return (y * NZ + z) * 2 + c


def move(value, step=(0, 0), dc=0):
    pairs = []
    for y in range(2):
        for z in range(NZ):
            for c in range(2):
                pairs.append((tensor_index(y, z, c), tensor_index(y ^ step[0], z ^ step[1], c ^ dc)))
    return lax.ppermute(value, "tensor", pairs)


def from_behind(value, dy=0):
    sections = lax.axis_size("section")
    tensors = 4 * NZ
    pairs = []
    for s in range(sections):
        for t in range(tensors):
            target = (s + 1) % sections * tensors + (t ^ dy * 2 * NZ)
            pairs.append((s * tensors + t, target))
    return lax.ppermute(value, ("section", "tensor"), pairs)


ANY = pl.BlockSpec(memory_space=pl.ANY)


def params(mib):
    return pltpu.CompilerParams(vmem_limit_bytes=mib * 2**20)


def cost(giga=0):
    return pl.CostEstimate(flops=giga * 10**9, bytes_accessed=0, transcendentals=0)


def bf16(*shape):
    return jax.ShapeDtypeStruct(shape, jnp.bfloat16)


def f32(*shape):
    return jax.ShapeDtypeStruct(shape, jnp.float32)


def wide(ref):
    return ref[...].astype(jnp.float32)


def full_spec(shape):
    return pl.BlockSpec(shape, lambda i, n=len(shape): (0,) * n)


def small(kernel, ins, outs, after, name, mib=16):
    picked = [isinstance(a, tuple) for a in ins]
    specs = [
        pl.BlockSpec((None, SHARD, D), lambda i, which=a[1]: (which, 0, 0))
        if is_picked
        else full_spec(a.shape)
        for a, is_picked in zip(ins, picked)
    ]
    ins = [a[0] if is_picked else a for a, is_picked in zip(ins, picked)]

    def body(*refs):
        kernel(refs[: len(ins)], refs[len(ins) + len(after) : -1])
        refs[-1][...] = jnp.zeros((8, 128), jnp.float32)

    outs = list(outs) + [f32(8, 128)]
    *results, token = pl.pallas_call(
        body,
        grid=(1,),
        in_specs=specs + [ANY] * len(after),
        out_specs=[full_spec(o.shape) for o in outs],
        out_shape=outs,
        compiler_params=params(mib),
        cost_estimate=cost(),
        name=name,
    )(*ins, *after)
    return results, (token,)


def norm(mine, other, gain, after):
    def kernel(ins, outs):
        rows = jnp.concatenate([wide(ins[0]), wide(ins[1])], axis=0)
        mean = jnp.mean(rows * rows, axis=1, keepdims=True)
        outs[0][...] = (rows * lax.rsqrt(mean + 1e-05) * wide(ins[2])).astype(jnp.bfloat16)

    return small(kernel, (mine, other, gain), [bf16(PIECE, D)], after, "norm")


def parts(over_a, over_b, after):
    def kernel(ins, outs):
        outs[0][...] = ins[0][:, :HALF]
        outs[1][...] = ins[1][:, HALF:]

    return small(kernel, (over_a, over_b), [bf16(PIECE, HALF)] * 2, after, "parts")


def halve(kept, received, after, base=None, lanes=()):
    def kernel(ins, outs):
        for lane in range(len(kept)):
            rows = wide(ins[2 * lane]) + wide(ins[2 * lane + 1])
            half = rows.shape[0] // 2
            keep = rows[:half]
            if base is not None:
                start, width, _ = lanes[lane]
                keep = keep + ins[-1][:, start : start + width].astype(jnp.float32)
            outs[2 * lane][...] = keep
            outs[2 * lane + 1][...] = rows[half:].astype(jnp.bfloat16)

    ins = [a for pair in zip(kept, received) for a in pair]
    if base is not None:
        ins.append(base)
    outs = []
    for a in kept:
        half = (a.shape[0] // 2, a.shape[1])
        outs += [f32(*half), bf16(*half)]
    results, token = small(kernel, ins, outs, after, "halve")
    return results[0::2], results[1::2], token


def project_kernel(
    own, over_a, over_b, far_a, far_b, wq_mine, wq_other, wkv_mine, wkv_other, cosine, sine, flag, *refs
):
    query, kv, acc_q, acc_kv = refs[-4:]
    step = pl.program_id(0)
    steps = pl.num_programs(0)
    far = jnp.where(step < steps // 2, far_a[...], far_b[...])
    x = jnp.concatenate([own[...], over_a[...], over_b[...], far], axis=0)

    @pl.when(step == 0)
    def _():
        acc_q[...] = jnp.zeros_like(acc_q)
        acc_kv[...] = jnp.zeros_like(acc_kv)

    for half, (wq, wkv) in enumerate(((wq_mine, wkv_mine), (wq_other, wkv_other))):
        acc_q[:, half * 512 : half * 512 + 512] += jnp.dot(
            x, wq[...], preferred_element_type=jnp.float32
        )
        acc_kv[:, half * HD : half * HD + HD] += jnp.dot(
            x, wkv[...], preferred_element_type=jnp.float32
        )

    @pl.when(step == steps - 1)
    def _():
        cos = cosine[...]
        sin = sine[...]

        def turn(u):
            return u * cos + pltpu.roll(u, HD // 2, 1) * sin

        for head in range(8):
            query[head] = turn(acc_q[:, head * HD : head * HD + HD]).astype(jnp.bfloat16)
        first = flag[...] == 0
        mine = acc_kv[:, :HD]
        other = acc_kv[:, HD:]
        low = jnp.where(first, mine, other)
        high = jnp.where(first, other, mine)
        lower = lax.broadcasted_iota(jnp.int32, (ROWS, HD), 1) < HD // 2
        keys = jnp.where(lower, low, pltpu.roll(high, HD // 2, 1))
        values = jnp.where(lower, pltpu.roll(low, HD // 2, 1), high)
        keys = keys.astype(jnp.bfloat16).astype(jnp.float32)
        kv[0] = turn(keys).astype(jnp.bfloat16)
        kv[1] = values.astype(jnp.bfloat16)


def lane_spec(start, width, chunk):
    first = start // chunk
    count = width // chunk
    return pl.BlockSpec(
        (ROWS // 2, chunk), lambda k, *_: (0, jnp.clip(k - first, 0, count - 1))
    )


def project(which, pieces, weights, cosine, sine, flag, after):
    steps = D // K_CHUNK
    near = pl.BlockSpec((PIECE, K_CHUNK), lambda k: (0, k))
    specs = [near, near, near]
    specs.append(pl.BlockSpec((PIECE, K_CHUNK), lambda k: (0, jnp.minimum(k, steps // 2 - 1))))
    specs.append(pl.BlockSpec((PIECE, K_CHUNK), lambda k: (0, jnp.maximum(k - steps // 2, 0))))
    for w in weights:
        specs.append(pl.BlockSpec((K_CHUNK, w.shape[1]), lambda k: (k, 0)))
    table = pl.BlockSpec((None, ROWS, HD), lambda k: (which, 0, 0))
    specs += [table, table, full_spec(flag.shape)] + [ANY] * len(after)
    return pl.pallas_call(
        project_kernel,
        out_shape=(bf16(8, ROWS, HD), bf16(2, ROWS, HD)),
        grid=(steps,),
        in_specs=specs,
        out_specs=(
            pl.BlockSpec((8, ROWS, HD), lambda k: (0, 0, 0)),
            pl.BlockSpec((2, ROWS, HD), lambda k: (0, 0, 0)),
        ),
        scratch_shapes=[
            pltpu.VMEM((ROWS, 1024), jnp.float32),
            pltpu.VMEM((ROWS, 2 * HD), jnp.float32),
        ],
        compiler_params=params(44),
        cost_estimate=cost(PROJECT_COST[which]),
        name="project",
    )(*pieces, *weights, cosine, sine, flag, *after)


def attend_kernel(blocks, order, lanes, scalars, query, cache, q_place, k_place, *refs):
    windows = refs[:blocks]
    weights = refs[blocks : blocks + 2]
    count = 2 * len(lanes)
    outs = refs[-5 - count : -5]
    token, raw, attended, wo, sems = refs[-5:]
    step = pl.program_id(0)

    def fetch(n, half):
        return pltpu.make_async_copy(
            weights[half].at[:, pl.ds(pl.multiple_of(n * N_CHUNK, N_CHUNK), N_CHUNK)],
            wo.at[n, pl.ds(half * 512, 512), :],
            sems.at[n, half],
        )

    @pl.when(step == 0)
    def _():
        for n in range(D // N_CHUNK):
            fetch(n, 0).start()
            fetch(n, 1).start()
        token[...] = jnp.zeros((8, 128), jnp.float32)
        scale = math.log2(math.e) / math.sqrt(HD)
        slot = lax.broadcasted_iota(jnp.int32, (1, CACHE), 1)
        cache_bias = jnp.where(slot < scalars[1], 0.0, -1e30)
        causal_bias = jnp.where(k_place[...] <= q_place[...], 0.0, -1e30)
        keys = jnp.concatenate([cache[0]] + [w[c, 0] for w in windows for c in range(2)], axis=0)
        values = jnp.concatenate([cache[1]] + [w[c, 1] for w in windows for c in range(2)], axis=0)
        before = CACHE + (blocks - 1) * BLOCK
        for head in range(8):
            scores = lax.dot_general(
                query[head], keys, (((1,), (1,)), ((), ())), preferred_element_type=jnp.float32
            )
            parts = [scores[:, :CACHE] + cache_bias]
            if blocks > 1:
                parts.append(scores[:, CACHE:before])
            parts.append(scores[:, before:] + causal_bias)
            scores = jnp.concatenate(parts, axis=1)
            top = jnp.max(scores, axis=1, keepdims=True)
            grown = jnp.exp2((scores - top) * scale)
            total = jnp.sum(grown, axis=1, keepdims=True)
            out = jnp.dot(grown.astype(jnp.bfloat16), values, preferred_element_type=jnp.float32)
            raw[:, head * HD : head * HD + HD] = out / total
        for lane, (_, _, target) in enumerate(lanes):
            places = reorder(order, target)
            rows = [raw[p * SHARD : p * SHARD + SHARD] for p in places]
            attended[lane] = jnp.concatenate(rows, axis=0).astype(jnp.bfloat16)

    fetch(step, 0).wait()
    fetch(step, 1).wait()
    for lane, (start, width, _) in enumerate(lanes):
        first, last = start // N_CHUNK, (start + width) // N_CHUNK - 1

        @pl.when(jnp.logical_and(step >= first, step <= last))
        def _(lane=lane):
            term = jnp.dot(attended[lane], wo[step], preferred_element_type=jnp.float32)
            term = term.astype(jnp.bfloat16)
            outs[2 * lane][...] = term[: ROWS // 2]
            outs[2 * lane + 1][...] = term[ROWS // 2 :]


def attend(order, lanes, scalars, query, cache, q_place, k_place, windows, wo, after):
    steps = D // N_CHUNK
    blocks = len(windows)
    whole = lambda a: pl.BlockSpec(a.shape, lambda n, s: (0,) * a.ndim)
    specs = [
        whole(query),
        pl.BlockSpec((2, CACHE, HD), lambda n, s: (0, 0, s[0])),
        whole(q_place),
        whole(k_place),
        *[whole(w) for w in windows],
        ANY,
        ANY,
        *[ANY] * len(after),
    ]
    out_shape = []
    out_specs = []
    for start, width, _ in lanes:
        out_shape += [bf16(ROWS // 2, width)] * 2
        out_specs += [lane_spec(start, width, N_CHUNK)] * 2
    *results, token = pl.pallas_call(
        functools.partial(attend_kernel, blocks, order, lanes),
        out_shape=(*out_shape, f32(8, 128)),
        grid_spec=pltpu.PrefetchScalarGridSpec(
            num_scalar_prefetch=1,
            grid=(steps,),
            in_specs=specs,
            out_specs=(*out_specs, pl.BlockSpec((8, 128), lambda n, s: (0, 0))),
            scratch_shapes=[
                pltpu.VMEM((ROWS, 1024), jnp.float32),
                pltpu.VMEM((len(lanes), ROWS, 1024), jnp.bfloat16),
                pltpu.VMEM((steps, 1024, N_CHUNK), jnp.bfloat16),
                pltpu.SemaphoreType.DMA((steps, 2)),
            ],
        ),
        compiler_params=params(48),
        cost_estimate=cost(ATTEND_COST[blocks - 1]),
        name="attend",
    )(scalars, query, cache, q_place, k_place, *windows, *wo, *after)
    return results[0::2], results[1::2], (token,)


def shards(incoming, norm_gain, w_query, w_key_value, w_out, kv_cache, offsets):
    index = lax.axis_index("tensor")
    core = index % 2
    z = index // 2 % NZ
    y = index // (2 * NZ)
    head = index // 2
    offset = offsets[0, 0]
    handed = []
    beside = []
    for b in range(3):
        handed.append((from_behind(incoming[0, b : b + 1]), 0))
        beside.append((from_behind(incoming[0, b : b + 1], 1), 0))
    pairs = [[i, i + 1] for i in range(0, 4 * NZ, 2)]
    share = lambda a: lax.all_gather(a, "tensor", axis_index_groups=pairs)
    wkv = w_key_value[0].reshape(D, 2 * w_key_value.shape[3])
    wq_other = move(w_query[0], dc=1)
    wkv_other = move(wkv, dc=1)
    wo_other = move(w_out[0], dc=1)
    weights = (w_query[0], wq_other, wkv, wkv_other)
    arrived = (wq_other[:8, :128], wkv_other[:8, :128])
    flag = jnp.full((1, HD), core, jnp.int32)

    within = jnp.arange(SHARD, dtype=jnp.int32)
    freq = 500000.0 ** (-jnp.arange(HD // 2, dtype=jnp.float32) * 2.0 / HD)
    def places(c):
        moves = [steps_to(ORDER_IN, block) for block in range(8)]
        return jnp.concatenate(
            [tensor_index(y ^ dy, z ^ dz, c) * SHARD + within for dy, dz in moves]
        )

    mine = places(core)
    q_place = mine[:, None]
    k_place = jnp.concatenate([places(0), places(1)])[None, :]
    position = (offsets[0][:, None] + mine[None, :]).astype(jnp.float32)
    angle = position[:, :, None] * freq
    cos = jnp.cos(angle)
    sin = jnp.sin(angle)
    cosines = jnp.concatenate([cos, cos], axis=2)
    sines = jnp.concatenate([-sin, sin], axis=2)
    scalars = jnp.stack([head, offset])
    cache = kv_cache[0]

    held = [None] * 3
    sent = [None] * 3
    queries = [None] * 3
    windows = []
    results = [None] * 3

    def send(b, lanes, values, bit):
        sent[b] = [move(a, lane[2][bit]) for a, lane in zip(values, lanes)]

    own = [None] * 3
    near = [None] * 3
    far = [None] * 3

    def start_block(b, after):
        (own[b],), token = norm(handed[b], beside[b], norm_gain, after)
        near[b] = (move(own[b], A), move(own[b], B))
        return token

    def grow(b, after):
        (over_a, over_b), token = parts(*near[b], after)
        far[b] = (move(over_a, B), move(over_b, A))
        return token

    def project_block(b, after):
        pieces = (own[b], *near[b], *far[b])
        queries[b], kv = project(b, pieces, weights, cosines, sines, flag, after)
        windows.append(share(kv))
        return (kv,)

    def attend_block(b, after):
        held[b], given, token = attend(
            ORDER_IN,
            SCATTER[b],
            scalars,
            queries[b],
            cache,
            q_place,
            k_place,
            tuple(windows[: b + 1]),
            (w_out[0], wo_other),
            after,
        )
        send(b, SCATTER[b], given, 2)
        return token

    def shrink(b, bit, after):
        base = handed[b] if bit == 0 else None
        held[b], given, token = halve(held[b], sent[b], after, base, SCATTER[b])
        send(b, SCATTER[b], given, bit)
        if bit == 0:
            results[b] = jnp.concatenate(
                [
                    (a + r.astype(jnp.float32)).astype(jnp.bfloat16)
                    for a, r in zip(held[b], sent[b])
                ],
                axis=1,
            )
        return token

    t = start_block(0, (cosines, sines, scalars, q_place, k_place, *arrived))
    t = grow(0, (*t, wo_other[:8, :128]))
    t = start_block(1, t)
    t = project_block(0, t)
    t = grow(1, t)
    t = start_block(2, t)
    t = attend_block(0, t)
    t = project_block(1, t)
    t = grow(2, t)
    t = attend_block(1, t)
    t = shrink(0, 1, t)
    t = project_block(2, t)
    t = shrink(1, 1, t)
    t = shrink(0, 0, t)
    t = attend_block(2, t)
    t = shrink(1, 0, t)
    t = shrink(2, 1, t)
    t = shrink(2, 0, t)
    return jnp.stack(results)[None]


def solution(mesh):
    placed = (
        P("section", None, "tensor", None),
        P("section", None),
        P("section", None, "tensor"),
        P("section", None, None, "tensor"),
        P("section", "tensor", None),
        P("section", None, None, None),
        P("section", None),
    )
    return jax.shard_map(
        shards,
        mesh=mesh,
        in_specs=placed,
        out_specs=P("section", None, "tensor", None),
        check_vma=False,
    )
```

time: 292 us -> 223 us (0.76); the launches traced: 291 us -> 219 us
  waiting for transfers between devices: 134 us -> 74.3 us
  other arithmetic: 12.9 us -> 6.01 us
  starting transfers between devices: 51.7 us -> 45.3 us
  blocking collectives: 0 us -> 5.83 us
  local copies, waits for them, and re-layouts: 21.1 us -> 17 us
    ppermute x36 -> x30, waiting for transfers between devices: 110 us -> 67.2 us  [move(): return lax.ppermute(value, 'tensor', pairs)]
    ppermute x3 -> x6, waiting for transfers between devices: 24.1 us -> 7.13 us  [from_behind(): return lax.ppermute(value, ('section', 'tensor'), pairs)]
    slice x16 -> x3, local copies, waits for them, and re-layouts: 13.1 us -> 2.01 us  [the longest x2 1.35 us: shards(): arrived = (wq_other[:8, :128], wkv_other[:8, :128])]
    unnamed x72 -> x50, local copies, waits for them, and re-layouts: 2.16 us -> 9.2 us
    ppermute x36 -> x30, starting transfers between devices: 47.4 us -> 40.9 us  [move(): return lax.ppermute(value, 'tensor', pairs)]
    all_gather x0 -> x3, blocking collectives: none -> 5.83 us  [shards(): share = lambda a: lax.all_gather(a, 'tensor', axis_index_groups=pairs)]
    pallas_call x6 -> x18, Pallas kernels: 70.5 us -> 69.3 us  [the longest x3 32.7 us: attend(): pl.pallas_call(functools.partial(attend_kernel, blocks, order, lanes), ou...]
  transfers between devices with their start and end apart: 39 -> 36, of which waited for: 22 -> 15; matrix products, arithmetic and copies ran while one was open for 10% -> 6% of each run, Pallas kernels for 20% -> 32%
where the time goes in v2:
time: 223 us; the launch traced here: 219 us
  waiting for transfers between devices  74.3 us (33%)
  Pallas kernels  69.3 us (31%)
  starting transfers between devices  45.3 us (20%)
  local copies, waits for them, and re-layouts  17 us (8%)
  other arithmetic  6.01 us (3%)
  blocking collectives  5.83 us (3%)
    ppermute x30, waiting for transfers between devices, move(): return lax.ppermute(value, 'tensor', pairs)  67.2 us
    ppermute x30, starting transfers between devices, move(): return lax.ppermute(value, 'tensor', pairs)  40.9 us
    pallas_call x3, Pallas kernels, attend(): pl.pallas_call(functools.partial(attend_kernel, blocks, order, lanes), ou...  32.7 us
    pallas_call x3, Pallas kernels, project(): pl.pallas_call(project_kernel, out_shape=(bf16(8, ROWS, HD), bf16(2, ROWS...  29.8 us
    unnamed x50, local copies, waits for them, and re-layouts  9.2 us
    ppermute x6, waiting for transfers between devices, from_behind(): return lax.ppermute(value, ('section', 'tensor'), pairs)  7.13 us
    pallas_call x12, Pallas kernels, small(): pl.pallas_call(body, grid=(1,), in_specs=specs + [ANY] * len(after), out_...  6.83 us
    all_gather x3, blocking collectives, shards(): share = lambda a: lax.all_gather(a, 'tensor', axis_index_groups=pairs)  5.83 us
  transfers between devices with their start and end apart: 36, of which 15 were waited for; matrix products, arithmetic and copies ran while one was open for 6% of the time, Pallas kernels for 32%

profile of v2, /device:TPU:0, one launch (start us, length us, event | category | flops | bytes accessed | tf_op | source)
XLA Modules:
  0.0 218.5 jit_solution(11160040776225783430)
XLA Ops:
  0.5 2.3 %slice_bitcast_fusion.2 = (bf16[1,24,8192]{2,1,0:T(8,128)(2,1)}, bf16[1,24,8192]{2,1,0:T(8,128)(2,1)}, bf16[1,24,8192]{2,1,0:T(8,128)(2,1)}) fusion(bf16[1,3,24,8192]{3,2,1,0:T(8,128)(2,1)} %param.7), kind=kLoop, calls=%fused_computation.13 | loop fusion | bytes 2359296 | tf_op jit(solution)/shard_map/squeeze | solution.py:361
  2.8 2.6 %collective-permute-start.1 = (bf16[1,24,8192]{2,1,0:T(8,128)(2,1)}, bf16[1,24,8192]{2,1,0:T(8,128)(2,1)S(1)}, u32[]{:S(2)}, u32[]{:S(2)}) collective-permute-start(bf16[1,24,8192]{2,1,0:T(8,128)(2,1)} %get-tuple-element.123), channel_id=1, source_target_pairs={{0,24},{1,25},{2,26},{3,27},{4,28},{5,29},{6,30},{7,31},{8,16},{9,... | collective-permute-start | bytes 1179656 | tf_op jit(solution)/shard_map/ppermute | solution.py:70
  5.4 1.5 collective-permute-start
  6.8 3.2 %copy.17.wkv_mine = bf16[8192,128]{1,0:T(8,128)(2,1)S(1)} copy(bf16[8192,128]{0,1:T(8,128)(2,1)} %bitcast.39) | data formatting | bytes 4194304 | tf_op jit(solution)/shard_map/reshape;squeeze | solution.py:365
  10.6 1.9 fusion.1
  12.9 1.2 pad_maximum_fusion.refs_3_.cosine
  15.3 4.0 %collective-permute-done.3.wkv_other = bf16[8192,128]{1,0:T(8,128)(2,1)} collective-permute-done((bf16[8192,128]{1,0:T(8,128)(2,1)S(1)}, bf16[8192,128]{1,0:T(8,128)(2,1)}, u32[]{:S(2)}, u32[]{:S(2)}) %collective-permute-start.3) | collective-permute-done | bytes 2097184 | tf_op jit(solution)/shard_map/ppermute | solution.py:59
  20.6 5.6 %collective-permute-done.refs_0_.refs_2_ = bf16[1,24,8192]{2,1,0:T(8,128)(2,1)S(1)} collective-permute-done((bf16[1,24,8192]{2,1,0:T(8,128)(2,1)}, bf16[1,24,8192]{2,1,0:T(8,128)(2,1)S(1)}, u32[]{:S(2)}, u32[]{:S(2)}) %collective-permute-start) | collective-permute-done | bytes 393248 | tf_op jit(solution)/shard_map/ppermute | solution.py:70
  26.7 4.1 %collective-permute-start.5 = (bf16[48,8192]{1,0:T(8,128)(2,1)S(1)}, bf16[48,8192]{1,0:T(8,128)(2,1)S(1)}, u32[]{:S(2)}, u32[]{:S(2)}) collective-permute-start(bf16[48,8192]{1,0:T(8,128)(2,1)S(1)} %get-tuple-element.64.own), channel_id=1, source_target_pairs={{0,6},{1,7},{2,4},{3,5},{4,2},{5,3},{6,0},{7,1},{8,14},{9,15},{10,... | collective-permute-start | bytes 2359304 | tf_op jit(solution)/shard_map/ppermute | solution.py:59
  31.7 16.0 %collective-permute-done.5.refs_1_.over_b = bf16[48,8192]{1,0:T(8,128)(2,1)S(1)} collective-permute-done((bf16[48,8192]{1,0:T(8,128)(2,1)S(1)}, bf16[48,8192]{1,0:T(8,128)(2,1)S(1)}, u32[]{:S(2)}, u32[]{:S(2)}) %collective-permute-start.5) | collective-permute-done | bytes 786464 | tf_op jit(solution)/shard_map/ppermute | solution.py:59
  47.7 1.5 collective-permute-done.4.refs_0_.over_a
  49.2 1.6 collective-permute-start.7
  51.0 1.5 collective-permute-done.9.refs_0_.refs_4_
  53.6 9.0 %collective-permute-done.7.far_a = bf16[48,4096]{1,0:T(8,128)(2,1)S(1)} collective-permute-done((bf16[48,4096]{1,0:T(8,128)(2,1)S(1)}, bf16[48,4096]{1,0:T(8,128)(2,1)S(1)}, u32[]{:S(2)}, u32[]{:S(2)}) %collective-permute-start.7) | collective-permute-done | bytes 393248 | tf_op jit(solution)/shard_map/ppermute | solution.py:59
  62.6 9.9 %project.3 = (bf16[8,192,128]{2,1,0:T(8,128)(2,1)S(1)}, bf16[2,192,128]{2,1,0:T(8,128)(2,1)S(1)}) custom-call(bf16[48,8192]{1,0:T(8,128)(2,1)S(1)} %get-tuple-element.64.own, bf16[48,8192]{1,0:T(8,128)(2,1)S(1)} %collective-permute-done.4.refs_0_.over_a, bf16[48,8192]{1,0:T(8,128)(2,1)S(1)} %collective-permute-done.5.refs_1_.over_b, ...), custom_call_target="tpu_custom_call" | custom-call | flops 12000000000 | tf_op jit(solution)/shard_map/project/pallas_call | solution.py:231
  72.6 3.8 %collective-permute-done.14.refs_1_.over_b = bf16[48,8192]{1,0:T(8,128)(2,1)S(1)} collective-permute-done((bf16[48,8192]{1,0:T(8,128)(2,1)S(1)}, bf16[48,8192]{1,0:T(8,128)(2,1)S(1)}, u32[]{:S(2)}, u32[]{:S(2)}) %collective-permute-start.14) | collective-permute-done | bytes 786464 | tf_op jit(solution)/shard_map/ppermute | solution.py:59
  76.7 1.6 collective-permute-start.16
  78.3 1.9 all-gather
  80.2 1.4 norm.5
  81.6 1.7 collective-permute-start.19
  83.3 1.7 collective-permute-start.18
  85.0 10.6 %attend.3 = (bf16[96,8192]{1,0:T(8,128)(2,1)S(1)}, bf16[96,8192]{1,0:T(8,128)(2,1)}, f32[8,128]{1,0:T(8,128)S(1)}) custom-call(s32[2]{0:T(128)S(1)} %pad_add_fusion.refs_5_.scalars, bf16[8,192,128]{2,1,0:T(8,128)(2,1)S(1)} %get-tuple-element.70.query, bf16[2,384,1024]{2,1,0:T(8,128)(2,1)S(1)} %bitcast.26, s32[192,1]{1,0:T(8,128)S(1)} %copy.18.refs_6_.q_place, ...), custom_call_target="tpu_custom_call" | custom-call | tf_op jit(solution)/shard_map/attend/pallas_call | solution.py:329
  98.1 1.1 copy-done.11
  101.3 9.9 %project.4 = (bf16[8,192,128]{2,1,0:T(8,128)(2,1)S(1)}, bf16[2,192,128]{2,1,0:T(8,128)(2,1)S(1)}) custom-call(bf16[48,8192]{1,0:T(8,128)(2,1)S(1)} %copy-done.11, bf16[48,8192]{1,0:T(8,128)(2,1)S(1)} %copy-done.4, bf16[48,8192]{1,0:T(8,128)(2,1)S(1)} %copy-done.2, bf16[48,4096]{1,0:T(8,128)(2,1)S(1)} %copy-done.17, bf16[48,4096]{1,0:T(8,128)(2,1)S(1)} %copy-done.19, ...), custom_call_target="tpu_custom_call" | custom-call | flops 12000000000 | tf_op jit(solution)/shard_map/project/pallas_call | solution.py:231
  111.2 1.9 all-gather.1
  113.2 1.6 collective-permute-start.23
  115.8 11.7 %attend.4 = (bf16[96,4096]{1,0:T(8,128)(2,1)S(1)}, bf16[96,4096]{1,0:T(8,128)(2,1)}, bf16[96,4096]{1,0:T(8,128)(2,1)S(1)}, bf16[96,4096]{1,0:T(8,128)(2,1)}, f32[8,128]{1,0:T(8,128)S(1)}) custom-call(s32[2]{0:T(128)S(1)} %pad_add_fusion.refs_5_.scalars, bf16[8,192,128]{2,1,0:T(8,128)(2,1)S(1)} %copy-done.21, bf16[2,384,1024]{2,1,0:T(8,128)(2,1)S(1)} %bitcast.27, ...), custom_call_target="tpu_custom_call" | custom-call | flops 12000000000 | tf_op jit(solution)/shard_map/attend/pallas_call | solution.py:329
  127.5 2.1 collective-permute-start.21
  129.6 10.2 %collective-permute-start.22 = (bf16[96,4096]{1,0:T(8,128)(2,1)}, bf16[96,4096]{1,0:T(8,128)(2,1)}, u32[]{:S(2)}, u32[]{:S(2)}) collective-permute-start(bf16[96,4096]{1,0:T(8,128)(2,1)} %get-tuple-element.90), channel_id=1, source_target_pairs={{0,8},{1,9},{2,10},{3,11},{4,12},{5,13},{6,14},{7,15},{8,0},{9,1},... | collective-permute-start | bytes 2359304 | tf_op jit(solution)/shard_map/ppermute | solution.py:59
  139.8 1.2 halve.6
  140.9 1.7 collective-permute-start.20
  146.2 10.0 %project.5 = (bf16[8,192,128]{2,1,0:T(8,128)(2,1)S(1)}, bf16[2,192,128]{2,1,0:T(8,128)(2,1)S(1)}) custom-call(bf16[48,8192]{1,0:T(8,128)(2,1)} %get-tuple-element.82.own, bf16[48,8192]{1,0:T(8,128)(2,1)S(1)} %collective-permute-done.18.refs_0_.over_a, bf16[48,8192]{1,0:T(8,128)(2,1)S(1)} %collective-permute-done.19.refs_1_.over_b, ...), custom_call_target="tpu_custom_call" | custom-call | flops 12000000000 | tf_op jit(solution)/shard_map/project/pallas_call | solution.py:231
  156.2 1.9 all-gather.2
  158.2 1.7 halve.7
  160.9 1.6 collective-permute-start.27
  162.7 10.4 %attend.5 = (bf16[96,4096]{1,0:T(8,128)(2,1)S(1)}, bf16[96,4096]{1,0:T(8,128)(2,1)S(1)}, bf16[96,4096]{1,0:T(8,128)(2,1)S(1)}, bf16[96,4096]{1,0:T(8,128)(2,1)S(1)}, f32[8,128]{1,0:T(8,128)S(1)}) custom-call(s32[2]{0:T(128)S(1)} %pad_add_fusion.refs_5_.scalars, bf16[8,192,128]{2,1,0:T(8,128)(2,1)S(1)} %get-tuple-element.102.query, ...), custom_call_target="tpu_custom_call" | custom-call | flops 12000000000 | tf_op jit(solution)/shard_map/attend/pallas_call | solution.py:329
  173.3 1.7 collective-permute-start.28
  175.1 2.0 collective-permute-start.29
  177.1 1.6 collective-permute-start.30
  179.7 2.6 %collective-permute-done.28 = bf16[24,4096]{1,0:T(8,128)(2,1)S(1)} collective-permute-done((bf16[24,4096]{1,0:T(8,128)(2,1)S(1)}, bf16[24,4096]{1,0:T(8,128)(2,1)S(1)}, u32[]{:S(2)}, u32[]{:S(2)}) %collective-permute-start.28) | collective-permute-done | bytes 196640 | tf_op jit(solution)/shard_map/ppermute | solution.py:59
  182.3 7.3 %collective-permute-done.29 = bf16[24,4096]{1,0:T(8,128)(2,1)S(1)} collective-permute-done((bf16[24,4096]{1,0:T(8,128)(2,1)S(1)}, bf16[24,4096]{1,0:T(8,128)(2,1)S(1)}, u32[]{:S(2)}, u32[]{:S(2)}) %collective-permute-start.29) | collective-permute-done | bytes 196640 | tf_op jit(solution)/shard_map/ppermute | solution.py:59
  189.7 8.2 %collective-permute-done.30.refs_1_ = bf16[96,4096]{1,0:T(8,128)(2,1)S(1)} collective-permute-done((bf16[96,4096]{1,0:T(8,128)(2,1)S(1)}, bf16[96,4096]{1,0:T(8,128)(2,1)S(1)}, u32[]{:S(2)}, u32[]{:S(2)}) %collective-permute-start.30) | collective-permute-done | bytes 786464 | tf_op jit(solution)/shard_map/ppermute | solution.py:59
  198.3 1.8 collective-permute-start.33
  200.1 8.1 %collective-permute-done.32.refs_1_ = bf16[48,4096]{1,0:T(8,128)(2,1)S(1)} collective-permute-done((bf16[48,4096]{1,0:T(8,128)(2,1)S(1)}, bf16[48,4096]{1,0:T(8,128)(2,1)S(1)}, u32[]{:S(2)}, u32[]{:S(2)}) %collective-permute-start.32) | collective-permute-done | bytes 393248 | tf_op jit(solution)/shard_map/ppermute | solution.py:59
  208.1 1.3 collective-permute-done.33.refs_3_
  211.9 4.0 %collective-permute-done.34 = bf16[24,4096]{1,0:T(8,128)(2,1)S(1)} collective-permute-done((bf16[24,4096]{1,0:T(8,128)(2,1)S(1)}, bf16[24,4096]{1,0:T(8,128)(2,1)S(1)}, u32[]{:S(2)}, u32[]{:S(2)}) %collective-permute-start.34) | collective-permute-done | bytes 196640 | tf_op jit(solution)/shard_map/ppermute | solution.py:59
  215.9 1.2 collective-permute-done.35
  217.2 1.1 maximum_bitcast_fusion
  (131 shorter events, 21.2 us)
Async XLA Ops:
  0.0 20.0 %collective-permute-start.2 = (bf16[8192,512]{1,0:T(8,128)(2,1)}, bf16[8192,512]{1,0:T(8,128)(2,1)}, u32[]{:S(2)}, u32[]{:S(2)}) collective-permute-start(bf16[8192,512]{1,0:T(8,128)(2,1)} %bitcast.43), channel_id=1, source_target_pairs={{0,1},{1,0},{2,3},{3,2},{4,5},{5,4},{6,7},{7,6},{8,9},{9,8},{10,11... | collective-permute-start | bytes 25165832 | tf_op jit(solution)/shard_map/ppermute | solution.py:59
  0.0 31.0 %collective-permute-start.6 = (bf16[512,8192]{1,0:T(8,128)(2,1)}, bf16[512,8192]{1,0:T(8,128)(2,1)}, u32[]{:S(2)}, u32[]{:S(2)}) collective-permute-start(bf16[512,8192]{1,0:T(8,128)(2,1)} %bitcast.35), channel_id=1, source_target_pairs={{0,1},{1,0},{2,3},{3,2},{4,5},{5,4},{6,7},{7,6},{8,9},{9,8},{10,11... | collective-permute-start | bytes 25165832 | tf_op jit(solution)/shard_map/ppermute | solution.py:59
  2.8 17.9 %collective-permute-start.1 = (bf16[1,24,8192]{2,1,0:T(8,128)(2,1)}, bf16[1,24,8192]{2,1,0:T(8,128)(2,1)S(1)}, u32[]{:S(2)}, u32[]{:S(2)}) collective-permute-start(bf16[1,24,8192]{2,1,0:T(8,128)(2,1)} %get-tuple-element.123), channel_id=1, source_target_pairs={{0,24},{1,25},{2,26},{3,27},{4,28},{5,29},{6,30},{7,31},{8,16},{9,... | collective-permute-start | bytes 1179656 | tf_op jit(solution)/shard_map/ppermute | solution.py:70
  5.4 20.9 %collective-permute-start = (bf16[1,24,8192]{2,1,0:T(8,128)(2,1)}, bf16[1,24,8192]{2,1,0:T(8,128)(2,1)S(1)}, u32[]{:S(2)}, u32[]{:S(2)}) collective-permute-start(bf16[1,24,8192]{2,1,0:T(8,128)(2,1)} %get-tuple-element.123), channel_id=1, source_target_pairs={{0,16},{1,17},{2,18},{3,19},{4,20},{5,21},{6,22},{7,23},{8,24},{9,... | collective-permute-start | bytes 1179656 | tf_op jit(solution)/shard_map/ppermute | solution.py:70
  10.1 16.2 %copy-start.9 = (bf16[1,8192]{1,0:T(2,128)(2,1)S(1)}, bf16[1,8192]{1,0:T(2,128)(2,1)}, u32[]{:S(2)}) copy-start(bf16[1,8192]{1,0:T(2,128)(2,1)} %refs_2_.5) | copy-start | bytes 49156
  10.1 9.2 %collective-permute-start.3 = (bf16[8192,128]{1,0:T(8,128)(2,1)S(1)}, bf16[8192,128]{1,0:T(8,128)(2,1)}, u32[]{:S(2)}, u32[]{:S(2)}) collective-permute-start(bf16[8192,128]{1,0:T(8,128)(2,1)S(1)} %copy.17.wkv_mine), channel_id=1, source_target_pairs={{0,1},{1,0},{2,3},{3,2},{4,5},{5,4},{6,7},{7,6},{8,9},{9,8},{10,11... | collective-permute-start | bytes 6291464 | tf_op jit(solution)/shard_map/ppermute | solution.py:59
  12.8 18.1 %copy-start.23 = (bf16[1,24,8192]{2,1,0:T(8,128)(2,1)S(1)}, bf16[1,24,8192]{2,1,0:T(8,128)(2,1)}, u32[]{:S(2)}) copy-start(bf16[1,24,8192]{2,1,0:T(8,128)(2,1)} %get-tuple-element.125) | copy-start | bytes 1179652
  15.3 35.5 %copy-start.22 = (bf16[1,24,8192]{2,1,0:T(8,128)(2,1)S(1)}, bf16[1,24,8192]{2,1,0:T(8,128)(2,1)}, u32[]{:S(2)}) copy-start(bf16[1,24,8192]{2,1,0:T(8,128)(2,1)} %get-tuple-element.124) | copy-start | bytes 1179652
  26.7 21.0 %collective-permute-start.5 = (bf16[48,8192]{1,0:T(8,128)(2,1)S(1)}, bf16[48,8192]{1,0:T(8,128)(2,1)S(1)}, u32[]{:S(2)}, u32[]{:S(2)}) collective-permute-start(bf16[48,8192]{1,0:T(8,128)(2,1)S(1)} %get-tuple-element.64.own), channel_id=1, source_target_pairs={{0,6},{1,7},{2,4},{3,5},{4,2},{5,3},{6,0},{7,1},{8,14},{9,15},{10,... | collective-permute-start | bytes 2359304 | tf_op jit(solution)/shard_map/ppermute | solution.py:59
  30.9 18.3 %collective-permute-start.4 = (bf16[48,8192]{1,0:T(8,128)(2,1)S(1)}, bf16[48,8192]{1,0:T(8,128)(2,1)S(1)}, u32[]{:S(2)}, u32[]{:S(2)}) collective-permute-start(bf16[48,8192]{1,0:T(8,128)(2,1)S(1)} %get-tuple-element.64.own), channel_id=1, source_target_pairs={{0,2},{1,3},{2,0},{3,1},{4,6},{5,7},{6,4},{7,5},{8,10},{9,11},{10,... | collective-permute-start | bytes 2359304 | tf_op jit(solution)/shard_map/ppermute | solution.py:59
  30.9 20.0 %collective-permute-start.10 = (bf16[1,24,8192]{2,1,0:T(8,128)(2,1)S(1)}, bf16[1,24,8192]{2,1,0:T(8,128)(2,1)S(1)}, u32[]{:S(2)}, u32[]{:S(2)}) collective-permute-start(bf16[1,24,8192]{2,1,0:T(8,128)(2,1)S(1)} %copy-done.23), channel_id=1, source_target_pairs={{0,24},{1,25},{2,26},{3,27},{4,28},{5,29},{6,30},{7,31},{8,16},{9,... | collective-permute-start | bytes 1179656 | tf_op jit(solution)/shard_map/ppermute | solution.py:70
  30.9 21.6 %collective-permute-start.9 = (bf16[1,24,8192]{2,1,0:T(8,128)(2,1)S(1)}, bf16[1,24,8192]{2,1,0:T(8,128)(2,1)S(1)}, u32[]{:S(2)}, u32[]{:S(2)}) collective-permute-start(bf16[1,24,8192]{2,1,0:T(8,128)(2,1)S(1)} %copy-done.23), channel_id=1, source_target_pairs={{0,16},{1,17},{2,18},{3,19},{4,20},{5,21},{6,22},{7,23},{8,24},{9,... | collective-permute-start | bytes 1179656 | tf_op jit(solution)/shard_map/ppermute | solution.py:70
  49.2 13.3 %collective-permute-start.7 = (bf16[48,4096]{1,0:T(8,128)(2,1)S(1)}, bf16[48,4096]{1,0:T(8,128)(2,1)S(1)}, u32[]{:S(2)}, u32[]{:S(2)}) collective-permute-start(bf16[48,4096]{1,0:T(8,128)(2,1)S(1)} %get-tuple-element.66), channel_id=1, source_target_pairs={{0,6},{1,7},{2,4},{3,5},{4,2},{5,3},{6,0},{7,1},{8,14},{9,15},{10,... | collective-permute-start | bytes 1179656 | tf_op jit(solution)/shard_map/ppermute | solution.py:59
  50.8 11.8 %collective-permute-start.8 = (bf16[48,4096]{1,0:T(8,128)(2,1)S(1)}, bf16[48,4096]{1,0:T(8,128)(2,1)S(1)}, u32[]{:S(2)}, u32[]{:S(2)}) collective-permute-start(bf16[48,4096]{1,0:T(8,128)(2,1)S(1)} %get-tuple-element.67), channel_id=1, source_target_pairs={{0,2},{1,3},{2,0},{3,1},{4,6},{5,7},{6,4},{7,5},{8,10},{9,11},{10,... | collective-permute-start | bytes 1179656 | tf_op jit(solution)/shard_map/ppermute | solution.py:59
  50.8 29.4 %collective-permute-start.12 = (bf16[1,24,8192]{2,1,0:T(8,128)(2,1)S(1)}, bf16[1,24,8192]{2,1,0:T(8,128)(2,1)S(1)}, u32[]{:S(2)}, u32[]{:S(2)}) collective-permute-start(bf16[1,24,8192]{2,1,0:T(8,128)(2,1)S(1)} %copy-done.22), channel_id=1, source_target_pairs={{0,24},{1,25},{2,26},{3,27},{4,28},{5,29},{6,30},{7,31},{8,16},{9,... | collective-permute-start | bytes 1179656 | tf_op jit(solution)/shard_map/ppermute | solution.py:70
  50.8 29.4 %collective-permute-start.11 = (bf16[1,24,8192]{2,1,0:T(8,128)(2,1)S(1)}, bf16[1,24,8192]{2,1,0:T(8,128)(2,1)S(1)}, u32[]{:S(2)}, u32[]{:S(2)}) collective-permute-start(bf16[1,24,8192]{2,1,0:T(8,128)(2,1)S(1)} %copy-done.22), channel_id=1, source_target_pairs={{0,16},{1,17},{2,18},{3,19},{4,20},{5,21},{6,22},{7,23},{8,24},{9,... | collective-permute-start | bytes 1179656 | tf_op jit(solution)/shard_map/ppermute | solution.py:70
  53.0 19.5 %copy-start.10 = (bf16[48,8192]{1,0:T(8,128)(2,1)}, bf16[48,8192]{1,0:T(8,128)(2,1)S(1)}, u32[]{:S(2)}) copy-start(bf16[48,8192]{1,0:T(8,128)(2,1)S(1)} %get-tuple-element.72.own) | copy-start | bytes 2359300
  53.0 23.3 %collective-permute-start.14 = (bf16[48,8192]{1,0:T(8,128)(2,1)S(1)}, bf16[48,8192]{1,0:T(8,128)(2,1)S(1)}, u32[]{:S(2)}, u32[]{:S(2)}) collective-permute-start(bf16[48,8192]{1,0:T(8,128)(2,1)S(1)} %get-tuple-element.72.own), channel_id=1, source_target_pairs={{0,6},{1,7},{2,4},{3,5},{4,2},{5,3},{6,0},{7,1},{8,14},{9,15},{10,... | collective-permute-start | bytes 2359304 | tf_op jit(solution)/shard_map/ppermute | solution.py:59
  62.6 14.1 %collective-permute-start.13 = (bf16[48,8192]{1,0:T(8,128)(2,1)S(1)}, bf16[48,8192]{1,0:T(8,128)(2,1)S(1)}, u32[]{:S(2)}, u32[]{:S(2)}) collective-permute-start(bf16[48,8192]{1,0:T(8,128)(2,1)S(1)} %get-tuple-element.72.own), channel_id=1, source_target_pairs={{0,2},{1,3},{2,0},{3,1},{4,6},{5,7},{6,4},{7,5},{8,10},{9,11},{10,... | collective-permute-start | bytes 2359304 | tf_op jit(solution)/shard_map/ppermute | solution.py:59
  72.5 12.5 %copy-start = (bf16[1,2,384,1024]{3,2,1,0:T(8,128)(2,1)S(1)}, bf16[1,2,384,1024]{3,2,1,0:T(8,128)(2,1)}, u32[]{:S(2)}) copy-start(bf16[1,2,384,1024]{3,2,1,0:T(8,128)(2,1)} %param.12) | copy-start | bytes 4718596
  76.6 8.4 %copy-start.3 = (bf16[48,8192]{1,0:T(8,128)(2,1)}, bf16[48,8192]{1,0:T(8,128)(2,1)S(1)}, u32[]{:S(2)}) copy-start(bf16[48,8192]{1,0:T(8,128)(2,1)S(1)} %collective-permute-done.13.refs_0_.over_a) | copy-start | bytes 2359300
  76.7 19.9 %collective-permute-start.16 = (bf16[48,4096]{1,0:T(8,128)(2,1)S(1)}, bf16[48,4096]{1,0:T(8,128)(2,1)S(1)}, u32[]{:S(2)}, u32[]{:S(2)}) collective-permute-start(bf16[48,4096]{1,0:T(8,128)(2,1)S(1)} %get-tuple-element.77), channel_id=1, source_target_pairs={{0,6},{1,7},{2,4},{3,5},{4,2},{5,3},{6,0},{7,1},{8,14},{9,15},{10,... | collective-permute-start | bytes 1179656 | tf_op jit(solution)/shard_map/ppermute | solution.py:59
  78.3 19.1 %collective-permute-start.17 = (bf16[48,4096]{1,0:T(8,128)(2,1)S(1)}, bf16[48,4096]{1,0:T(8,128)(2,1)S(1)}, u32[]{:S(2)}, u32[]{:S(2)}) collective-permute-start(bf16[48,4096]{1,0:T(8,128)(2,1)S(1)} %get-tuple-element.78), channel_id=1, source_target_pairs={{0,2},{1,3},{2,0},{3,1},{4,6},{5,7},{6,4},{7,5},{8,10},{9,11},{10,... | collective-permute-start | bytes 1179656 | tf_op jit(solution)/shard_map/ppermute | solution.py:59
  81.6 31.5 %collective-permute-start.19 = (bf16[48,8192]{1,0:T(8,128)(2,1)}, bf16[48,8192]{1,0:T(8,128)(2,1)S(1)}, u32[]{:S(2)}, u32[]{:S(2)}) collective-permute-start(bf16[48,8192]{1,0:T(8,128)(2,1)} %get-tuple-element.82.own), channel_id=1, source_target_pairs={{0,6},{1,7},{2,4},{3,5},{4,2},{5,3},{6,0},{7,1},{8,14},{9,15},{10,... | collective-permute-start | bytes 2359304 | tf_op jit(solution)/shard_map/ppermute | solution.py:59
  83.3 29.8 %collective-permute-start.18 = (bf16[48,8192]{1,0:T(8,128)(2,1)}, bf16[48,8192]{1,0:T(8,128)(2,1)S(1)}, u32[]{:S(2)}, u32[]{:S(2)}) collective-permute-start(bf16[48,8192]{1,0:T(8,128)(2,1)} %get-tuple-element.82.own), channel_id=1, source_target_pairs={{0,2},{1,3},{2,0},{3,1},{4,6},{5,7},{6,4},{7,5},{8,10},{9,11},{10,... | collective-permute-start | bytes 2359304 | tf_op jit(solution)/shard_map/ppermute | solution.py:59
  85.0 13.1 %copy-start.2 = (bf16[48,8192]{1,0:T(8,128)(2,1)S(1)}, bf16[48,8192]{1,0:T(8,128)(2,1)}, u32[]{:S(2)}) copy-start(bf16[48,8192]{1,0:T(8,128)(2,1)} %copy-done.1) | copy-start | bytes 2359300
  85.0 13.1 %copy-start.4 = (bf16[48,8192]{1,0:T(8,128)(2,1)S(1)}, bf16[48,8192]{1,0:T(8,128)(2,1)}, u32[]{:S(2)}) copy-start(bf16[48,8192]{1,0:T(8,128)(2,1)} %copy-done.3) | copy-start | bytes 2359300
  95.6 44.2 %collective-permute-start.15 = (bf16[96,8192]{1,0:T(8,128)(2,1)}, bf16[96,8192]{1,0:T(8,128)(2,1)S(1)}, u32[]{:S(2)}, u32[]{:S(2)}) collective-permute-start(bf16[96,8192]{1,0:T(8,128)(2,1)} %get-tuple-element.76), channel_id=1, source_target_pairs={{0,8},{1,9},{2,10},{3,11},{4,12},{5,13},{6,14},{7,15},{8,0},{9,1},... | collective-permute-start | bytes 4718600 | tf_op jit(solution)/shard_map/ppermute | solution.py:59
  113.2 29.5 %collective-permute-start.23 = (bf16[48,4096]{1,0:T(8,128)(2,1)S(1)}, bf16[48,4096]{1,0:T(8,128)(2,1)S(1)}, u32[]{:S(2)}, u32[]{:S(2)}) collective-permute-start(bf16[48,4096]{1,0:T(8,128)(2,1)S(1)} %get-tuple-element.91), channel_id=1, source_target_pairs={{0,6},{1,7},{2,4},{3,5},{4,2},{5,3},{6,0},{7,1},{8,14},{9,15},{10,... | collective-permute-start | bytes 1179656 | tf_op jit(solution)/shard_map/ppermute | solution.py:59
  114.8 28.6 %collective-permute-start.24 = (bf16[48,4096]{1,0:T(8,128)(2,1)S(1)}, bf16[48,4096]{1,0:T(8,128)(2,1)S(1)}, u32[]{:S(2)}, u32[]{:S(2)}) collective-permute-start(bf16[48,4096]{1,0:T(8,128)(2,1)S(1)} %get-tuple-element.92), channel_id=1, source_target_pairs={{0,2},{1,3},{2,0},{3,1},{4,6},{5,7},{6,4},{7,5},{8,10},{9,11},{10,... | collective-permute-start | bytes 1179656 | tf_op jit(solution)/shard_map/ppermute | solution.py:59
  127.5 13.4 %copy-start.5 = (bf16[96,4096]{1,0:T(8,128)(2,1)}, bf16[96,4096]{1,0:T(8,128)(2,1)S(1)}, u32[]{:S(2)}) copy-start(bf16[96,4096]{1,0:T(8,128)(2,1)S(1)} %get-tuple-element.87.refs_0_) | copy-start | bytes 2359300
  127.5 13.4 %copy-start.7 = (bf16[96,4096]{1,0:T(8,128)(2,1)}, bf16[96,4096]{1,0:T(8,128)(2,1)S(1)}, u32[]{:S(2)}) copy-start(bf16[96,4096]{1,0:T(8,128)(2,1)S(1)} %get-tuple-element.89.refs_2_) | copy-start | bytes 2359300
  127.5 30.7 %collective-permute-start.21 = (bf16[96,4096]{1,0:T(8,128)(2,1)}, bf16[96,4096]{1,0:T(8,128)(2,1)}, u32[]{:S(2)}, u32[]{:S(2)}) collective-permute-start(bf16[96,4096]{1,0:T(8,128)(2,1)} %get-tuple-element.88), channel_id=1, source_target_pairs={{0,2},{1,3},{2,0},{3,1},{4,6},{5,7},{6,4},{7,5},{8,10},{9,11},{10,... | collective-permute-start | bytes 2359304 | tf_op jit(solution)/shard_map/ppermute | solution.py:59
  129.6 28.6 %collective-permute-start.22 = (bf16[96,4096]{1,0:T(8,128)(2,1)}, bf16[96,4096]{1,0:T(8,128)(2,1)}, u32[]{:S(2)}, u32[]{:S(2)}) collective-permute-start(bf16[96,4096]{1,0:T(8,128)(2,1)} %get-tuple-element.90), channel_id=1, source_target_pairs={{0,8},{1,9},{2,10},{3,11},{4,12},{5,13},{6,14},{7,15},{8,0},{9,1},... | collective-permute-start | bytes 2359304 | tf_op jit(solution)/shard_map/ppermute | solution.py:59
  140.9 21.6 %collective-permute-start.20 = (bf16[48,8192]{1,0:T(8,128)(2,1)}, bf16[48,8192]{1,0:T(8,128)(2,1)S(1)}, u32[]{:S(2)}, u32[]{:S(2)}) collective-permute-start(bf16[48,8192]{1,0:T(8,128)(2,1)} %get-tuple-element.86), channel_id=1, source_target_pairs={{0,6},{1,7},{2,4},{3,5},{4,2},{5,3},{6,0},{7,1},{8,14},{9,15},{10,... | collective-permute-start | bytes 2359304 | tf_op jit(solution)/shard_map/ppermute | solution.py:59
  146.2 12.0 %copy-start.6 = (bf16[96,4096]{1,0:T(8,128)(2,1)S(1)}, bf16[96,4096]{1,0:T(8,128)(2,1)}, u32[]{:S(2)}) copy-start(bf16[96,4096]{1,0:T(8,128)(2,1)} %copy-done.5) | copy-start | bytes 2359300
  146.2 12.0 %copy-start.8 = (bf16[96,4096]{1,0:T(8,128)(2,1)S(1)}, bf16[96,4096]{1,0:T(8,128)(2,1)}, u32[]{:S(2)}) copy-start(bf16[96,4096]{1,0:T(8,128)(2,1)} %copy-done.7) | copy-start | bytes 2359300
  159.9 13.2 %collective-permute-start.26 = (bf16[48,4096]{1,0:T(8,128)(2,1)S(1)}, bf16[48,4096]{1,0:T(8,128)(2,1)S(1)}, u32[]{:S(2)}, u32[]{:S(2)}) collective-permute-start(bf16[48,4096]{1,0:T(8,128)(2,1)S(1)} %get-tuple-element.99), channel_id=1, source_target_pairs={{0,8},{1,9},{2,10},{3,11},{4,12},{5,13},{6,14},{7,15},{8,0},{9,1},... | collective-permute-start | bytes 1179656 | tf_op jit(solution)/shard_map/ppermute | solution.py:59
  160.9 12.2 %collective-permute-start.27 = (bf16[48,4096]{1,0:T(8,128)(2,1)S(1)}, bf16[48,4096]{1,0:T(8,128)(2,1)S(1)}, u32[]{:S(2)}, u32[]{:S(2)}) collective-permute-start(bf16[48,4096]{1,0:T(8,128)(2,1)S(1)} %get-tuple-element.101), channel_id=1, source_target_pairs={{0,6},{1,7},{2,4},{3,5},{4,2},{5,3},{6,0},{7,1},{8,14},{9,15},{10,... | collective-permute-start | bytes 1179656 | tf_op jit(solution)/shard_map/ppermute | solution.py:59
  173.3 9.0 %collective-permute-start.28 = (bf16[24,4096]{1,0:T(8,128)(2,1)S(1)}, bf16[24,4096]{1,0:T(8,128)(2,1)S(1)}, u32[]{:S(2)}, u32[]{:S(2)}) collective-permute-start(bf16[24,4096]{1,0:T(8,128)(2,1)S(1)} %get-tuple-element.106), channel_id=1, source_target_pairs={{0,6},{1,7},{2,4},{3,5},{4,2},{5,3},{6,0},{7,1},{8,14},{9,15},{10,... | collective-permute-start | bytes 589832 | tf_op jit(solution)/shard_map/ppermute | solution.py:59
  175.1 36.2 %collective-permute-start.25 = (bf16[24,8192]{1,0:T(8,128)(2,1)S(1)}, bf16[24,8192]{1,0:T(8,128)(2,1)S(1)}, u32[]{:S(2)}, u32[]{:S(2)}) collective-permute-start(bf16[24,8192]{1,0:T(8,128)(2,1)S(1)} %get-tuple-element.97), channel_id=1, source_target_pairs={{0,2},{1,3},{2,0},{3,1},{4,6},{5,7},{6,4},{7,5},{8,10},{9,11},{10,... | collective-permute-start | bytes 1179656 | tf_op jit(solution)/shard_map/ppermute | solution.py:59
  175.1 14.6 %collective-permute-start.29 = (bf16[24,4096]{1,0:T(8,128)(2,1)S(1)}, bf16[24,4096]{1,0:T(8,128)(2,1)S(1)}, u32[]{:S(2)}, u32[]{:S(2)}) collective-permute-start(bf16[24,4096]{1,0:T(8,128)(2,1)S(1)} %get-tuple-element.108), channel_id=1, source_target_pairs={{0,2},{1,3},{2,0},{3,1},{4,6},{5,7},{6,4},{7,5},{8,10},{9,11},{10,... | collective-permute-start | bytes 589832 | tf_op jit(solution)/shard_map/ppermute | solution.py:59
  177.1 20.8 %collective-permute-start.30 = (bf16[96,4096]{1,0:T(8,128)(2,1)S(1)}, bf16[96,4096]{1,0:T(8,128)(2,1)S(1)}, u32[]{:S(2)}, u32[]{:S(2)}) collective-permute-start(bf16[96,4096]{1,0:T(8,128)(2,1)S(1)} %get-tuple-element.110), channel_id=1, source_target_pairs={{0,6},{1,7},{2,4},{3,5},{4,2},{5,3},{6,0},{7,1},{8,14},{9,15},{10,... | collective-permute-start | bytes 2359304 | tf_op jit(solution)/shard_map/ppermute | solution.py:59
  178.7 19.2 %collective-permute-start.31 = (bf16[96,4096]{1,0:T(8,128)(2,1)S(1)}, bf16[96,4096]{1,0:T(8,128)(2,1)S(1)}, u32[]{:S(2)}, u32[]{:S(2)}) collective-permute-start(bf16[96,4096]{1,0:T(8,128)(2,1)S(1)} %get-tuple-element.112), channel_id=1, source_target_pairs={{0,8},{1,9},{2,10},{3,11},{4,12},{5,13},{6,14},{7,15},{8,0},{9,1},... | collective-permute-start | bytes 2359304 | tf_op jit(solution)/shard_map/ppermute | solution.py:59
  198.2 9.9 %collective-permute-start.32 = (bf16[48,4096]{1,0:T(8,128)(2,1)S(1)}, bf16[48,4096]{1,0:T(8,128)(2,1)S(1)}, u32[]{:S(2)}, u32[]{:S(2)}) collective-permute-start(bf16[48,4096]{1,0:T(8,128)(2,1)S(1)} %get-tuple-element.115), channel_id=1, source_target_pairs={{0,2},{1,3},{2,0},{3,1},{4,6},{5,7},{6,4},{7,5},{8,10},{9,11},{10,... | collective-permute-start | bytes 1179656 | tf_op jit(solution)/shard_map/ppermute | solution.py:59
  198.3 11.1 %collective-permute-start.33 = (bf16[48,4096]{1,0:T(8,128)(2,1)S(1)}, bf16[48,4096]{1,0:T(8,128)(2,1)S(1)}, u32[]{:S(2)}, u32[]{:S(2)}) collective-permute-start(bf16[48,4096]{1,0:T(8,128)(2,1)S(1)} %get-tuple-element.117), channel_id=1, source_target_pairs={{0,6},{1,7},{2,4},{3,5},{4,2},{5,3},{6,0},{7,1},{8,14},{9,15},{10,... | collective-permute-start | bytes 1179656 | tf_op jit(solution)/shard_map/ppermute | solution.py:59
  210.2 5.7 %collective-permute-start.34 = (bf16[24,4096]{1,0:T(8,128)(2,1)S(1)}, bf16[24,4096]{1,0:T(8,128)(2,1)S(1)}, u32[]{:S(2)}, u32[]{:S(2)}) collective-permute-start(bf16[24,4096]{1,0:T(8,128)(2,1)S(1)} %get-tuple-element.120), channel_id=1, source_target_pairs={{0,8},{1,9},{2,10},{3,11},{4,12},{5,13},{6,14},{7,15},{8,0},{9,1},... | collective-permute-start | bytes 589832 | tf_op jit(solution)/shard_map/ppermute | solution.py:59
  211.3 5.8 %collective-permute-start.35 = (bf16[24,4096]{1,0:T(8,128)(2,1)S(1)}, bf16[24,4096]{1,0:T(8,128)(2,1)S(1)}, u32[]{:S(2)}, u32[]{:S(2)}) collective-permute-start(bf16[24,4096]{1,0:T(8,128)(2,1)S(1)} %get-tuple-element.122), channel_id=1, source_target_pairs={{0,2},{1,3},{2,0},{3,1},{4,6},{5,7},{6,4},{7,5},{8,10},{9,11},{10,... | collective-permute-start | bytes 589832 | tf_op jit(solution)/shard_map/ppermute | solution.py:59
  (13 other events, 18.4 us)

commit v3 on v2

--- a/solution.py
+++ b/solution.py
@@ -15,9 +15,9 @@
 NZ = 4
 SHARD = 24
 ROWS = 192
-K_CHUNK = 2048
+K_CHUNK = 1024
 N_CHUNK = 2048
-PROJECT_COST = (12,12,12)
+PROJECT_COST = (12,0,12)
 ATTEND_COST = (0,12,12)
 Y, A, B = (1, 0), (0, 1), (0, 3)
 
@@ -71,6 +71,7 @@
 
 
 ANY = pl.BlockSpec(memory_space=pl.ANY)
+HBM = pl.BlockSpec(memory_space=pltpu.HBM)
 
 
 def params(mib):
@@ -168,9 +169,30 @@
 def project_kernel(
     own, over_a, over_b, far_a, far_b, wq_mine, wq_other, wkv_mine, wkv_other, cosine, sine, flag, *refs
 ):
-    query, kv, acc_q, acc_kv = refs[-4:]
+    query, kv, acc_q, acc_kv, wq, wkv, sems = refs[-7:]
     step = pl.program_id(0)
     steps = pl.num_programs(0)
+
+    def fetch(k):
+        rows = pl.ds(pl.multiple_of(k * K_CHUNK, K_CHUNK), K_CHUNK)
+        return [
+            pltpu.make_async_copy(source.at[rows], target.at[half, k], sems.at[kind + half, k])
+            for half, kind, source, target in (
+                (0, 0, wq_mine, wq),
+                (1, 0, wq_other, wq),
+                (0, 2, wkv_mine, wkv),
+                (1, 2, wkv_other, wkv),
+            )
+        ]
+
+    @pl.when(step == 0)
+    def _():
+        for k in range(D // K_CHUNK):
+            for copy in fetch(k):
+                copy.start()
+
+    for copy in fetch(step):
+        copy.wait()
     far = jnp.where(step < steps // 2, far_a[...], far_b[...])
     x = jnp.concatenate([own[...], over_a[...], over_b[...], far], axis=0)
 
@@ -179,13 +201,12 @@
         acc_q[...] = jnp.zeros_like(acc_q)
         acc_kv[...] = jnp.zeros_like(acc_kv)
 
-    for half, (wq, wkv) in enumerate(((wq_mine, wkv_mine), (wq_other, wkv_other))):
+    for half in range(2):
         acc_q[:, half * 512 : half * 512 + 512] += jnp.dot(
-            x, wq[...], preferred_element_type=jnp.float32
+            x, wq[half, step], preferred_element_type=jnp.float32
         )
-        acc_kv[:, half * HD : half * HD + HD] += jnp.dot(
-            x, wkv[...], preferred_element_type=jnp.float32
-        )
+    both = jnp.concatenate([wkv[0, step], wkv[1, step]], axis=1)
+    acc_kv[...] += jnp.dot(x, both, preferred_element_type=jnp.float32)
 
     @pl.when(step == steps - 1)
     def _():
@@ -225,7 +246,7 @@
     specs.append(pl.BlockSpec((PIECE, K_CHUNK), lambda k: (0, jnp.minimum(k, steps // 2 - 1))))
     specs.append(pl.BlockSpec((PIECE, K_CHUNK), lambda k: (0, jnp.maximum(k - steps // 2, 0))))
     for w in weights:
-        specs.append(pl.BlockSpec((K_CHUNK, w.shape[1]), lambda k: (k, 0)))
+        specs.append(HBM)
     table = pl.BlockSpec((None, ROWS, HD), lambda k: (which, 0, 0))
     specs += [table, table, full_spec(flag.shape)] + [ANY] * len(after)
     return pl.pallas_call(
@@ -240,6 +261,9 @@
         scratch_shapes=[
             pltpu.VMEM((ROWS, 1024), jnp.float32),
             pltpu.VMEM((ROWS, 2 * HD), jnp.float32),
+            pltpu.VMEM((2, steps, K_CHUNK, 512), jnp.bfloat16),
+            pltpu.VMEM((2, steps, K_CHUNK, HD), jnp.bfloat16),
+            pltpu.SemaphoreType.DMA((4, steps)),
         ],
         compiler_params=params(44),
         cost_estimate=cost(PROJECT_COST[which]),
@@ -317,8 +341,8 @@
         whole(q_place),
         whole(k_place),
         *[whole(w) for w in windows],
-        ANY,
-        ANY,
+        HBM,
+        HBM,
         *[ANY] * len(after),
     ]
     out_shape = []

time: 223 us -> 214 us (0.960); the launches traced: 219 us -> 214 us
  waiting for transfers between devices: 74.3 us -> 84.7 us
  starting transfers between devices: 45.3 us -> 35.7 us
  local copies, waits for them, and re-layouts: 17 us -> 10.7 us
    ppermute x30, waiting for transfers between devices: 67.2 us -> 77.5 us  [move(): return lax.ppermute(value, 'tensor', pairs)]
    ppermute x30, starting transfers between devices: 40.9 us -> 31.3 us  [move(): return lax.ppermute(value, 'tensor', pairs)]
    unnamed x50 -> x28, local copies, waits for them, and re-layouts: 9.2 us -> 2.87 us
  transfers between devices with their start and end apart: 36 -> 36, of which waited for: 15 -> 17; matrix products, arithmetic and copies ran while one was open for 6% -> 6% of each run, Pallas kernels for 32% -> 32%
where the time goes in v3:
time: 214 us
  waiting for transfers between devices  84.7 us (40%)
  Pallas kernels  69.9 us (33%)
  starting transfers between devices  35.7 us (17%)
  local copies, waits for them, and re-layouts  10.7 us (5%)
  blocking collectives  6.01 us (3%)
  other arithmetic  5.97 us (3%)
    ppermute x30, waiting for transfers between devices, move(): return lax.ppermute(value, 'tensor', pairs)  77.5 us
    pallas_call x3, Pallas kernels, attend(): pl.pallas_call(functools.partial(attend_kernel, blocks, order, lanes), ou...  32.7 us
    ppermute x30, starting transfers between devices, move(): return lax.ppermute(value, 'tensor', pairs)  31.3 us
    pallas_call x3, Pallas kernels, project(): pl.pallas_call(project_kernel, out_shape=(bf16(8, ROWS, HD), bf16(2, ROWS...  30.6 us
    ppermute x6, waiting for transfers between devices, from_behind(): return lax.ppermute(value, ('section', 'tensor'), pairs)  7.15 us
    pallas_call x12, Pallas kernels, small(): pl.pallas_call(body, grid=(1,), in_specs=specs + [ANY] * len(after), out_...  6.59 us
    all_gather x3, blocking collectives, shards(): share = lambda a: lax.all_gather(a, 'tensor', axis_index_groups=pairs)  6.01 us
    ppermute x6, starting transfers between devices, from_behind(): return lax.ppermute(value, ('section', 'tensor'), pairs)  4.37 us
  transfers between devices with their start and end apart: 36, of which 17 were waited for; matrix products, arithmetic and copies ran while one was open for 6% of the time, Pallas kernels for 32%

profile of v3, /device:TPU:0, one launch (start us, length us, event | category | flops | bytes accessed | tf_op | source)
XLA Modules:
  0.0 213.5 jit_solution(15459187663596449884)
XLA Ops:
  0.5 2.3 %slice_bitcast_fusion.2 = (bf16[1,24,8192]{2,1,0:T(8,128)(2,1)}, bf16[1,24,8192]{2,1,0:T(8,128)(2,1)}, bf16[1,24,8192]{2,1,0:T(8,128)(2,1)}) fusion(bf16[1,3,24,8192]{3,2,1,0:T(8,128)(2,1)} %param.7), kind=kLoop, calls=%fused_computation.13 | loop fusion | bytes 2359296 | tf_op jit(solution)/shard_map/squeeze | solution.py:385
  2.8 2.6 %collective-permute-start.1 = (bf16[1,24,8192]{2,1,0:T(8,128)(2,1)}, bf16[1,24,8192]{2,1,0:T(8,128)(2,1)S(1)}, u32[]{:S(2)}, u32[]{:S(2)}) collective-permute-start(bf16[1,24,8192]{2,1,0:T(8,128)(2,1)} %get-tuple-element.123), channel_id=1, source_target_pairs={{0,24},{1,25},{2,26},{3,27},{4,28},{5,29},{6,30},{7,31},{8,16},{9,... | collective-permute-start | bytes 1179656 | tf_op jit(solution)/shard_map/ppermute | solution.py:70
  5.4 1.5 collective-permute-start
  6.9 3.2 %copy.17.wkv_mine = bf16[8192,128]{1,0:T(8,128)(2,1)S(1)} copy(bf16[8192,128]{0,1:T(8,128)(2,1)} %bitcast.43) | data formatting | bytes 4194304 | tf_op jit(solution)/shard_map/reshape;squeeze | solution.py:389
  10.7 2.0 fusion.1
  13.0 1.2 pad_maximum_fusion.refs_3_.cosine
  14.2 1.1 pad_maximum_fusion.1.refs_4_.sine
  15.3 4.0 %collective-permute-done.3.wkv_other = bf16[8192,128]{1,0:T(8,128)(2,1)} collective-permute-done((bf16[8192,128]{1,0:T(8,128)(2,1)S(1)}, bf16[8192,128]{1,0:T(8,128)(2,1)}, u32[]{:S(2)}, u32[]{:S(2)}) %collective-permute-start.3) | collective-permute-done | bytes 2097184 | tf_op jit(solution)/shard_map/ppermute | solution.py:59
  20.6 5.6 %collective-permute-done.refs_0_.refs_2_ = bf16[1,24,8192]{2,1,0:T(8,128)(2,1)S(1)} collective-permute-done((bf16[1,24,8192]{2,1,0:T(8,128)(2,1)}, bf16[1,24,8192]{2,1,0:T(8,128)(2,1)S(1)}, u32[]{:S(2)}, u32[]{:S(2)}) %collective-permute-start) | collective-permute-done | bytes 393248 | tf_op jit(solution)/shard_map/ppermute | solution.py:70
  26.8 4.1 %collective-permute-start.5 = (bf16[48,8192]{1,0:T(8,128)(2,1)S(1)}, bf16[48,8192]{1,0:T(8,128)(2,1)S(1)}, u32[]{:S(2)}, u32[]{:S(2)}) collective-permute-start(bf16[48,8192]{1,0:T(8,128)(2,1)S(1)} %get-tuple-element.64.own), channel_id=1, source_target_pairs={{0,6},{1,7},{2,4},{3,5},{4,2},{5,3},{6,0},{7,1},{8,14},{9,15},{10,... | collective-permute-start | bytes 2359304 | tf_op jit(solution)/shard_map/ppermute | solution.py:59
  31.7 16.0 %collective-permute-done.5.refs_1_.over_b = bf16[48,8192]{1,0:T(8,128)(2,1)S(1)} collective-permute-done((bf16[48,8192]{1,0:T(8,128)(2,1)S(1)}, bf16[48,8192]{1,0:T(8,128)(2,1)S(1)}, u32[]{:S(2)}, u32[]{:S(2)}) %collective-permute-start.5) | collective-permute-done | bytes 786464 | tf_op jit(solution)/shard_map/ppermute | solution.py:59
  47.7 1.5 collective-permute-done.4.refs_0_.over_a
  49.3 1.6 collective-permute-start.7
  51.0 1.5 collective-permute-done.9.refs_0_.refs_4_
  53.6 9.0 %collective-permute-done.7.far_a = bf16[48,4096]{1,0:T(8,128)(2,1)S(1)} collective-permute-done((bf16[48,4096]{1,0:T(8,128)(2,1)S(1)}, bf16[48,4096]{1,0:T(8,128)(2,1)S(1)}, u32[]{:S(2)}, u32[]{:S(2)}) %collective-permute-start.7) | collective-permute-done | bytes 393248 | tf_op jit(solution)/shard_map/ppermute | solution.py:59
  62.6 8.7 %project.3 = (bf16[8,192,128]{2,1,0:T(8,128)(2,1)S(1)}, bf16[2,192,128]{2,1,0:T(8,128)(2,1)S(1)}) custom-call(bf16[48,8192]{1,0:T(8,128)(2,1)S(1)} %get-tuple-element.64.own, bf16[48,8192]{1,0:T(8,128)(2,1)S(1)} %collective-permute-done.4.refs_0_.over_a, bf16[48,8192]{1,0:T(8,128)(2,1)S(1)} %collective-permute-done.5.refs_1_.over_b, ...), custom_call_target="tpu_custom_call" | custom-call | flops 12000000000 | tf_op jit(solution)/shard_map/project/pallas_call | solution.py:252
  71.4 5.0 %collective-permute-done.14.refs_1_.over_b = bf16[48,8192]{1,0:T(8,128)(2,1)S(1)} collective-permute-done((bf16[48,8192]{1,0:T(8,128)(2,1)S(1)}, bf16[48,8192]{1,0:T(8,128)(2,1)S(1)}, u32[]{:S(2)}, u32[]{:S(2)}) %collective-permute-start.14) | collective-permute-done | bytes 786464 | tf_op jit(solution)/shard_map/ppermute | solution.py:59
  76.7 1.4 norm.5
  78.1 1.5 collective-permute-start.19
  79.6 2.1 all-gather
  81.7 10.6 %attend.3 = (bf16[96,8192]{1,0:T(8,128)(2,1)S(1)}, bf16[96,8192]{1,0:T(8,128)(2,1)}, f32[8,128]{1,0:T(8,128)S(1)}) custom-call(s32[2]{0:T(128)S(1)} %pad_add_fusion.refs_5_.scalars, bf16[8,192,128]{2,1,0:T(8,128)(2,1)S(1)} %get-tuple-element.70.query, bf16[2,384,1024]{2,1,0:T(8,128)(2,1)S(1)} %bitcast.26, s32[192,1]{1,0:T(8,128)S(1)} %copy.18.refs_6_.q_place, ...), custom_call_target="tpu_custom_call" | custom-call | tf_op jit(solution)/shard_map/attend/pallas_call | solution.py:353
  93.4 1.7 collective-permute-start.16
  95.1 1.4 collective-permute-start.17
  96.5 9.0 %collective-permute-done.16.far_a = bf16[48,4096]{1,0:T(8,128)(2,1)S(1)} collective-permute-done((bf16[48,4096]{1,0:T(8,128)(2,1)S(1)}, bf16[48,4096]{1,0:T(8,128)(2,1)S(1)}, u32[]{:S(2)}, u32[]{:S(2)}) %collective-permute-start.16) | collective-permute-done | bytes 393248 | tf_op jit(solution)/shard_map/ppermute | solution.py:59
  105.7 8.7 %project.4 = (bf16[8,192,128]{2,1,0:T(8,128)(2,1)S(1)}, bf16[2,192,128]{2,1,0:T(8,128)(2,1)S(1)}) custom-call(bf16[48,8192]{1,0:T(8,128)(2,1)S(1)} %copy-done.3, bf16[48,8192]{1,0:T(8,128)(2,1)S(1)} %collective-permute-done.13.refs_0_.over_a, bf16[48,8192]{1,0:T(8,128)(2,1)S(1)} %collective-permute-done.14.refs_1_.over_b, ...), custom_call_target="tpu_custom_call" | custom-call | tf_op jit(solution)/shard_map/project/pallas_call | solution.py:252
  114.4 1.9 all-gather.1
  116.4 1.2 parts.5
  118.5 1.6 collective-permute-start.23
  121.9 11.7 %attend.4 = (bf16[96,4096]{1,0:T(8,128)(2,1)S(1)}, bf16[96,4096]{1,0:T(8,128)(2,1)}, bf16[96,4096]{1,0:T(8,128)(2,1)S(1)}, bf16[96,4096]{1,0:T(8,128)(2,1)}, f32[8,128]{1,0:T(8,128)S(1)}) custom-call(s32[2]{0:T(128)S(1)} %pad_add_fusion.refs_5_.scalars, bf16[8,192,128]{2,1,0:T(8,128)(2,1)S(1)} %copy-done.10, bf16[2,384,1024]{2,1,0:T(8,128)(2,1)S(1)} %bitcast.27, ...), custom_call_target="tpu_custom_call" | custom-call | flops 12000000000 | tf_op jit(solution)/shard_map/attend/pallas_call | solution.py:353
  134.5 1.2 collective-permute-start.21
  136.7 1.2 halve.6
  137.9 1.7 collective-permute-start.20
  139.6 13.2 %project.5 = (bf16[8,192,128]{2,1,0:T(8,128)(2,1)S(1)}, bf16[2,192,128]{2,1,0:T(8,128)(2,1)S(1)}) custom-call(bf16[48,8192]{1,0:T(8,128)(2,1)} %get-tuple-element.82.own, bf16[48,8192]{1,0:T(8,128)(2,1)} %collective-permute-done.18.refs_0_.over_a, bf16[48,8192]{1,0:T(8,128)(2,1)S(1)} %copy-done.5, bf16[48,4096]{1,0:T(8,128)(2,1)S(1)} %collective-permute-done.23.far_a, ...), custom_call_target="tpu_custom_call" | custom-call | flops 12000000000 | tf_op jit(solution)/shard_map/project/pallas_call | solution.py:252
  152.8 1.9 all-gather.2
  156.2 1.7 collective-permute-start.27
  158.0 10.4 %attend.5 = (bf16[96,4096]{1,0:T(8,128)(2,1)S(1)}, bf16[96,4096]{1,0:T(8,128)(2,1)S(1)}, bf16[96,4096]{1,0:T(8,128)(2,1)S(1)}, bf16[96,4096]{1,0:T(8,128)(2,1)S(1)}, f32[8,128]{1,0:T(8,128)S(1)}) custom-call(s32[2]{0:T(128)S(1)} %pad_add_fusion.refs_5_.scalars, bf16[8,192,128]{2,1,0:T(8,128)(2,1)S(1)} %get-tuple-element.102.query, ...), custom_call_target="tpu_custom_call" | custom-call | flops 12000000000 | tf_op jit(solution)/shard_map/attend/pallas_call | solution.py:353
  168.7 1.7 collective-permute-start.28
  170.4 2.0 collective-permute-start.29
  172.5 1.6 collective-permute-start.30
  175.0 2.6 %collective-permute-done.28 = bf16[24,4096]{1,0:T(8,128)(2,1)S(1)} collective-permute-done((bf16[24,4096]{1,0:T(8,128)(2,1)S(1)}, bf16[24,4096]{1,0:T(8,128)(2,1)S(1)}, u32[]{:S(2)}, u32[]{:S(2)}) %collective-permute-start.28) | collective-permute-done | bytes 196640 | tf_op jit(solution)/shard_map/ppermute | solution.py:59
  177.6 7.3 %collective-permute-done.29 = bf16[24,4096]{1,0:T(8,128)(2,1)S(1)} collective-permute-done((bf16[24,4096]{1,0:T(8,128)(2,1)S(1)}, bf16[24,4096]{1,0:T(8,128)(2,1)S(1)}, u32[]{:S(2)}, u32[]{:S(2)}) %collective-permute-start.29) | collective-permute-done | bytes 196640 | tf_op jit(solution)/shard_map/ppermute | solution.py:59
  184.9 8.2 %collective-permute-done.30.refs_1_ = bf16[96,4096]{1,0:T(8,128)(2,1)S(1)} collective-permute-done((bf16[96,4096]{1,0:T(8,128)(2,1)S(1)}, bf16[96,4096]{1,0:T(8,128)(2,1)S(1)}, u32[]{:S(2)}, u32[]{:S(2)}) %collective-permute-start.30) | collective-permute-done | bytes 786464 | tf_op jit(solution)/shard_map/ppermute | solution.py:59
  193.6 1.8 collective-permute-start.33
  195.3 8.0 %collective-permute-done.32.refs_1_ = bf16[48,4096]{1,0:T(8,128)(2,1)S(1)} collective-permute-done((bf16[48,4096]{1,0:T(8,128)(2,1)S(1)}, bf16[48,4096]{1,0:T(8,128)(2,1)S(1)}, u32[]{:S(2)}, u32[]{:S(2)}) %collective-permute-start.32) | collective-permute-done | bytes 393248 | tf_op jit(solution)/shard_map/ppermute | solution.py:59
  203.4 1.3 collective-permute-done.33.refs_3_
  207.1 4.0 %collective-permute-done.34 = bf16[24,4096]{1,0:T(8,128)(2,1)S(1)} collective-permute-done((bf16[24,4096]{1,0:T(8,128)(2,1)S(1)}, bf16[24,4096]{1,0:T(8,128)(2,1)S(1)}, u32[]{:S(2)}, u32[]{:S(2)}) %collective-permute-start.34) | collective-permute-done | bytes 196640 | tf_op jit(solution)/shard_map/ppermute | solution.py:59
  211.1 1.2 collective-permute-done.35
  212.4 1.1 maximum_bitcast_fusion
  (109 shorter events, 17.2 us)
Async XLA Ops:
  0.0 20.0 %collective-permute-start.2 = (bf16[8192,512]{1,0:T(8,128)(2,1)}, bf16[8192,512]{1,0:T(8,128)(2,1)}, u32[]{:S(2)}, u32[]{:S(2)}) collective-permute-start(bf16[8192,512]{1,0:T(8,128)(2,1)} %bitcast.35), channel_id=1, source_target_pairs={{0,1},{1,0},{2,3},{3,2},{4,5},{5,4},{6,7},{7,6},{8,9},{9,8},{10,11... | collective-permute-start | bytes 25165832 | tf_op jit(solution)/shard_map/ppermute | solution.py:59
  0.0 31.0 %collective-permute-start.6 = (bf16[512,8192]{1,0:T(8,128)(2,1)}, bf16[512,8192]{1,0:T(8,128)(2,1)}, u32[]{:S(2)}, u32[]{:S(2)}) collective-permute-start(bf16[512,8192]{1,0:T(8,128)(2,1)} %bitcast.39), channel_id=1, source_target_pairs={{0,1},{1,0},{2,3},{3,2},{4,5},{5,4},{6,7},{7,6},{8,9},{9,8},{10,11... | collective-permute-start | bytes 25165832 | tf_op jit(solution)/shard_map/ppermute | solution.py:59
  2.8 17.9 %collective-permute-start.1 = (bf16[1,24,8192]{2,1,0:T(8,128)(2,1)}, bf16[1,24,8192]{2,1,0:T(8,128)(2,1)S(1)}, u32[]{:S(2)}, u32[]{:S(2)}) collective-permute-start(bf16[1,24,8192]{2,1,0:T(8,128)(2,1)} %get-tuple-element.123), channel_id=1, source_target_pairs={{0,24},{1,25},{2,26},{3,27},{4,28},{5,29},{6,30},{7,31},{8,16},{9,... | collective-permute-start | bytes 1179656 | tf_op jit(solution)/shard_map/ppermute | solution.py:70
  5.4 20.9 %collective-permute-start = (bf16[1,24,8192]{2,1,0:T(8,128)(2,1)}, bf16[1,24,8192]{2,1,0:T(8,128)(2,1)S(1)}, u32[]{:S(2)}, u32[]{:S(2)}) collective-permute-start(bf16[1,24,8192]{2,1,0:T(8,128)(2,1)} %get-tuple-element.123), channel_id=1, source_target_pairs={{0,16},{1,17},{2,18},{3,19},{4,20},{5,21},{6,22},{7,23},{8,24},{9,... | collective-permute-start | bytes 1179656 | tf_op jit(solution)/shard_map/ppermute | solution.py:70
  6.9 3.7 %copy-start.13 = (s32[1,3]{1,0:T(1,128)S(1)}, s32[1,3]{1,0:T(1,128)}, u32[]{:S(2)}) copy-start(s32[1,3]{1,0:T(1,128)} %param.13) | copy-start | bytes 40
  10.1 16.2 %copy-start.8 = (bf16[1,8192]{1,0:T(2,128)(2,1)S(1)}, bf16[1,8192]{1,0:T(2,128)(2,1)}, u32[]{:S(2)}) copy-start(bf16[1,8192]{1,0:T(2,128)(2,1)} %refs_2_.5) | copy-start | bytes 49156
  10.1 9.2 %collective-permute-start.3 = (bf16[8192,128]{1,0:T(8,128)(2,1)S(1)}, bf16[8192,128]{1,0:T(8,128)(2,1)}, u32[]{:S(2)}, u32[]{:S(2)}) collective-permute-start(bf16[8192,128]{1,0:T(8,128)(2,1)S(1)} %copy.17.wkv_mine), channel_id=1, source_target_pairs={{0,1},{1,0},{2,3},{3,2},{4,5},{5,4},{6,7},{7,6},{8,9},{9,8},{10,11... | collective-permute-start | bytes 6291464 | tf_op jit(solution)/shard_map/ppermute | solution.py:59
  12.8 18.0 %copy-start.12 = (bf16[1,24,8192]{2,1,0:T(8,128)(2,1)S(1)}, bf16[1,24,8192]{2,1,0:T(8,128)(2,1)}, u32[]{:S(2)}) copy-start(bf16[1,24,8192]{2,1,0:T(8,128)(2,1)} %get-tuple-element.125) | copy-start | bytes 1179652
  15.3 35.5 %copy-start.11 = (bf16[1,24,8192]{2,1,0:T(8,128)(2,1)S(1)}, bf16[1,24,8192]{2,1,0:T(8,128)(2,1)}, u32[]{:S(2)}) copy-start(bf16[1,24,8192]{2,1,0:T(8,128)(2,1)} %get-tuple-element.124) | copy-start | bytes 1179652
  26.8 21.0 %collective-permute-start.5 = (bf16[48,8192]{1,0:T(8,128)(2,1)S(1)}, bf16[48,8192]{1,0:T(8,128)(2,1)S(1)}, u32[]{:S(2)}, u32[]{:S(2)}) collective-permute-start(bf16[48,8192]{1,0:T(8,128)(2,1)S(1)} %get-tuple-element.64.own), channel_id=1, source_target_pairs={{0,6},{1,7},{2,4},{3,5},{4,2},{5,3},{6,0},{7,1},{8,14},{9,15},{10,... | collective-permute-start | bytes 2359304 | tf_op jit(solution)/shard_map/ppermute | solution.py:59
  30.9 18.3 %collective-permute-start.4 = (bf16[48,8192]{1,0:T(8,128)(2,1)S(1)}, bf16[48,8192]{1,0:T(8,128)(2,1)S(1)}, u32[]{:S(2)}, u32[]{:S(2)}) collective-permute-start(bf16[48,8192]{1,0:T(8,128)(2,1)S(1)} %get-tuple-element.64.own), channel_id=1, source_target_pairs={{0,2},{1,3},{2,0},{3,1},{4,6},{5,7},{6,4},{7,5},{8,10},{9,11},{10,... | collective-permute-start | bytes 2359304 | tf_op jit(solution)/shard_map/ppermute | solution.py:59
  30.9 20.0 %collective-permute-start.10 = (bf16[1,24,8192]{2,1,0:T(8,128)(2,1)S(1)}, bf16[1,24,8192]{2,1,0:T(8,128)(2,1)S(1)}, u32[]{:S(2)}, u32[]{:S(2)}) collective-permute-start(bf16[1,24,8192]{2,1,0:T(8,128)(2,1)S(1)} %copy-done.12), channel_id=1, source_target_pairs={{0,24},{1,25},{2,26},{3,27},{4,28},{5,29},{6,30},{7,31},{8,16},{9,... | collective-permute-start | bytes 1179656 | tf_op jit(solution)/shard_map/ppermute | solution.py:70
  30.9 21.6 %collective-permute-start.9 = (bf16[1,24,8192]{2,1,0:T(8,128)(2,1)S(1)}, bf16[1,24,8192]{2,1,0:T(8,128)(2,1)S(1)}, u32[]{:S(2)}, u32[]{:S(2)}) collective-permute-start(bf16[1,24,8192]{2,1,0:T(8,128)(2,1)S(1)} %copy-done.12), channel_id=1, source_target_pairs={{0,16},{1,17},{2,18},{3,19},{4,20},{5,21},{6,22},{7,23},{8,24},{9,... | collective-permute-start | bytes 1179656 | tf_op jit(solution)/shard_map/ppermute | solution.py:70
  49.3 13.3 %collective-permute-start.7 = (bf16[48,4096]{1,0:T(8,128)(2,1)S(1)}, bf16[48,4096]{1,0:T(8,128)(2,1)S(1)}, u32[]{:S(2)}, u32[]{:S(2)}) collective-permute-start(bf16[48,4096]{1,0:T(8,128)(2,1)S(1)} %get-tuple-element.66), channel_id=1, source_target_pairs={{0,6},{1,7},{2,4},{3,5},{4,2},{5,3},{6,0},{7,1},{8,14},{9,15},{10,... | collective-permute-start | bytes 1179656 | tf_op jit(solution)/shard_map/ppermute | solution.py:59
  50.8 11.8 %collective-permute-start.8 = (bf16[48,4096]{1,0:T(8,128)(2,1)S(1)}, bf16[48,4096]{1,0:T(8,128)(2,1)S(1)}, u32[]{:S(2)}, u32[]{:S(2)}) collective-permute-start(bf16[48,4096]{1,0:T(8,128)(2,1)S(1)} %get-tuple-element.67), channel_id=1, source_target_pairs={{0,2},{1,3},{2,0},{3,1},{4,6},{5,7},{6,4},{7,5},{8,10},{9,11},{10,... | collective-permute-start | bytes 1179656 | tf_op jit(solution)/shard_map/ppermute | solution.py:59
  50.8 25.9 %collective-permute-start.12 = (bf16[1,24,8192]{2,1,0:T(8,128)(2,1)S(1)}, bf16[1,24,8192]{2,1,0:T(8,128)(2,1)S(1)}, u32[]{:S(2)}, u32[]{:S(2)}) collective-permute-start(bf16[1,24,8192]{2,1,0:T(8,128)(2,1)S(1)} %copy-done.11), channel_id=1, source_target_pairs={{0,24},{1,25},{2,26},{3,27},{4,28},{5,29},{6,30},{7,31},{8,16},{9,... | collective-permute-start | bytes 1179656 | tf_op jit(solution)/shard_map/ppermute | solution.py:70
  50.8 25.9 %collective-permute-start.11 = (bf16[1,24,8192]{2,1,0:T(8,128)(2,1)S(1)}, bf16[1,24,8192]{2,1,0:T(8,128)(2,1)S(1)}, u32[]{:S(2)}, u32[]{:S(2)}) collective-permute-start(bf16[1,24,8192]{2,1,0:T(8,128)(2,1)S(1)} %copy-done.11), channel_id=1, source_target_pairs={{0,16},{1,17},{2,18},{3,19},{4,20},{5,21},{6,22},{7,23},{8,24},{9,... | collective-permute-start | bytes 1179656 | tf_op jit(solution)/shard_map/ppermute | solution.py:70
  53.0 18.3 %copy-start.2 = (bf16[48,8192]{1,0:T(8,128)(2,1)}, bf16[48,8192]{1,0:T(8,128)(2,1)S(1)}, u32[]{:S(2)}) copy-start(bf16[48,8192]{1,0:T(8,128)(2,1)S(1)} %get-tuple-element.72.own) | copy-start | bytes 2359300
  53.0 23.3 %collective-permute-start.14 = (bf16[48,8192]{1,0:T(8,128)(2,1)S(1)}, bf16[48,8192]{1,0:T(8,128)(2,1)S(1)}, u32[]{:S(2)}, u32[]{:S(2)}) collective-permute-start(bf16[48,8192]{1,0:T(8,128)(2,1)S(1)} %get-tuple-element.72.own), channel_id=1, source_target_pairs={{0,6},{1,7},{2,4},{3,5},{4,2},{5,3},{6,0},{7,1},{8,14},{9,15},{10,... | collective-permute-start | bytes 2359304 | tf_op jit(solution)/shard_map/ppermute | solution.py:59
  62.6 14.1 %collective-permute-start.13 = (bf16[48,8192]{1,0:T(8,128)(2,1)S(1)}, bf16[48,8192]{1,0:T(8,128)(2,1)S(1)}, u32[]{:S(2)}, u32[]{:S(2)}) collective-permute-start(bf16[48,8192]{1,0:T(8,128)(2,1)S(1)} %get-tuple-element.72.own), channel_id=1, source_target_pairs={{0,2},{1,3},{2,0},{3,1},{4,6},{5,7},{6,4},{7,5},{8,10},{9,11},{10,... | collective-permute-start | bytes 2359304 | tf_op jit(solution)/shard_map/ppermute | solution.py:59
  71.4 10.4 %copy-start = (bf16[1,2,384,1024]{3,2,1,0:T(8,128)(2,1)S(1)}, bf16[1,2,384,1024]{3,2,1,0:T(8,128)(2,1)}, u32[]{:S(2)}) copy-start(bf16[1,2,384,1024]{3,2,1,0:T(8,128)(2,1)} %param.12) | copy-start | bytes 4718596
  78.1 38.3 %collective-permute-start.19 = (bf16[48,8192]{1,0:T(8,128)(2,1)}, bf16[48,8192]{1,0:T(8,128)(2,1)S(1)}, u32[]{:S(2)}, u32[]{:S(2)}) collective-permute-start(bf16[48,8192]{1,0:T(8,128)(2,1)} %get-tuple-element.82.own), channel_id=1, source_target_pairs={{0,6},{1,7},{2,4},{3,5},{4,2},{5,3},{6,0},{7,1},{8,14},{9,15},{10,... | collective-permute-start | bytes 2359304 | tf_op jit(solution)/shard_map/ppermute | solution.py:59
  79.6 36.8 %collective-permute-start.18 = (bf16[48,8192]{1,0:T(8,128)(2,1)}, bf16[48,8192]{1,0:T(8,128)(2,1)}, u32[]{:S(2)}, u32[]{:S(2)}) collective-permute-start(bf16[48,8192]{1,0:T(8,128)(2,1)} %get-tuple-element.82.own), channel_id=1, source_target_pairs={{0,2},{1,3},{2,0},{3,1},{4,6},{5,7},{6,4},{7,5},{8,10},{9,11},{10,... | collective-permute-start | bytes 2359304 | tf_op jit(solution)/shard_map/ppermute | solution.py:59
  81.7 24.0 %copy-start.3 = (bf16[48,8192]{1,0:T(8,128)(2,1)S(1)}, bf16[48,8192]{1,0:T(8,128)(2,1)}, u32[]{:S(2)}) copy-start(bf16[48,8192]{1,0:T(8,128)(2,1)} %copy-done.2) | copy-start | bytes 2359300
  92.3 44.4 %collective-permute-start.15 = (bf16[96,8192]{1,0:T(8,128)(2,1)}, bf16[96,8192]{1,0:T(8,128)(2,1)S(1)}, u32[]{:S(2)}, u32[]{:S(2)}) collective-permute-start(bf16[96,8192]{1,0:T(8,128)(2,1)} %get-tuple-element.76), channel_id=1, source_target_pairs={{0,8},{1,9},{2,10},{3,11},{4,12},{5,13},{6,14},{7,15},{8,0},{9,1},... | collective-permute-start | bytes 4718600 | tf_op jit(solution)/shard_map/ppermute | solution.py:59
  93.4 12.1 %collective-permute-start.16 = (bf16[48,4096]{1,0:T(8,128)(2,1)S(1)}, bf16[48,4096]{1,0:T(8,128)(2,1)S(1)}, u32[]{:S(2)}, u32[]{:S(2)}) collective-permute-start(bf16[48,4096]{1,0:T(8,128)(2,1)S(1)} %get-tuple-element.77), channel_id=1, source_target_pairs={{0,6},{1,7},{2,4},{3,5},{4,2},{5,3},{6,0},{7,1},{8,14},{9,15},{10,... | collective-permute-start | bytes 1179656 | tf_op jit(solution)/shard_map/ppermute | solution.py:59
  95.1 10.6 %collective-permute-start.17 = (bf16[48,4096]{1,0:T(8,128)(2,1)S(1)}, bf16[48,4096]{1,0:T(8,128)(2,1)S(1)}, u32[]{:S(2)}, u32[]{:S(2)}) collective-permute-start(bf16[48,4096]{1,0:T(8,128)(2,1)S(1)} %get-tuple-element.78), channel_id=1, source_target_pairs={{0,2},{1,3},{2,0},{3,1},{4,6},{5,7},{6,4},{7,5},{8,10},{9,11},{10,... | collective-permute-start | bytes 1179656 | tf_op jit(solution)/shard_map/ppermute | solution.py:59
  114.4 6.5 %copy-start.9 = (bf16[8,192,128]{2,1,0:T(8,128)(2,1)}, bf16[8,192,128]{2,1,0:T(8,128)(2,1)S(1)}, u32[]{:S(2)}) copy-start(bf16[8,192,128]{2,1,0:T(8,128)(2,1)S(1)} %get-tuple-element.80.query) | copy-start | bytes 1179652
  118.5 21.1 %collective-permute-start.23 = (bf16[48,4096]{1,0:T(8,128)(2,1)S(1)}, bf16[48,4096]{1,0:T(8,128)(2,1)S(1)}, u32[]{:S(2)}, u32[]{:S(2)}) collective-permute-start(bf16[48,4096]{1,0:T(8,128)(2,1)S(1)} %get-tuple-element.91), channel_id=1, source_target_pairs={{0,6},{1,7},{2,4},{3,5},{4,2},{5,3},{6,0},{7,1},{8,14},{9,15},{10,... | collective-permute-start | bytes 1179656 | tf_op jit(solution)/shard_map/ppermute | solution.py:59
  120.1 19.5 %collective-permute-start.24 = (bf16[48,4096]{1,0:T(8,128)(2,1)S(1)}, bf16[48,4096]{1,0:T(8,128)(2,1)S(1)}, u32[]{:S(2)}, u32[]{:S(2)}) collective-permute-start(bf16[48,4096]{1,0:T(8,128)(2,1)S(1)} %get-tuple-element.92), channel_id=1, source_target_pairs={{0,2},{1,3},{2,0},{3,1},{4,6},{5,7},{6,4},{7,5},{8,10},{9,11},{10,... | collective-permute-start | bytes 1179656 | tf_op jit(solution)/shard_map/ppermute | solution.py:59
  120.9 1.0 copy-start.10
  134.5 20.3 %collective-permute-start.21 = (bf16[96,4096]{1,0:T(8,128)(2,1)}, bf16[96,4096]{1,0:T(8,128)(2,1)S(1)}, u32[]{:S(2)}, u32[]{:S(2)}) collective-permute-start(bf16[96,4096]{1,0:T(8,128)(2,1)} %get-tuple-element.88), channel_id=1, source_target_pairs={{0,2},{1,3},{2,0},{3,1},{4,6},{5,7},{6,4},{7,5},{8,10},{9,11},{10,... | collective-permute-start | bytes 2359304 | tf_op jit(solution)/shard_map/ppermute | solution.py:59
  135.7 19.1 %collective-permute-start.22 = (bf16[96,4096]{1,0:T(8,128)(2,1)}, bf16[96,4096]{1,0:T(8,128)(2,1)S(1)}, u32[]{:S(2)}, u32[]{:S(2)}) collective-permute-start(bf16[96,4096]{1,0:T(8,128)(2,1)} %get-tuple-element.90), channel_id=1, source_target_pairs={{0,8},{1,9},{2,10},{3,11},{4,12},{5,13},{6,14},{7,15},{8,0},{9,1},... | collective-permute-start | bytes 2359304 | tf_op jit(solution)/shard_map/ppermute | solution.py:59
  136.7 2.9 %copy-start.5 = (bf16[48,8192]{1,0:T(8,128)(2,1)S(1)}, bf16[48,8192]{1,0:T(8,128)(2,1)}, u32[]{:S(2)}) copy-start(bf16[48,8192]{1,0:T(8,128)(2,1)} %copy-done.4) | copy-start | bytes 2359300
  137.9 20.0 %collective-permute-start.20 = (bf16[48,8192]{1,0:T(8,128)(2,1)}, bf16[48,8192]{1,0:T(8,128)(2,1)S(1)}, u32[]{:S(2)}, u32[]{:S(2)}) collective-permute-start(bf16[48,8192]{1,0:T(8,128)(2,1)} %get-tuple-element.86), channel_id=1, source_target_pairs={{0,6},{1,7},{2,4},{3,5},{4,2},{5,3},{6,0},{7,1},{8,14},{9,15},{10,... | collective-permute-start | bytes 2359304 | tf_op jit(solution)/shard_map/ppermute | solution.py:59
  139.6 15.2 %copy-start.7 = (bf16[96,4096]{1,0:T(8,128)(2,1)S(1)}, bf16[96,4096]{1,0:T(8,128)(2,1)}, u32[]{:S(2)}) copy-start(bf16[96,4096]{1,0:T(8,128)(2,1)} %copy-done.6) | copy-start | bytes 2359300
  155.2 2.9 %copy-start.1 = (bf16[1,2,384,1024]{3,2,1,0:T(8,128)(2,1)S(1)}, bf16[1,2,384,1024]{3,2,1,0:T(8,128)(2,1)}, u32[]{:S(2)}) copy-start(bf16[1,2,384,1024]{3,2,1,0:T(8,128)(2,1)} %param.12) | copy-start | bytes 4718596
  155.2 13.3 %collective-permute-start.26 = (bf16[48,4096]{1,0:T(8,128)(2,1)S(1)}, bf16[48,4096]{1,0:T(8,128)(2,1)S(1)}, u32[]{:S(2)}, u32[]{:S(2)}) collective-permute-start(bf16[48,4096]{1,0:T(8,128)(2,1)S(1)} %get-tuple-element.99), channel_id=1, source_target_pairs={{0,8},{1,9},{2,10},{3,11},{4,12},{5,13},{6,14},{7,15},{8,0},{9,1},... | collective-permute-start | bytes 1179656 | tf_op jit(solution)/shard_map/ppermute | solution.py:59
  156.2 12.3 %collective-permute-start.27 = (bf16[48,4096]{1,0:T(8,128)(2,1)S(1)}, bf16[48,4096]{1,0:T(8,128)(2,1)S(1)}, u32[]{:S(2)}, u32[]{:S(2)}) collective-permute-start(bf16[48,4096]{1,0:T(8,128)(2,1)S(1)} %get-tuple-element.101), channel_id=1, source_target_pairs={{0,6},{1,7},{2,4},{3,5},{4,2},{5,3},{6,0},{7,1},{8,14},{9,15},{10,... | collective-permute-start | bytes 1179656 | tf_op jit(solution)/shard_map/ppermute | solution.py:59
  168.7 8.9 %collective-permute-start.28 = (bf16[24,4096]{1,0:T(8,128)(2,1)S(1)}, bf16[24,4096]{1,0:T(8,128)(2,1)S(1)}, u32[]{:S(2)}, u32[]{:S(2)}) collective-permute-start(bf16[24,4096]{1,0:T(8,128)(2,1)S(1)} %get-tuple-element.106), channel_id=1, source_target_pairs={{0,6},{1,7},{2,4},{3,5},{4,2},{5,3},{6,0},{7,1},{8,14},{9,15},{10,... | collective-permute-start | bytes 589832 | tf_op jit(solution)/shard_map/ppermute | solution.py:59
  170.4 36.1 %collective-permute-start.25 = (bf16[24,8192]{1,0:T(8,128)(2,1)S(1)}, bf16[24,8192]{1,0:T(8,128)(2,1)S(1)}, u32[]{:S(2)}, u32[]{:S(2)}) collective-permute-start(bf16[24,8192]{1,0:T(8,128)(2,1)S(1)} %get-tuple-element.97), channel_id=1, source_target_pairs={{0,2},{1,3},{2,0},{3,1},{4,6},{5,7},{6,4},{7,5},{8,10},{9,11},{10,... | collective-permute-start | bytes 1179656 | tf_op jit(solution)/shard_map/ppermute | solution.py:59
  170.4 14.4 %collective-permute-start.29 = (bf16[24,4096]{1,0:T(8,128)(2,1)S(1)}, bf16[24,4096]{1,0:T(8,128)(2,1)S(1)}, u32[]{:S(2)}, u32[]{:S(2)}) collective-permute-start(bf16[24,4096]{1,0:T(8,128)(2,1)S(1)} %get-tuple-element.108), channel_id=1, source_target_pairs={{0,2},{1,3},{2,0},{3,1},{4,6},{5,7},{6,4},{7,5},{8,10},{9,11},{10,... | collective-permute-start | bytes 589832 | tf_op jit(solution)/shard_map/ppermute | solution.py:59
  172.5 20.7 %collective-permute-start.30 = (bf16[96,4096]{1,0:T(8,128)(2,1)S(1)}, bf16[96,4096]{1,0:T(8,128)(2,1)S(1)}, u32[]{:S(2)}, u32[]{:S(2)}) collective-permute-start(bf16[96,4096]{1,0:T(8,128)(2,1)S(1)} %get-tuple-element.110), channel_id=1, source_target_pairs={{0,6},{1,7},{2,4},{3,5},{4,2},{5,3},{6,0},{7,1},{8,14},{9,15},{10,... | collective-permute-start | bytes 2359304 | tf_op jit(solution)/shard_map/ppermute | solution.py:59
  174.0 19.1 %collective-permute-start.31 = (bf16[96,4096]{1,0:T(8,128)(2,1)S(1)}, bf16[96,4096]{1,0:T(8,128)(2,1)S(1)}, u32[]{:S(2)}, u32[]{:S(2)}) collective-permute-start(bf16[96,4096]{1,0:T(8,128)(2,1)S(1)} %get-tuple-element.112), channel_id=1, source_target_pairs={{0,8},{1,9},{2,10},{3,11},{4,12},{5,13},{6,14},{7,15},{8,0},{9,1},... | collective-permute-start | bytes 2359304 | tf_op jit(solution)/shard_map/ppermute | solution.py:59
  193.5 9.9 %collective-permute-start.32 = (bf16[48,4096]{1,0:T(8,128)(2,1)S(1)}, bf16[48,4096]{1,0:T(8,128)(2,1)S(1)}, u32[]{:S(2)}, u32[]{:S(2)}) collective-permute-start(bf16[48,4096]{1,0:T(8,128)(2,1)S(1)} %get-tuple-element.115), channel_id=1, source_target_pairs={{0,2},{1,3},{2,0},{3,1},{4,6},{5,7},{6,4},{7,5},{8,10},{9,11},{10,... | collective-permute-start | bytes 1179656 | tf_op jit(solution)/shard_map/ppermute | solution.py:59
  193.6 11.1 %collective-permute-start.33 = (bf16[48,4096]{1,0:T(8,128)(2,1)S(1)}, bf16[48,4096]{1,0:T(8,128)(2,1)S(1)}, u32[]{:S(2)}, u32[]{:S(2)}) collective-permute-start(bf16[48,4096]{1,0:T(8,128)(2,1)S(1)} %get-tuple-element.117), channel_id=1, source_target_pairs={{0,6},{1,7},{2,4},{3,5},{4,2},{5,3},{6,0},{7,1},{8,14},{9,15},{10,... | collective-permute-start | bytes 1179656 | tf_op jit(solution)/shard_map/ppermute | solution.py:59
  205.4 5.7 %collective-permute-start.34 = (bf16[24,4096]{1,0:T(8,128)(2,1)S(1)}, bf16[24,4096]{1,0:T(8,128)(2,1)S(1)}, u32[]{:S(2)}, u32[]{:S(2)}) collective-permute-start(bf16[24,4096]{1,0:T(8,128)(2,1)S(1)} %get-tuple-element.120), channel_id=1, source_target_pairs={{0,8},{1,9},{2,10},{3,11},{4,12},{5,13},{6,14},{7,15},{8,0},{9,1},... | collective-permute-start | bytes 589832 | tf_op jit(solution)/shard_map/ppermute | solution.py:59
  206.6 5.8 %collective-permute-start.35 = (bf16[24,4096]{1,0:T(8,128)(2,1)S(1)}, bf16[24,4096]{1,0:T(8,128)(2,1)S(1)}, u32[]{:S(2)}, u32[]{:S(2)}) collective-permute-start(bf16[24,4096]{1,0:T(8,128)(2,1)S(1)} %get-tuple-element.122), channel_id=1, source_target_pairs={{0,2},{1,3},{2,0},{3,1},{4,6},{5,7},{6,4},{7,5},{8,10},{9,11},{10,... | collective-permute-start | bytes 589832 | tf_op jit(solution)/shard_map/ppermute | solution.py:59
  (2 other events, 1.8 us)
